TPU v7x, 512 devices: a whole 4x4x16 slice. The times are simulated.
512 devices in a mesh: dp: 32 (over y_lo, z), expert: 16 (over x, y_hi, core).
Axes of the slice: x: 4, y: 4 (y_hi: 2, y_lo: 2; y = y_hi * 2 + y_lo), z: 16, core: 2. Of those that a mesh axis runs over, the one named last changes fastest.
Arguments:
- tokens: bfloat16 [128, 256, 1280], P('dp', 'expert'), may hold values from -300 to 300
- cotangent: bfloat16 [128, 256, 1280], P('dp', 'expert'), may hold values from -6 to 6
- slot_params: bfloat16 [1280, 32], P(None, 'expert'), may hold values from -1 to 1
- w_in: bfloat16 [32, 1280, 5120], P('expert', None, 'dp'), may hold values from -0.15625 to 0.15625
- w_out: bfloat16 [32, 5120, 1280], P('expert', 'dp'), may hold values from -0.078125 to 0.078125
Outputs:
- token_grad: bfloat16 [128, 256, 1280], P('dp', 'expert')
- slot_grad: float32 [1280, 32], P(None, 'expert')
- w_in_grad: bfloat16 [32, 1280, 5120], P('expert', None, 'dp')
- w_out_grad: bfloat16 [32, 5120, 1280], P('expert', 'dp')
All inputs are finite; a program needn't handle non-finite values.
Results may differ from a plain program's by a relative error of at most 0.035.
Values may be sent and summed in bfloat16 or wider, within the bound.
No kernel may reach another device: no remote copies, remote signals or barrier semaphores. Data moves between devices by JAX's collectives and lax.ppermute only.
A program may use at most 64 MiB of HBM per device.

v0:
```python
import jax
import jax.numpy as jnp
from jax import lax
from jax.sharding import PartitionSpec as P


def gelu_exact(value):
    return jax.nn.gelu(value, approximate=False)


def expert_forward(slot_in, w_in, w_out):
    all_in = lax.all_gather(slot_in, "dp", axis=0, tiled=True)
    preact = jnp.einsum("bsd,sdh->bsh", all_in, w_in, preferred_element_type=jnp.float32)
    activated = gelu_exact(preact).astype(jnp.bfloat16)
    slot_out = lax.psum_scatter(
        jnp.einsum("bsh,shd->bsd", activated, w_out, preferred_element_type=jnp.float32).astype(
            jnp.bfloat16
        ),
        "dp",
        scatter_dimension=0,
        tiled=True,
    )
    return (all_in, preact, activated, slot_out)


def expert_backward(all_in, preact, activated, slot_out_grad, w_in, w_out):
    all_out_grad = lax.all_gather(slot_out_grad, "dp", axis=0, tiled=True)
    w_out_grad = jnp.einsum(
        "bsh,bsd->shd", activated, all_out_grad, preferred_element_type=jnp.float32
    ).astype(jnp.bfloat16)
    act_grad = jnp.einsum("bsd,shd->bsh", all_out_grad, w_out, preferred_element_type=jnp.float32)
    _, pullback = jax.vjp(gelu_exact, preact)
    preact_grad = pullback(act_grad)[0].astype(jnp.bfloat16)
    w_in_grad = jnp.einsum(
        "bsd,bsh->sdh", all_in, preact_grad, preferred_element_type=jnp.float32
    ).astype(jnp.bfloat16)
    slot_in_grad = lax.psum_scatter(
        jnp.einsum("bsh,sdh->bsd", preact_grad, w_in, preferred_element_type=jnp.float32).astype(
            jnp.bfloat16
        ),
        "dp",
        scatter_dimension=0,
        tiled=True,
    )
    return (w_in_grad, w_out_grad, slot_in_grad)


def param_total(param_local):
    return lax.psum(param_local, "dp")


def on_device(tokens, cotangent, slot_params, w_in, w_out):
    share_len = tokens.shape[1]
    full_tok, full_cot = (
        lax.all_gather(tokens, "expert", axis=1, tiled=True),
        lax.all_gather(cotangent, "expert", axis=1, tiled=True),
    )
    logits = jnp.einsum("bmd,ds->bsm", full_tok, slot_params, preferred_element_type=jnp.float32)
    dispatch = jax.nn.softmax(logits, axis=2)
    local_peak = jnp.max(logits, axis=1)
    peak_all = lax.pmax(local_peak, "expert")
    total_all = lax.psum(jnp.sum(jnp.exp(logits - peak_all[:, None, :]), axis=1), "expert")
    combine = jnp.exp(logits - peak_all[:, None, :]) / total_all[:, None, :]
    dispatch_b = dispatch.astype(jnp.bfloat16)
    combine_b = combine.astype(jnp.bfloat16)
    slot_in = jnp.einsum(
        "bsm,bmd->bsd", dispatch_b, full_tok, preferred_element_type=jnp.float32
    ).astype(jnp.bfloat16)
    all_in, preact, activated, slot_out = expert_forward(slot_in, w_in, w_out)
    combine_grad = jnp.einsum(
        "bmd,bsd->bsm", full_cot, slot_out, preferred_element_type=jnp.float32
    )
    slot_out_grad = jnp.einsum(
        "bsm,bmd->bsd", combine_b, full_cot, preferred_element_type=jnp.float32
    ).astype(jnp.bfloat16)
    row_sums = lax.psum(jnp.sum(combine * combine_grad, axis=1), "expert")
    w_in_grad, w_out_grad, slot_in_grad = expert_backward(
        all_in, preact, activated, slot_out_grad, w_in, w_out
    )
    dispatch_grad = jnp.einsum(
        "bsd,bmd->bsm", slot_in_grad, full_tok, preferred_element_type=jnp.float32
    )
    col_sums = jnp.sum(dispatch * dispatch_grad, axis=2, keepdims=True)
    logit_grad = (
        dispatch * (dispatch_grad - col_sums) + combine * (combine_grad - row_sums[:, None, :])
    ).astype(jnp.bfloat16)
    param_local = jnp.einsum(
        "bsm,bmd->ds", logit_grad, full_tok, preferred_element_type=jnp.float32
    )
    slot_grad = param_total(param_local)
    token_term = jnp.einsum(
        "bsm,bsd->bmd", dispatch_b, slot_in_grad, preferred_element_type=jnp.float32
    )
    token_term = token_term + jnp.einsum(
        "bsm,ds->bmd", logit_grad, slot_params, preferred_element_type=jnp.float32
    )
    summed = lax.psum(token_term.astype(jnp.bfloat16), "expert").astype(jnp.float32)
    own_rows = lax.dynamic_slice_in_dim(summed, lax.axis_index("expert") * share_len, share_len, 1)
    token_grad = own_rows.astype(jnp.bfloat16)
    return (token_grad, slot_grad, w_in_grad, w_out_grad)


def solution(mesh):
    placed = (
        P("dp", "expert", None),
        P("dp", "expert", None),
        P(None, "expert"),
        P("expert", None, "dp"),
        P("expert", "dp", None),
    )
    return jax.shard_map(
        on_device,
        mesh=mesh,
        in_specs=placed,
        out_specs=(
            P("dp", "expert", None),
            P(None, "expert"),
            P("expert", None, "dp"),
            P("expert", "dp", None),
        ),
        check_vma=False,
    )
```

profile of v0, /device:TPU:1, one launch (start us, length us, event | category | flops | bytes accessed | tf_op | source)
XLA Modules:
  0.0 752.9 jit_solution(2567639746068162083)
XLA Ops:
  8.0 0.7 all-gather.5.cloned.1.call-update
  8.7 74.2 %all-gather.3.cloned.1.call-done = bf16[4,256,1280]{2,1,0:T(8,128)(2,1)} async-done(((bf16[4,16,1280]{2,1,0:T(8,128)(2,1)}), bf16[4,256,1280]{2,1,0:T(8,128)(2,1)}) %all-gather.3.cloned.1.call-update) | async-done | bytes 2621456 | tf_op jit(solution)/shard_map/all_gather | solution.py:55
  82.9 2.7 fusion.59
  85.6 32.9 %pmax.7 = f32[4,256]{1,0:T(4,128)S(1)} all-reduce(f32[4,256]{1,0:T(4,128)S(1)} %get-tuple-element.6), channel_id=1, replica_groups=mesh['dp'=32,'expert'=16] {'expert'}, use_global_device_ids=true, to_apply=%region_3.0 | all-reduce | flops 1024 | bytes 8192 | tf_op jit(solution)/shard_map/pmax | solution.py:61
  118.5 35.5 %psum.28 = f32[4,256]{1,0:T(4,128)S(1)} all-reduce(f32[4,256]{1,0:T(4,128)S(1)} %fusion.50), channel_id=1, replica_groups=mesh['dp'=32,'expert'=16] {'expert'}, use_global_device_ids=true, to_apply=%region_5.0 | all-reduce | flops 1024 | bytes 8192 | tf_op jit(solution)/shard_map/psum | solution.py:62
  154.7 2.2 convolution_convert_fusion.4
  156.9 57.9 %all_gather.15 = bf16[128,2,1280]{2,1,0:T(2,128)(2,1)} all-gather(bf16[4,2,1280]{2,1,0:T(2,128)(2,1)S(1)} %convolution_convert_fusion.4), channel_id=1, replica_groups=mesh['dp'=32,'expert'=16] {'dp'}, dimensions={0}, use_global_device_ids=true | all-gather | bytes 675840 | tf_op jit(solution)/shard_map/all_gather | solution.py:27
  215.3 47.9 %all_gather.13 = bf16[128,2,1280]{2,1,0:T(2,128)(2,1)S(1)} all-gather(bf16[4,2,1280]{2,1,0:T(2,128)(2,1)S(1)} %convolution_convert_fusion.5), channel_id=1, replica_groups=mesh['dp'=32,'expert'=16] {'dp'}, dimensions={0}, use_global_device_ids=true | all-gather | bytes 675840 | tf_op jit(solution)/shard_map/all_gather | solution.py:12
  263.3 1.7 fusion.12
  266.8 1.5 copy.40
  268.4 1.2 fusion.2
  269.7 1.3 dynamic-slice
  271.5 251.9 %all-reduce.8.cloned.1.call-done = (bf16[128,2,1280]{2,0,1:T(8,128)(2,1)}, bf16[128,2,1280]{2,1,0:T(2,128)(2,1)}) async-done(((bf16[128,2,1280]{2,0,1:T(8,128)(2,1)}, bf16[128,2,1280]{2,1,0:T(2,128)(2,1)}), (bf16[128,2,1280]{2,0,1:T(8,128)(2,1)}, bf16[128,2,1280]{2,1,0:T(2,128)(2,1)})) %all-reduce.8.cloned.1.call-update) | async-done | bytes 1310736
  523.4 0.8 constant_dynamic-slice_fusion
  524.2 3.7 multiply_reduce_fusion.1
  527.9 56.0 %psum.29 = f32[4,256]{1,0:T(4,128)} all-reduce(f32[4,256]{1,0:T(4,128)} %get-tuple-element.10), channel_id=1, replica_groups=mesh['dp'=32,'expert'=16] {'expert'}, use_global_device_ids=true, to_apply=%region_10.0 | all-reduce | flops 1024 | bytes 8192 | tf_op jit(solution)/shard_map/psum | solution.py:76
  583.9 4.0 fusion.45
  587.9 1.4 fusion.43
  589.3 5.2 add_convert_fusion
  594.6 2.3 convolution_convert_fusion
  597.0 2.7 convolution_convert_fusion.1
  600.3 95.7 %psum.31 = f32[1280,2]{0,1:T(2,128)} all-reduce(f32[1280,2]{0,1:T(2,128)S(1)} %convolution_bitcast_fusion), channel_id=1, replica_groups=mesh['dp'=32,'expert'=16] {'dp'}, use_global_device_ids=true, to_apply=%region_12.0 | all-reduce | flops 2560 | bytes 20480 | tf_op jit(solution)/shard_map/psum | solution.py:49
  696.1 48.6 %all-reduce.6.cloned.1.call-done = bf16[4,256,1280]{2,1,0:T(8,128)(2,1)} async-done(((bf16[4,256,1280]{2,1,0:T(8,128)(2,1)}), bf16[4,256,1280]{2,1,0:T(8,128)(2,1)}) %all-reduce.6.cloned.1.call-update) | async-done | bytes 2621456 | tf_op jit(solution)/shard_map/psum | solution.py:97
  744.7 1.6 convert_convert_fusion
  (42 shorter events, 4.5 us)
Async XLA Ops:
  7.2 257.9 %copy-start = (bf16[2,160,1280]{2,1,0:T(8,128)(2,1)S(1)}, bf16[2,160,1280]{2,1,0:T(8,128)(2,1)}, u32[]{:S(2)}) copy-start(bf16[2,160,1280]{2,1,0:T(8,128)(2,1)} %param.9) | copy-start | bytes 2457604
  7.2 75.7 %all-gather.3.cloned.1.call-start = ((), (), s32[]{:S(2)}) async-start(), calls=%async_computation | async-start | bytes 2785280 | tf_op jit(solution)/shard_map/all_gather | solution.py:55
  7.9 146.8 %all-gather.5.cloned.1.call-start = ((), (), s32[]{:S(2)}) async-start(), calls=%async_computation.1 | async-start | bytes 2785280 | tf_op jit(solution)/shard_map/all_gather | solution.py:56
  8.7 514.8 %all-reduce.8.cloned.1.call-start = ((), (), s32[]{:S(2)}) async-start(), calls=%async_computation.3 | async-start | bytes 2621440
  82.9 131.9 %copy-start.1 = (bf16[4,256,1280]{2,1,0:T(8,128)(2,1)S(1)}, bf16[4,256,1280]{2,1,0:T(8,128)(2,1)}, u32[]{:S(2)}) copy-start(bf16[4,256,1280]{2,1,0:T(8,128)(2,1)} %all-gather.3.cloned.1.call-done) | copy-start | bytes 7864324
  154.0 61.3 %copy-start.5 = (f32[4,256]{1,0:T(4,128)}, f32[4,256]{1,0:T(4,128)S(1)}, u32[]{:S(2)}) copy-start(f32[4,256]{1,0:T(4,128)S(1)} %psum.28) | copy-start | bytes 12292
  154.7 60.6 %copy-start.11 = (f32[4,2]{1,0:T(4,128)}, f32[4,2]{1,0:T(4,128)S(1)}, u32[]{:S(2)}) copy-start(f32[4,2]{1,0:T(4,128)S(1)} %get-tuple-element.8) | copy-start | bytes 100
  263.3 2.5 copy-start.2
  265.0 0.7 copy-start.13
  265.1 1.1 copy-start.4
  266.2 2.2 copy-start.3
  269.6 475.1 %all-reduce.6.cloned.1.call-start = ((), (), s32[]{:S(2)}) async-start(), calls=%async_computation.2 | async-start | bytes 5242880 | tf_op jit(solution)/shard_map/psum | solution.py:97
  596.9 2.8 copy-start.6
  596.9 2.8 copy-start.7
  596.9 2.8 copy-start.8
  596.9 2.8 copy-start.9
  597.0 2.8 copy-start.10
  597.0 2.8 copy-start.12
Sparse Core Ops, SparseCore 0:
  11.4 71.5 all-gather.2
  86.3 64.9 all-gather.4
  269.7 253.6 all-reduce.7
  594.7 149.9 all-reduce.5
where the time goes:
time: 753 us
  waiting for transfers between devices  376 us (50%)
  blocking collectives  326 us (43%)
  matrix products  29.7 us (4%)
  between operations  14.5 us (2%)
    unnamed x5, waiting for transfers between devices  253 us
    psum x1, blocking collectives, param_total(): return lax.psum(param_local, 'dp')  95.7 us
    all_gather x1, waiting for transfers between devices, on_device(): lax.all_gather(tokens, 'expert', axis=1, tiled=True)  74.2 us
    all_gather x1, blocking collectives, expert_backward(): all_out_grad = lax.all_gather(slot_out_grad, 'dp', axis=0, tiled=True)  57.9 us
    psum x1, blocking collectives, on_device(): row_sums = lax.psum(jnp.sum(combine * combine_grad, axis=1), 'expert')  56 us
    psum x1, waiting for transfers between devices, on_device(): lax.psum(token_term.astype(jnp.bfloat16), 'expert').astype(jnp.float32)  48.6 us
    all_gather x1, blocking collectives, expert_forward(): all_in = lax.all_gather(slot_in, 'dp', axis=0, tiled=True)  47.9 us
    psum x1, blocking collectives, on_device(): lax.psum(jnp.sum(jnp.exp(logits - peak_all[:, None, :]), axis=1), 'expert')  35.5 us
  transfers between devices with their start and end apart: 4, of which 3 were waited for; matrix products, arithmetic and copies ran while one was open for 1% of the time, Pallas kernels for 0%

commit v1 on v0

v1 whole, which is shorter than its diff:
```python
import jax
import jax.numpy as jnp
from jax import lax
from jax.sharding import PartitionSpec as P

F32 = jnp.float32
BF16 = jnp.bfloat16


def gelu_exact(value):
    return jax.nn.gelu(value, approximate=False)


def split3(value):
    high = lax.reduce_precision(value, 8, 7)
    middle = lax.reduce_precision(value - high, 8, 7)
    low = value - high - middle
    return [high.astype(BF16), middle.astype(BF16), low.astype(BF16)]


def join3(terms):
    wide = terms.astype(F32)
    return wide[..., 0:1] + wide[..., 1:2] + wide[..., 2:3]


def along_z(value, step):
    depth = lax.axis_size("dp") // 2
    pairs = [
        (y * depth + z, y * depth + (z + step) % depth) for y in range(2) for z in range(depth)
    ]
    return lax.ppermute(value, "dp", pairs)


def across_y(value):
    depth = lax.axis_size("dp") // 2
    pairs = [(y * depth + z, (1 - y) * depth + z) for y in range(2) for z in range(depth)]
    return lax.ppermute(value, "dp", pairs)


def add_narrow(left, right):
    return (left.astype(F32) + right.astype(F32)).astype(BF16)


def gather_dp(own):
    half = lax.axis_size("dp") // 4
    both = jnp.concatenate([own, across_y(own)], axis=2)
    up, down = [both], [both]
    for _ in range(1, half):
        up.append(along_z(up[-1], 1))
        down.append(along_z(down[-1], -1))
    far = jnp.concatenate([along_z(up[-1][:1], 1), along_z(down[-1][1:], -1)], axis=0)
    return up, down, far


def reduce_dp(up, down, far):
    half = lax.axis_size("dp") // 4
    imgs = far.shape[2] // 2
    to_low = along_z(far[:1], -1)
    to_high = along_z(far[1:], 1)
    for r in range(half - 1, 0, -1):
        if r == half - 1:
            low = jnp.concatenate([add_narrow(up[r][:1], to_low), up[r][1:]], axis=0)
            high = jnp.concatenate([down[r][:1], add_narrow(down[r][1:], to_high)], axis=0)
        else:
            low = add_narrow(up[r], to_low)
            high = add_narrow(down[r], to_high)
        to_low = along_z(low, -1)
        to_high = along_z(high, 1)
    total = up[0].astype(F32) + to_low.astype(F32) + to_high.astype(F32)
    other = across_y(total[:, :, imgs:].astype(BF16))
    return total[:, :, :imgs] + other.astype(F32)


def exchange(value, axis):
    return lax.all_to_all(value, axis, split_axis=0, concat_axis=0, tiled=True)


def everywhere(value, axis):
    return exchange(jnp.broadcast_to(value[None], (lax.axis_size(axis),) + value.shape), axis)


def expert_part(gathered, w_in, w_out):
    all_in, all_out_grad = gathered[0], gathered[1]
    preact = jnp.einsum("sbd,sdh->sbh", all_in, w_in, preferred_element_type=F32)
    activated_wide, pullback = jax.vjp(gelu_exact, preact)
    activated = activated_wide.astype(BF16)
    slot_out = jnp.einsum("sbh,shd->sbd", activated, w_out, preferred_element_type=F32)
    act_grad = jnp.einsum("sbd,shd->sbh", all_out_grad, w_out, preferred_element_type=F32)
    preact_grad = pullback(act_grad)[0].astype(BF16)
    slot_in_grad = jnp.einsum("sbh,sdh->sbd", preact_grad, w_in, preferred_element_type=F32)
    w_out_grad = jnp.einsum(
        "sbh,sbd->shd", activated, all_out_grad, preferred_element_type=F32
    ).astype(BF16)
    w_in_grad = jnp.einsum(
        "sbd,sbh->sdh", all_in, preact_grad, preferred_element_type=F32
    ).astype(BF16)
    partial = jnp.stack([slot_out.astype(BF16), slot_in_grad.astype(BF16)])
    return partial, w_in_grad, w_out_grad


def on_device(tokens, cotangent, slot_params, w_in, w_out):
    imgs, share, d = tokens.shape
    peers = lax.axis_size("expert")
    own_slots = slot_params.shape[1]
    slots = peers * own_slots
    rows = own_slots * imgs

    params = everywhere(slot_params.T, "expert").reshape(slots, d)
    logits = jnp.einsum("sd,bmd->sbm", params, tokens, preferred_element_type=F32)
    combine = jax.nn.softmax(logits, axis=0)
    combine_b = combine.astype(BF16)
    peak = jnp.max(logits, axis=2, keepdims=True)
    weight = jnp.exp(logits - peak)
    mass = jnp.sum(weight, axis=2, keepdims=True)
    part_in = jnp.einsum("sbm,bmd->sbd", weight.astype(BF16), tokens, preferred_element_type=F32)
    part_grad = jnp.einsum("sbm,bmd->sbd", combine_b, cotangent, preferred_element_type=F32)
    stats = jnp.concatenate(
        split3(peak) + split3(mass) + [jnp.zeros((slots, imgs, 122), BF16)], axis=2
    )
    sent = jnp.concatenate([part_in.astype(BF16), stats, part_grad.astype(BF16)], axis=2)
    taken = exchange(sent.reshape(peers, rows, 2 * d + 128), "expert")

    peaks = join3(taken[:, :, d : d + 3])
    masses = join3(taken[:, :, d + 3 : d + 6])
    top = jnp.max(peaks, axis=0)
    scale = jnp.exp(peaks - top[None])
    total = jnp.sum(masses * scale, axis=0)
    slot_in_wide = jnp.sum(taken[:, :, :d].astype(F32) * scale, axis=0) / total
    slot_out_grad = jnp.sum(taken[:, :, d + 128 :].astype(F32), axis=0)
    own = jnp.stack([slot_in_wide.astype(BF16), slot_out_grad.astype(BF16)])

    up, down, far = gather_dp(own.reshape(2, own_slots, imgs, d))
    chunks = up + down[1:] + [far]
    partial, w_in_grad, w_out_grad = expert_part(jnp.concatenate(chunks, axis=2), w_in, w_out)
    pieces = jnp.split(partial, len(chunks), axis=2)
    half = len(up)
    owned = reduce_dp(pieces[:half], [None] + pieces[half : 2 * half - 1], pieces[-1])
    owned_b = owned.astype(BF16).reshape(2, rows, d)

    col = jnp.sum(owned_b[1].astype(F32) * slot_in_wide, axis=1, keepdims=True)
    stats = jnp.concatenate(
        split3(top) + split3(total) + split3(col) + [jnp.zeros((rows, 119), BF16)], axis=1
    )
    back = everywhere(jnp.concatenate([owned_b[0], owned_b[1], stats], axis=1), "expert")
    back = back.reshape(slots, imgs, 2 * d + 128)
    slot_out, slot_in_grad = back[:, :, :d], back[:, :, d : 2 * d]
    top = join3(back[:, :, 2 * d : 2 * d + 3])
    total = join3(back[:, :, 2 * d + 3 : 2 * d + 6])
    col = join3(back[:, :, 2 * d + 6 : 2 * d + 9])

    dispatch = jnp.exp(logits - top) / total
    dispatch_b = dispatch.astype(BF16)
    combine_grad = jnp.einsum("bmd,sbd->sbm", cotangent, slot_out, preferred_element_type=F32)
    dispatch_grad = jnp.einsum("sbd,bmd->sbm", slot_in_grad, tokens, preferred_element_type=F32)
    row_sums = jnp.sum(combine * combine_grad, axis=0, keepdims=True)
    logit_grad = (
        dispatch * (dispatch_grad - col) + combine * (combine_grad - row_sums)
    ).astype(BF16)
    token_grad = jnp.einsum("sbm,sbd->bmd", dispatch_b, slot_in_grad, preferred_element_type=F32)
    token_grad = token_grad + jnp.einsum(
        "sbm,sd->bmd", logit_grad, params, preferred_element_type=F32
    )
    token_grad = token_grad.astype(BF16)

    share_grad = jnp.einsum("sbm,bmd->sd", logit_grad, tokens, preferred_element_type=F32)
    share_grad = jnp.sum(exchange(share_grad.reshape(peers, own_slots, d), "expert"), axis=0)
    n_dp = lax.axis_size("dp")
    share_grad = exchange(share_grad.reshape(n_dp, 1, own_slots * d // n_dp), "dp")
    share_grad = everywhere(jnp.sum(share_grad, axis=0), "dp")
    slot_grad = share_grad.reshape(own_slots, d).T
    return (token_grad, slot_grad, w_in_grad, w_out_grad)


def solution(mesh):
    placed = (
        P("dp", "expert", None),
        P("dp", "expert", None),
        P(None, "expert"),
        P("expert", None, "dp"),
        P("expert", "dp", None),
    )
    return jax.shard_map(
        on_device,
        mesh=mesh,
        in_specs=placed,
        out_specs=(
            P("dp", "expert", None),
            P(None, "expert"),
            P("expert", None, "dp"),
            P("expert", "dp", None),
        ),
        check_vma=False,
    )
```

time: 753 us -> 297 us (0.39)
  waiting for transfers between devices: 376 us -> 81.8 us
  blocking collectives: 326 us -> 33.3 us
  starting transfers between devices: 0.16 us -> 152 us
  matrix products: 29.7 us -> 10.7 us
  between operations: 14.5 us -> 1.53 us
  local copies, waits for them, and re-layouts: 4.08 us -> 12 us
    unnamed x5 -> x0, waiting for transfers between devices: 253 us -> none
    psum x3 -> x0, blocking collectives: 187 us -> none  [the longest x1 95.7 us: param_total(): return lax.psum(param_local, 'dp')]
    ppermute x0 -> x34, starting transfers between devices: none -> 110 us  [the longest x32 106 us: along_z(): return lax.ppermute(value, 'dp', pairs)]
    all_gather x2 -> x0, blocking collectives: 106 us -> none  [the longest x1 57.9 us: expert_backward(): all_out_grad = lax.all_gather(slot_out_grad, 'dp', axis=0, tiled=True)]
    all_gather x2 -> x0, waiting for transfers between devices: 74.2 us -> none  [the longest x1 74.2 us: on_device(): lax.all_gather(tokens, 'expert', axis=1, tiled=True)]
    psum x1 -> x0, waiting for transfers between devices: 48.6 us -> none  [on_device(): lax.psum(token_term.astype(jnp.bfloat16), 'expert').astype(jnp.float32)]
    all_to_all x0 -> x4, starting transfers between devices: none -> 42 us  [exchange(): return lax.all_to_all(value, axis, split_axis=0, concat_axis=0, tiled=True)]
    all_to_all x0 -> x4, waiting for transfers between devices: none -> 41 us  [exchange(): return lax.all_to_all(value, axis, split_axis=0, concat_axis=0, tiled=True)]
  transfers between devices with their start and end apart: 4 -> 38, of which waited for: 3 -> 18; matrix products, arithmetic and copies ran while one was open for 1% -> 2% of each run, Pallas kernels for 0% -> 0%
where the time goes in v1:
time: 297 us; the launch traced here: 295 us
  starting transfers between devices  152 us (51%)
  waiting for transfers between devices  81.8 us (28%)
  blocking collectives  33.3 us (11%)
  local copies, waits for them, and re-layouts  12 us (4%)
  matrix products  10.7 us (4%)
  other arithmetic  3.49 us (1%)
    ppermute x32, starting transfers between devices, along_z(): return lax.ppermute(value, 'dp', pairs)  106 us
    all_to_all x4, starting transfers between devices, exchange(): return lax.all_to_all(value, axis, split_axis=0, concat_axis=0, tiled=True)  42 us
    all_to_all x4, waiting for transfers between devices, exchange(): return lax.all_to_all(value, axis, split_axis=0, concat_axis=0, tiled=True)  41 us
    ppermute x32, waiting for transfers between devices, along_z(): return lax.ppermute(value, 'dp', pairs)  36.2 us
    all_to_all x2, blocking collectives, exchange(): return lax.all_to_all(value, axis, split_axis=0, concat_axis=0, tiled=True)  33.3 us
  transfers between devices with their start and end apart: 38, of which 18 were waited for; matrix products, arithmetic and copies ran while one was open for 2% of the time, Pallas kernels for 0%

profile of v1, /device:TPU:1, one launch (start us, length us, event | category | flops | bytes accessed | tf_op | source)
XLA Modules:
  0.0 294.9 jit_solution(13683896257611229464)
XLA Ops:
  1.5 16.7 %all_to_all.30 = bf16[16,2,1280]{2,1,0:T(2,128)(2,1)S(1)} all-to-all(bf16[16,2,1280]{2,1,0:T(2,128)(2,1)S(1)} %broadcast_in_dim.10), channel_id=1, replica_groups=mesh['dp'=32,'expert'=16] {'expert'}, dimensions={0} | all-to-all | bytes 163840 | tf_op jit(solution)/shard_map/all_to_all | solution.py:75
  24.2 16.5 %all_to_all.31 = bf16[16,8,2688]{2,1,0:T(8,128)(2,1)S(1)} all-to-all(bf16[16,8,2688]{2,1,0:T(8,128)(2,1)S(1)} %concatenate.30), channel_id=1, replica_groups=mesh['dp'=32,'expert'=16] {'expert'}, dimensions={0} | all-to-all | bytes 1376256 | tf_op jit(solution)/shard_map/all_to_all | solution.py:75
  46.7 10.0 %collective-permute-start.8 = (bf16[2,2,8,1280]{3,2,1,0:T(8,128)(2,1)S(1)}, bf16[2,2,8,1280]{3,2,1,0:T(8,128)(2,1)S(1)}, u32[]{:S(2)}, u32[]{:S(2)}) collective-permute-start(bf16[2,2,8,1280]{3,2,1,0:T(8,128)(2,1)S(1)} %pad_maximum_fusion.1), channel_id=1, source_target_pairs={{0,240},{16,0},{32,16},{48,32},{64,48},{80,64},{96,80},{112,96},{1... | collective-permute-start | bytes 245768 | tf_op jit(solution)/shard_map/ppermute | solution.py:31
  58.6 4.6 %collective-permute-start.9 = (bf16[2,2,8,1280]{3,2,1,0:T(8,128)(2,1)S(1)}, bf16[2,2,8,1280]{3,2,1,0:T(8,128)(2,1)S(1)}, u32[]{:S(2)}, u32[]{:S(2)}) collective-permute-start(bf16[2,2,8,1280]{3,2,1,0:T(8,128)(2,1)S(1)} %collective-permute-done.8), channel_id=1, source_target_pairs={{0,240},{16,0},{32,16},{48,32},{64,48},{80,64},{96,80},{112,96},{1... | collective-permute-start | bytes 245768 | tf_op jit(solution)/shard_map/ppermute | solution.py:31
  65.2 4.6 %collective-permute-start.10 = (bf16[2,2,8,1280]{3,2,1,0:T(8,128)(2,1)S(1)}, bf16[2,2,8,1280]{3,2,1,0:T(8,128)(2,1)S(1)}, u32[]{:S(2)}, u32[]{:S(2)}) collective-permute-start(bf16[2,2,8,1280]{3,2,1,0:T(8,128)(2,1)S(1)} %collective-permute-done.9), channel_id=1, source_target_pairs={{0,240},{16,0},{32,16},{48,32},{64,48},{80,64},{96,80},{112,96},{1... | collective-permute-start | bytes 245768 | tf_op jit(solution)/shard_map/ppermute | solution.py:31
  71.7 4.6 %collective-permute-start.11 = (bf16[2,2,8,1280]{3,2,1,0:T(8,128)(2,1)S(1)}, bf16[2,2,8,1280]{3,2,1,0:T(8,128)(2,1)S(1)}, u32[]{:S(2)}, u32[]{:S(2)}) collective-permute-start(bf16[2,2,8,1280]{3,2,1,0:T(8,128)(2,1)S(1)} %collective-permute-done.10), channel_id=1, source_target_pairs={{0,240},{16,0},{32,16},{48,32},{64,48},{80,64},{96,80},{112,96},{1... | collective-permute-start | bytes 245768 | tf_op jit(solution)/shard_map/ppermute | solution.py:31
  78.2 4.6 %collective-permute-start.12 = (bf16[2,2,8,1280]{3,2,1,0:T(8,128)(2,1)S(1)}, bf16[2,2,8,1280]{3,2,1,0:T(8,128)(2,1)S(1)}, u32[]{:S(2)}, u32[]{:S(2)}) collective-permute-start(bf16[2,2,8,1280]{3,2,1,0:T(8,128)(2,1)S(1)} %collective-permute-done.11), channel_id=1, source_target_pairs={{0,240},{16,0},{32,16},{48,32},{64,48},{80,64},{96,80},{112,96},{1... | collective-permute-start | bytes 245768 | tf_op jit(solution)/shard_map/ppermute | solution.py:31
  84.8 4.6 %collective-permute-start.13 = (bf16[2,2,8,1280]{3,2,1,0:T(8,128)(2,1)S(1)}, bf16[2,2,8,1280]{3,2,1,0:T(8,128)(2,1)S(1)}, u32[]{:S(2)}, u32[]{:S(2)}) collective-permute-start(bf16[2,2,8,1280]{3,2,1,0:T(8,128)(2,1)S(1)} %collective-permute-done.12), channel_id=1, source_target_pairs={{0,240},{16,0},{32,16},{48,32},{64,48},{80,64},{96,80},{112,96},{1... | collective-permute-start | bytes 245768 | tf_op jit(solution)/shard_map/ppermute | solution.py:31
  91.3 4.8 %collective-permute-start.14 = (bf16[2,2,8,1280]{3,2,1,0:T(8,128)(2,1)S(1)}, bf16[2,2,8,1280]{3,2,1,0:T(8,128)(2,1)S(1)}, u32[]{:S(2)}, u32[]{:S(2)}) collective-permute-start(bf16[2,2,8,1280]{3,2,1,0:T(8,128)(2,1)S(1)} %collective-permute-done.13), channel_id=1, source_target_pairs={{0,240},{16,0},{32,16},{48,32},{64,48},{80,64},{96,80},{112,96},{1... | collective-permute-start | bytes 245768 | tf_op jit(solution)/shard_map/ppermute | solution.py:31
  98.5 4.6 %collective-permute-start.16 = (bf16[1,2,8,1280]{3,2,1,0:T(8,128)(2,1)S(1)}, bf16[1,2,8,1280]{3,2,1,0:T(8,128)(2,1)S(1)}, u32[]{:S(2)}, u32[]{:S(2)}) collective-permute-start(bf16[1,2,8,1280]{3,2,1,0:T(8,128)(2,1)S(1)} %slice.179), channel_id=1, source_target_pairs={{0,240},{16,0},{32,16},{48,32},{64,48},{80,64},{96,80},{112,96},{1... | collective-permute-start | bytes 122888 | tf_op jit(solution)/shard_map/ppermute | solution.py:31
  129.5 4.6 %collective-permute-start.20 = (bf16[2,2,8,1280]{3,2,1,0:T(8,128)(2,1)S(1)}, bf16[2,2,8,1280]{3,2,1,0:T(8,128)(2,1)S(1)}, u32[]{:S(2)}, u32[]{:S(2)}) collective-permute-start(bf16[2,2,8,1280]{3,2,1,0:T(8,128)(2,1)S(1)} %add_convert_fusion.10), channel_id=1, source_target_pairs={{0,240},{16,0},{32,16},{48,32},{64,48},{80,64},{96,80},{112,96},{1... | collective-permute-start | bytes 245768 | tf_op jit(solution)/shard_map/ppermute | solution.py:31
  135.6 4.9 %collective-permute-start.21 = (bf16[2,2,8,1280]{3,2,1,0:T(8,128)(2,1)S(1)}, bf16[2,2,8,1280]{3,2,1,0:T(8,128)(2,1)S(1)}, u32[]{:S(2)}, u32[]{:S(2)}) collective-permute-start(bf16[2,2,8,1280]{3,2,1,0:T(8,128)(2,1)S(1)} %add_convert_fusion.9), channel_id=1, source_target_pairs={{0,240},{16,0},{32,16},{48,32},{64,48},{80,64},{96,80},{112,96},{1... | collective-permute-start | bytes 245768 | tf_op jit(solution)/shard_map/ppermute | solution.py:31
  142.5 4.7 %collective-permute-start.22 = (bf16[2,2,8,1280]{3,2,1,0:T(8,128)(2,1)S(1)}, bf16[2,2,8,1280]{3,2,1,0:T(8,128)(2,1)S(1)}, u32[]{:S(2)}, u32[]{:S(2)}) collective-permute-start(bf16[2,2,8,1280]{3,2,1,0:T(8,128)(2,1)S(1)} %add_convert_fusion.8), channel_id=1, source_target_pairs={{0,240},{16,0},{32,16},{48,32},{64,48},{80,64},{96,80},{112,96},{1... | collective-permute-start | bytes 245768 | tf_op jit(solution)/shard_map/ppermute | solution.py:31
  148.9 5.3 %collective-permute-start.23 = (bf16[2,2,8,1280]{3,2,1,0:T(8,128)(2,1)S(1)}, bf16[2,2,8,1280]{3,2,1,0:T(8,128)(2,1)S(1)}, u32[]{:S(2)}, u32[]{:S(2)}) collective-permute-start(bf16[2,2,8,1280]{3,2,1,0:T(8,128)(2,1)S(1)} %get-tuple-element.10), channel_id=1, source_target_pairs={{0,240},{16,0},{32,16},{48,32},{64,48},{80,64},{96,80},{112,96},{1... | collective-permute-start | bytes 245768 | tf_op jit(solution)/shard_map/ppermute | solution.py:31
  162.6 4.5 %collective-permute-done.28 = bf16[2,2,8,1280]{3,2,1,0:T(8,128)(2,1)S(1)} collective-permute-done((bf16[2,2,8,1280]{3,2,1,0:T(8,128)(2,1)S(1)}, bf16[2,2,8,1280]{3,2,1,0:T(8,128)(2,1)S(1)}, u32[]{:S(2)}, u32[]{:S(2)}) %collective-permute-start.28) | collective-permute-done | bytes 81952 | tf_op jit(solution)/shard_map/ppermute | solution.py:31
  181.9 4.6 %collective-permute-start.24 = (bf16[2,2,8,1280]{3,2,1,0:T(8,128)(2,1)S(1)}, bf16[2,2,8,1280]{3,2,1,0:T(8,128)(2,1)S(1)}, u32[]{:S(2)}, u32[]{:S(2)}) collective-permute-start(bf16[2,2,8,1280]{3,2,1,0:T(8,128)(2,1)S(1)} %get-tuple-element.8), channel_id=1, source_target_pairs={{0,240},{16,0},{32,16},{48,32},{64,48},{80,64},{96,80},{112,96},{1... | collective-permute-start | bytes 245768 | tf_op jit(solution)/shard_map/ppermute | solution.py:31
  188.5 5.1 %collective-permute-done.32 = bf16[2,2,8,1280]{3,2,1,0:T(8,128)(2,1)S(1)} collective-permute-done((bf16[2,2,8,1280]{3,2,1,0:T(8,128)(2,1)S(1)}, bf16[2,2,8,1280]{3,2,1,0:T(8,128)(2,1)S(1)}, u32[]{:S(2)}, u32[]{:S(2)}) %collective-permute-start.32) | collective-permute-done | bytes 81952 | tf_op jit(solution)/shard_map/ppermute | solution.py:31
  200.1 27.7 %all-to-all-start.2 = ((bf16[16,8,2688]{2,1,0:T(8,128)(2,1)}), bf16[16,8,2688]{2,1,0:T(8,128)(2,1)S(1)}, u32[]{:S(2)}, u32[]{:S(2)}) async-start(bf16[16,8,2688]{2,1,0:T(8,128)(2,1)} %broadcast_in_dim.13), calls=%async_computation.2 | async-start | bytes 1376256 | tf_op jit(solution)/shard_map/all_to_all | solution.py:75
  229.2 11.3 %all-to-all-done.2 = bf16[16,8,2688]{2,1,0:T(8,128)(2,1)S(1)} async-done(((bf16[16,8,2688]{2,1,0:T(8,128)(2,1)}), bf16[16,8,2688]{2,1,0:T(8,128)(2,1)S(1)}, u32[]{:S(2)}, u32[]{:S(2)}) %all-to-all-start.2) | async-done | bytes 688160 | tf_op jit(solution)/shard_map/all_to_all | solution.py:75
  245.0 4.8 %all-to-all-start.3 = ((f32[16,2,1280]{2,1,0:T(2,128)}), f32[16,2,1280]{2,1,0:T(2,128)S(1)}, u32[]{:S(2)}, u32[]{:S(2)}) async-start(f32[16,2,1280]{2,1,0:T(2,128)} %reshape.338), calls=%async_computation.3 | async-start | bytes 327680 | tf_op jit(solution)/shard_map/all_to_all | solution.py:75
  251.1 6.8 %all-to-all-done.3 = f32[16,2,1280]{2,1,0:T(2,128)S(1)} async-done(((f32[16,2,1280]{2,1,0:T(2,128)}), f32[16,2,1280]{2,1,0:T(2,128)S(1)}, u32[]{:S(2)}, u32[]{:S(2)}) %all-to-all-start.3) | async-done | bytes 163872 | tf_op jit(solution)/shard_map/all_to_all | solution.py:75
  258.6 5.8 %all-to-all-start.4 = ((f32[32,1,80]{2,1,0:T(1,128)}), f32[32,1,80]{2,1,0:T(1,128)S(1)}, u32[]{:S(2)}, u32[]{:S(2)}) async-start(f32[32,1,80]{2,1,0:T(1,128)} %reshape.339), calls=%async_computation.4 | async-start | bytes 32768 | tf_op jit(solution)/shard_map/all_to_all | solution.py:75
  264.6 11.9 %all-to-all-done.4 = f32[32,1,80]{2,1,0:T(1,128)S(1)} async-done(((f32[32,1,80]{2,1,0:T(1,128)}), f32[32,1,80]{2,1,0:T(1,128)S(1)}, u32[]{:S(2)}, u32[]{:S(2)}) %all-to-all-start.4) | async-done | bytes 10272 | tf_op jit(solution)/shard_map/all_to_all | solution.py:75
  282.0 11.0 %all-to-all-done.5 = f32[32,1,80]{2,1,0:T(1,128)S(1)} async-done(((f32[32,1,80]{2,1,0:T(1,128)}), f32[32,1,80]{2,1,0:T(1,128)S(1)}, u32[]{:S(2)}, u32[]{:S(2)}) %all-to-all-start.5) | async-done | bytes 10272 | tf_op jit(solution)/shard_map/all_to_all | solution.py:75
  (183 shorter events, 104.9 us)
Async XLA Ops:
  46.7 11.9 %collective-permute-start.8 = (bf16[2,2,8,1280]{3,2,1,0:T(8,128)(2,1)S(1)}, bf16[2,2,8,1280]{3,2,1,0:T(8,128)(2,1)S(1)}, u32[]{:S(2)}, u32[]{:S(2)}) collective-permute-start(bf16[2,2,8,1280]{3,2,1,0:T(8,128)(2,1)S(1)} %pad_maximum_fusion.1), channel_id=1, source_target_pairs={{0,240},{16,0},{32,16},{48,32},{64,48},{80,64},{96,80},{112,96},{1... | collective-permute-start | bytes 245768 | tf_op jit(solution)/shard_map/ppermute | solution.py:31
  56.7 6.5 %collective-permute-start.1 = (bf16[2,2,8,1280]{3,2,1,0:T(8,128)(2,1)S(1)}, bf16[2,2,8,1280]{3,2,1,0:T(8,128)(2,1)S(1)}, u32[]{:S(2)}, u32[]{:S(2)}) collective-permute-start(bf16[2,2,8,1280]{3,2,1,0:T(8,128)(2,1)S(1)} %pad_maximum_fusion.1), channel_id=1, source_target_pairs={{0,16},{16,32},{32,48},{48,64},{64,80},{80,96},{96,112},{112,128},... | collective-permute-start | bytes 245768 | tf_op jit(solution)/shard_map/ppermute | solution.py:31
  58.6 6.5 %collective-permute-start.9 = (bf16[2,2,8,1280]{3,2,1,0:T(8,128)(2,1)S(1)}, bf16[2,2,8,1280]{3,2,1,0:T(8,128)(2,1)S(1)}, u32[]{:S(2)}, u32[]{:S(2)}) collective-permute-start(bf16[2,2,8,1280]{3,2,1,0:T(8,128)(2,1)S(1)} %collective-permute-done.8), channel_id=1, source_target_pairs={{0,240},{16,0},{32,16},{48,32},{64,48},{80,64},{96,80},{112,96},{1... | collective-permute-start | bytes 245768 | tf_op jit(solution)/shard_map/ppermute | solution.py:31
  63.2 6.5 %collective-permute-start.2 = (bf16[2,2,8,1280]{3,2,1,0:T(8,128)(2,1)S(1)}, bf16[2,2,8,1280]{3,2,1,0:T(8,128)(2,1)S(1)}, u32[]{:S(2)}, u32[]{:S(2)}) collective-permute-start(bf16[2,2,8,1280]{3,2,1,0:T(8,128)(2,1)S(1)} %collective-permute-done.1), channel_id=1, source_target_pairs={{0,16},{16,32},{32,48},{48,64},{64,80},{80,96},{96,112},{112,128},... | collective-permute-start | bytes 245768 | tf_op jit(solution)/shard_map/ppermute | solution.py:31
  65.2 6.5 %collective-permute-start.10 = (bf16[2,2,8,1280]{3,2,1,0:T(8,128)(2,1)S(1)}, bf16[2,2,8,1280]{3,2,1,0:T(8,128)(2,1)S(1)}, u32[]{:S(2)}, u32[]{:S(2)}) collective-permute-start(bf16[2,2,8,1280]{3,2,1,0:T(8,128)(2,1)S(1)} %collective-permute-done.9), channel_id=1, source_target_pairs={{0,240},{16,0},{32,16},{48,32},{64,48},{80,64},{96,80},{112,96},{1... | collective-permute-start | bytes 245768 | tf_op jit(solution)/shard_map/ppermute | solution.py:31
  69.8 6.5 %collective-permute-start.3 = (bf16[2,2,8,1280]{3,2,1,0:T(8,128)(2,1)S(1)}, bf16[2,2,8,1280]{3,2,1,0:T(8,128)(2,1)S(1)}, u32[]{:S(2)}, u32[]{:S(2)}) collective-permute-start(bf16[2,2,8,1280]{3,2,1,0:T(8,128)(2,1)S(1)} %collective-permute-done.2), channel_id=1, source_target_pairs={{0,16},{16,32},{32,48},{48,64},{64,80},{80,96},{96,112},{112,128},... | collective-permute-start | bytes 245768 | tf_op jit(solution)/shard_map/ppermute | solution.py:31
  71.7 6.5 %collective-permute-start.11 = (bf16[2,2,8,1280]{3,2,1,0:T(8,128)(2,1)S(1)}, bf16[2,2,8,1280]{3,2,1,0:T(8,128)(2,1)S(1)}, u32[]{:S(2)}, u32[]{:S(2)}) collective-permute-start(bf16[2,2,8,1280]{3,2,1,0:T(8,128)(2,1)S(1)} %collective-permute-done.10), channel_id=1, source_target_pairs={{0,240},{16,0},{32,16},{48,32},{64,48},{80,64},{96,80},{112,96},{1... | collective-permute-start | bytes 245768 | tf_op jit(solution)/shard_map/ppermute | solution.py:31
  76.3 6.5 %collective-permute-start.4 = (bf16[2,2,8,1280]{3,2,1,0:T(8,128)(2,1)S(1)}, bf16[2,2,8,1280]{3,2,1,0:T(8,128)(2,1)S(1)}, u32[]{:S(2)}, u32[]{:S(2)}) collective-permute-start(bf16[2,2,8,1280]{3,2,1,0:T(8,128)(2,1)S(1)} %collective-permute-done.3), channel_id=1, source_target_pairs={{0,16},{16,32},{32,48},{48,64},{64,80},{80,96},{96,112},{112,128},... | collective-permute-start | bytes 245768 | tf_op jit(solution)/shard_map/ppermute | solution.py:31
  78.2 6.5 %collective-permute-start.12 = (bf16[2,2,8,1280]{3,2,1,0:T(8,128)(2,1)S(1)}, bf16[2,2,8,1280]{3,2,1,0:T(8,128)(2,1)S(1)}, u32[]{:S(2)}, u32[]{:S(2)}) collective-permute-start(bf16[2,2,8,1280]{3,2,1,0:T(8,128)(2,1)S(1)} %collective-permute-done.11), channel_id=1, source_target_pairs={{0,240},{16,0},{32,16},{48,32},{64,48},{80,64},{96,80},{112,96},{1... | collective-permute-start | bytes 245768 | tf_op jit(solution)/shard_map/ppermute | solution.py:31
  82.8 6.5 %collective-permute-start.5 = (bf16[2,2,8,1280]{3,2,1,0:T(8,128)(2,1)S(1)}, bf16[2,2,8,1280]{3,2,1,0:T(8,128)(2,1)S(1)}, u32[]{:S(2)}, u32[]{:S(2)}) collective-permute-start(bf16[2,2,8,1280]{3,2,1,0:T(8,128)(2,1)S(1)} %collective-permute-done.4), channel_id=1, source_target_pairs={{0,16},{16,32},{32,48},{48,64},{64,80},{80,96},{96,112},{112,128},... | collective-permute-start | bytes 245768 | tf_op jit(solution)/shard_map/ppermute | solution.py:31
  89.3 7.2 %collective-permute-start.6 = (bf16[2,2,8,1280]{3,2,1,0:T(8,128)(2,1)S(1)}, bf16[2,2,8,1280]{3,2,1,0:T(8,128)(2,1)S(1)}, u32[]{:S(2)}, u32[]{:S(2)}) collective-permute-start(bf16[2,2,8,1280]{3,2,1,0:T(8,128)(2,1)S(1)} %collective-permute-done.5), channel_id=1, source_target_pairs={{0,16},{16,32},{32,48},{48,64},{64,80},{80,96},{96,112},{112,128},... | collective-permute-start | bytes 245768 | tf_op jit(solution)/shard_map/ppermute | solution.py:31
  91.3 7.2 %collective-permute-start.14 = (bf16[2,2,8,1280]{3,2,1,0:T(8,128)(2,1)S(1)}, bf16[2,2,8,1280]{3,2,1,0:T(8,128)(2,1)S(1)}, u32[]{:S(2)}, u32[]{:S(2)}) collective-permute-start(bf16[2,2,8,1280]{3,2,1,0:T(8,128)(2,1)S(1)} %collective-permute-done.13), channel_id=1, source_target_pairs={{0,240},{16,0},{32,16},{48,32},{64,48},{80,64},{96,80},{112,96},{1... | collective-permute-start | bytes 245768 | tf_op jit(solution)/shard_map/ppermute | solution.py:31
  96.5 6.7 %collective-permute-start.7 = (bf16[2,2,8,1280]{3,2,1,0:T(8,128)(2,1)S(1)}, bf16[2,2,8,1280]{3,2,1,0:T(8,128)(2,1)S(1)}, u32[]{:S(2)}, u32[]{:S(2)}) collective-permute-start(bf16[2,2,8,1280]{3,2,1,0:T(8,128)(2,1)S(1)} %collective-permute-done.6), channel_id=1, source_target_pairs={{0,16},{16,32},{32,48},{48,64},{64,80},{80,96},{96,112},{112,128},... | collective-permute-start | bytes 245768 | tf_op jit(solution)/shard_map/ppermute | solution.py:31
  98.5 6.7 %collective-permute-start.16 = (bf16[1,2,8,1280]{3,2,1,0:T(8,128)(2,1)S(1)}, bf16[1,2,8,1280]{3,2,1,0:T(8,128)(2,1)S(1)}, u32[]{:S(2)}, u32[]{:S(2)}) collective-permute-start(bf16[1,2,8,1280]{3,2,1,0:T(8,128)(2,1)S(1)} %slice.179), channel_id=1, source_target_pairs={{0,240},{16,0},{32,16},{48,32},{64,48},{80,64},{96,80},{112,96},{1... | collective-permute-start | bytes 122888 | tf_op jit(solution)/shard_map/ppermute | solution.py:31
  127.5 6.6 %collective-permute-start.25 = (bf16[1,2,8,1280]{3,2,1,0:T(8,128)(2,1)S(1)}, bf16[1,2,8,1280]{3,2,1,0:T(8,128)(2,1)S(1)}, u32[]{:S(2)}, u32[]{:S(2)}) collective-permute-start(bf16[1,2,8,1280]{3,2,1,0:T(8,128)(2,1)S(1)} %get-tuple-element.22), channel_id=1, source_target_pairs={{0,16},{16,32},{32,48},{48,64},{64,80},{80,96},{96,112},{112,128},... | collective-permute-start | bytes 122888 | tf_op jit(solution)/shard_map/ppermute | solution.py:31
  135.6 6.9 %collective-permute-start.21 = (bf16[2,2,8,1280]{3,2,1,0:T(8,128)(2,1)S(1)}, bf16[2,2,8,1280]{3,2,1,0:T(8,128)(2,1)S(1)}, u32[]{:S(2)}, u32[]{:S(2)}) collective-permute-start(bf16[2,2,8,1280]{3,2,1,0:T(8,128)(2,1)S(1)} %add_convert_fusion.9), channel_id=1, source_target_pairs={{0,240},{16,0},{32,16},{48,32},{64,48},{80,64},{96,80},{112,96},{1... | collective-permute-start | bytes 245768 | tf_op jit(solution)/shard_map/ppermute | solution.py:31
  140.5 6.7 %collective-permute-start.26 = (bf16[2,2,8,1280]{3,2,1,0:T(8,128)(2,1)S(1)}, bf16[2,2,8,1280]{3,2,1,0:T(8,128)(2,1)S(1)}, u32[]{:S(2)}, u32[]{:S(2)}) collective-permute-start(bf16[2,2,8,1280]{3,2,1,0:T(8,128)(2,1)S(1)} %pad_maximum_fusion.4), channel_id=1, source_target_pairs={{0,16},{16,32},{32,48},{48,64},{64,80},{80,96},{96,112},{112,128},... | collective-permute-start | bytes 245768 | tf_op jit(solution)/shard_map/ppermute | solution.py:31
  148.9 7.3 %collective-permute-start.23 = (bf16[2,2,8,1280]{3,2,1,0:T(8,128)(2,1)S(1)}, bf16[2,2,8,1280]{3,2,1,0:T(8,128)(2,1)S(1)}, u32[]{:S(2)}, u32[]{:S(2)}) collective-permute-start(bf16[2,2,8,1280]{3,2,1,0:T(8,128)(2,1)S(1)} %get-tuple-element.10), channel_id=1, source_target_pairs={{0,240},{16,0},{32,16},{48,32},{64,48},{80,64},{96,80},{112,96},{1... | collective-permute-start | bytes 245768 | tf_op jit(solution)/shard_map/ppermute | solution.py:31
  181.9 6.6 %collective-permute-start.24 = (bf16[2,2,8,1280]{3,2,1,0:T(8,128)(2,1)S(1)}, bf16[2,2,8,1280]{3,2,1,0:T(8,128)(2,1)S(1)}, u32[]{:S(2)}, u32[]{:S(2)}) collective-permute-start(bf16[2,2,8,1280]{3,2,1,0:T(8,128)(2,1)S(1)} %get-tuple-element.8), channel_id=1, source_target_pairs={{0,240},{16,0},{32,16},{48,32},{64,48},{80,64},{96,80},{112,96},{1... | collective-permute-start | bytes 245768 | tf_op jit(solution)/shard_map/ppermute | solution.py:31
  186.5 7.1 %collective-permute-start.32 = (bf16[2,2,8,1280]{3,2,1,0:T(8,128)(2,1)S(1)}, bf16[2,2,8,1280]{3,2,1,0:T(8,128)(2,1)S(1)}, u32[]{:S(2)}, u32[]{:S(2)}) collective-permute-start(bf16[2,2,8,1280]{3,2,1,0:T(8,128)(2,1)S(1)} %add_convert_fusion), channel_id=1, source_target_pairs={{0,16},{16,32},{32,48},{48,64},{64,80},{80,96},{96,112},{112,128},... | collective-permute-start | bytes 245768 | tf_op jit(solution)/shard_map/ppermute | solution.py:31
  200.1 40.5 %all-to-all-start.2 = ((bf16[16,8,2688]{2,1,0:T(8,128)(2,1)}), bf16[16,8,2688]{2,1,0:T(8,128)(2,1)S(1)}, u32[]{:S(2)}, u32[]{:S(2)}) async-start(bf16[16,8,2688]{2,1,0:T(8,128)(2,1)} %broadcast_in_dim.13), calls=%async_computation.2 | async-start | bytes 1376256 | tf_op jit(solution)/shard_map/all_to_all | solution.py:75
  245.0 12.8 %all-to-all-start.3 = ((f32[16,2,1280]{2,1,0:T(2,128)}), f32[16,2,1280]{2,1,0:T(2,128)S(1)}, u32[]{:S(2)}, u32[]{:S(2)}) async-start(f32[16,2,1280]{2,1,0:T(2,128)} %reshape.338), calls=%async_computation.3 | async-start | bytes 327680 | tf_op jit(solution)/shard_map/all_to_all | solution.py:75
  258.6 17.9 %all-to-all-start.4 = ((f32[32,1,80]{2,1,0:T(1,128)}), f32[32,1,80]{2,1,0:T(1,128)S(1)}, u32[]{:S(2)}, u32[]{:S(2)}) async-start(f32[32,1,80]{2,1,0:T(1,128)} %reshape.339), calls=%async_computation.4 | async-start | bytes 32768 | tf_op jit(solution)/shard_map/all_to_all | solution.py:75
  277.2 15.8 %all-to-all-start.5 = ((f32[32,1,80]{2,1,0:T(1,128)}), f32[32,1,80]{2,1,0:T(1,128)S(1)}, u32[]{:S(2)}, u32[]{:S(2)}) async-start(f32[32,1,80]{2,1,0:T(1,128)} %broadcast_in_dim.14), calls=%async_computation.5 | async-start | bytes 32768 | tf_op jit(solution)/shard_map/all_to_all | solution.py:75
  (24 other events, 254.0 us)

commit v2 on v1

v2 whole, which is shorter than its diff:
```python
import jax
import jax.numpy as jnp
import numpy as np
from jax import lax
from jax.sharding import PartitionSpec as P

F32 = jnp.float32
BF16 = jnp.bfloat16


def gelu_exact(value):
    return jax.nn.gelu(value, approximate=False)


def split3(value):
    high = lax.reduce_precision(value, 8, 7)
    middle = lax.reduce_precision(value - high, 8, 7)
    low = value - high - middle
    return [high.astype(BF16), middle.astype(BF16), low.astype(BF16)]


def join3(terms):
    wide = terms.astype(F32)
    return wide[..., 0:1] + wide[..., 1:2] + wide[..., 2:3]


def groups_of(axis, sizes, inner):
    shape = [lax.axis_size(axis) // sizes[0] // sizes[1], sizes[0], sizes[1]]
    ids = np.arange(lax.axis_size(axis)).reshape(shape)
    outer = [part for part in range(3) if part not in inner]
    width = int(np.prod([shape[part] for part in inner]))
    return ids.transpose(outer + list(inner)).reshape(-1, width).tolist()


def exchange(value, axis, groups=None):
    return lax.all_to_all(
        value, axis, split_axis=0, concat_axis=0, axis_index_groups=groups, tiled=True
    )


def everywhere(value, axis, groups=None):
    peers = lax.axis_size(axis) if groups is None else len(groups[0])
    return exchange(jnp.broadcast_to(value[None], (peers,) + value.shape), axis, groups)


def dp_groups(*inner):
    depth = lax.axis_size("dp") // 2
    near = 4 if depth >= 16 else 2
    return groups_of("dp", (depth // near, near), inner)


def expert_groups(*inner):
    return groups_of("expert", (2, 2), inner)


def gather_dp(own):
    rows, d = own.shape[1:]
    far = everywhere(own, "dp", dp_groups(1))
    near = everywhere(far, "dp", dp_groups(2))
    near = jnp.transpose(near, (2, 0, 1, 3, 4)).reshape(2, -1, d)
    return everywhere(near, "dp", dp_groups(0))


def reduce_dp(partial, rows):
    d = partial.shape[-1]
    near, far = len(dp_groups(2)[0]), len(dp_groups(1)[0])
    total = jnp.sum(exchange(partial, "dp", dp_groups(0)).astype(F32), axis=0).astype(BF16)
    total = jnp.transpose(total.reshape(2, near, far * rows, d), (1, 0, 2, 3))
    total = jnp.sum(exchange(total, "dp", dp_groups(2)).astype(F32), axis=0).astype(BF16)
    total = jnp.transpose(total.reshape(2, far, rows, d), (1, 0, 2, 3))
    return jnp.sum(exchange(total, "dp", dp_groups(1)).astype(F32), axis=0)


def expert_part(gathered, w_in, w_out, imgs):
    slots, d, width = w_in.shape
    all_in = gathered[:, 0].reshape(-1, d)
    all_out_grad = gathered[:, 1].reshape(-1, d)
    row = lax.broadcasted_iota(jnp.int32, (slots, all_in.shape[0], 1), 1)
    slot = lax.broadcasted_iota(jnp.int32, (slots, all_in.shape[0], 1), 0)
    mine = (row // imgs) % slots == slot
    preact = jnp.einsum("rd,sdh->srh", all_in, w_in, preferred_element_type=F32)
    activated_wide, pullback = jax.vjp(gelu_exact, preact)
    activated = jnp.where(mine, activated_wide, 0.0).astype(BF16)
    slot_out = jnp.einsum("srh,shd->rd", activated, w_out, preferred_element_type=F32)
    act_grad = jnp.einsum("rd,shd->srh", all_out_grad, w_out, preferred_element_type=F32)
    preact_grad = jnp.where(mine, pullback(act_grad)[0], 0.0).astype(BF16)
    slot_in_grad = jnp.einsum("srh,sdh->rd", preact_grad, w_in, preferred_element_type=F32)
    w_out_grad = jnp.einsum(
        "srh,rd->shd", activated, all_out_grad, preferred_element_type=F32
    ).astype(BF16)
    w_in_grad = jnp.einsum(
        "rd,srh->sdh", all_in, preact_grad, preferred_element_type=F32
    ).astype(BF16)
    shape = (gathered.shape[0], 1) + gathered.shape[2:]
    partial = jnp.concatenate(
        [slot_out.astype(BF16).reshape(shape), slot_in_grad.astype(BF16).reshape(shape)], axis=1
    )
    return partial, w_in_grad, w_out_grad


def on_device(tokens, cotangent, slot_params, w_in, w_out):
    imgs, share, d = tokens.shape
    peers = lax.axis_size("expert")
    own_slots = slot_params.shape[1]
    slots = peers * own_slots
    rows = own_slots * imgs

    params = everywhere(slot_params.T, "expert", expert_groups(1, 2))
    params = everywhere(params, "expert", expert_groups(0)).reshape(slots, d)
    logits = jnp.einsum("sd,bmd->sbm", params, tokens, preferred_element_type=F32)
    combine = jax.nn.softmax(logits, axis=0)
    combine_b = combine.astype(BF16)
    peak = jnp.max(logits, axis=2, keepdims=True)
    weight = jnp.exp(logits - peak)
    mass = jnp.sum(weight, axis=2, keepdims=True)
    part_in = jnp.einsum("sbm,bmd->sbd", weight.astype(BF16), tokens, preferred_element_type=F32)
    part_grad = jnp.einsum("sbm,bmd->sbd", combine_b, cotangent, preferred_element_type=F32)
    stats = jnp.concatenate(
        split3(peak) + split3(mass) + [jnp.zeros((slots, imgs, 122), BF16)], axis=2
    )
    sent = jnp.concatenate([part_in.astype(BF16), stats, part_grad.astype(BF16)], axis=2)
    taken = exchange(sent.reshape(peers, rows, 2 * d + 128), "expert")

    peaks = join3(taken[:, :, d : d + 3])
    masses = join3(taken[:, :, d + 3 : d + 6])
    top = jnp.max(peaks, axis=0)
    scale = jnp.exp(peaks - top[None])
    total = jnp.sum(masses * scale, axis=0)
    slot_in_wide = jnp.sum(taken[:, :, :d].astype(F32) * scale, axis=0) / total
    slot_out_grad = jnp.sum(taken[:, :, d + 128 :].astype(F32), axis=0)
    own = jnp.stack([slot_in_wide.astype(BF16), slot_out_grad.astype(BF16)])

    gathered = gather_dp(own)
    partial, w_in_grad, w_out_grad = expert_part(gathered, w_in, w_out, imgs)
    owned_b = reduce_dp(partial, rows).astype(BF16)

    col = jnp.sum(owned_b[1].astype(F32) * slot_in_wide, axis=1, keepdims=True)
    stats = jnp.concatenate(
        split3(top) + split3(total) + split3(col) + [jnp.zeros((rows, 119), BF16)], axis=1
    )
    back = everywhere(jnp.concatenate([owned_b[0], owned_b[1], stats], axis=1), "expert")
    back = back.reshape(slots, imgs, 2 * d + 128)
    slot_out, slot_in_grad = back[:, :, :d], back[:, :, d : 2 * d]
    top = join3(back[:, :, 2 * d : 2 * d + 3])
    total = join3(back[:, :, 2 * d + 3 : 2 * d + 6])
    col = join3(back[:, :, 2 * d + 6 : 2 * d + 9])

    dispatch = jnp.exp(logits - top) / total
    dispatch_b = dispatch.astype(BF16)
    combine_grad = jnp.einsum("bmd,sbd->sbm", cotangent, slot_out, preferred_element_type=F32)
    dispatch_grad = jnp.einsum("sbd,bmd->sbm", slot_in_grad, tokens, preferred_element_type=F32)
    row_sums = jnp.sum(combine * combine_grad, axis=0, keepdims=True)
    logit_grad = (
        dispatch * (dispatch_grad - col) + combine * (combine_grad - row_sums)
    ).astype(BF16)
    token_grad = jnp.einsum("sbm,sbd->bmd", dispatch_b, slot_in_grad, preferred_element_type=F32)
    token_grad = token_grad + jnp.einsum(
        "sbm,sd->bmd", logit_grad, params, preferred_element_type=F32
    )
    token_grad = token_grad.astype(BF16)

    share_grad = jnp.einsum("sbm,bmd->sd", logit_grad, tokens, preferred_element_type=F32)
    share_grad = share_grad.reshape(peers // 4, 4 * own_slots, d)
    share_grad = jnp.sum(exchange(share_grad, "expert", expert_groups(0)), axis=0)
    share_grad = share_grad.reshape(4, own_slots, d)
    share_grad = jnp.sum(exchange(share_grad, "expert", expert_groups(1, 2)), axis=0)
    share_grad = jnp.sum(everywhere(share_grad, "dp", dp_groups(1)), axis=0)
    share_grad = jnp.sum(everywhere(share_grad, "dp", dp_groups(0, 2)), axis=0)
    slot_grad = share_grad.T
    return (token_grad, slot_grad, w_in_grad, w_out_grad)


def solution(mesh):
    placed = (
        P("dp", "expert", None),
        P("dp", "expert", None),
        P(None, "expert"),
        P("expert", None, "dp"),
        P("expert", "dp", None),
    )
    return jax.shard_map(
        on_device,
        mesh=mesh,
        in_specs=placed,
        out_specs=(
            P("dp", "expert", None),
            P(None, "expert"),
            P("expert", None, "dp"),
            P("expert", "dp", None),
        ),
        check_vma=False,
    )
```

time: 297 us -> 245 us (0.82)
  starting transfers between devices: 152 us -> 22 us
  blocking collectives: 33.3 us -> 147 us
  waiting for transfers between devices: 81.8 us -> 45.8 us
    all_to_all x2 -> x9, blocking collectives: 33.3 us -> 147 us  [exchange(): lax.all_to_all(value, axis, split_axis=0, concat_axis=0, axis_index_group...]
    ppermute x34 -> x0, starting transfers between devices: 110 us -> none  [the longest x32 106 us: along_z(): return lax.ppermute(value, 'dp', pairs)]
    ppermute x34 -> x0, waiting for transfers between devices: 40.8 us -> none  [the longest x32 36.2 us: along_z(): return lax.ppermute(value, 'dp', pairs)]
    all_to_all x4 -> x5, starting transfers between devices: 42 us -> 22 us  [exchange(): lax.all_to_all(value, axis, split_axis=0, concat_axis=0, axis_index_group...]
    all_to_all x4 -> x5, waiting for transfers between devices: 41 us -> 45.8 us  [exchange(): lax.all_to_all(value, axis, split_axis=0, concat_axis=0, axis_index_group...]
  transfers between devices with their start and end apart: 38 -> 5, of which waited for: 18 -> 5; matrix products, arithmetic and copies ran while one was open for 2% -> 2% of each run, Pallas kernels for 0% -> 0%
where the time goes in v2:
time: 245 us; the launch traced here: 243 us
  blocking collectives  147 us (60%)
  waiting for transfers between devices  45.8 us (19%)
  starting transfers between devices  22 us (9%)
  local copies, waits for them, and re-layouts  10.9 us (4%)
  matrix products  10.9 us (4%)
  other arithmetic  5.24 us (2%)
    all_to_all x9, blocking collectives, exchange(): lax.all_to_all(value, axis, split_axis=0, concat_axis=0, axis_index_group...  147 us
    all_to_all x5, waiting for transfers between devices, exchange(): lax.all_to_all(value, axis, split_axis=0, concat_axis=0, axis_index_group...  45.8 us
    all_to_all x5, starting transfers between devices, exchange(): lax.all_to_all(value, axis, split_axis=0, concat_axis=0, axis_index_group...  22 us
  transfers between devices with their start and end apart: 5, of which 5 were waited for; matrix products, arithmetic and copies ran while one was open for 2% of the time, Pallas kernels for 0%

profile of v2, /device:TPU:1, one launch (start us, length us, event | category | flops | bytes accessed | tf_op | source)
XLA Modules:
  0.0 243.4 jit_solution(3087972303216648412)
XLA Ops:
  1.5 13.9 %all_to_all.70 = bf16[4,2,1280]{2,1,0:T(2,128)(2,1)S(1)} all-to-all(bf16[4,2,1280]{2,1,0:T(2,128)(2,1)S(1)} %broadcast_in_dim.38), channel_id=1, replica_groups={{0,1,2,3},{4,5,6,7},{8,9,10,11},{12,13,14,15},{16,17,18,19},{20,21,22,2..., dimensions={0} | all-to-all | bytes 40960 | tf_op jit(solution)/shard_map/all_to_all | solution.py:36
  15.4 6.9 %all_to_all.71 = bf16[4,4,2,1280]{3,2,1,0:T(2,128)(2,1)S(1)} all-to-all(bf16[4,4,2,1280]{3,2,1,0:T(2,128)(2,1)S(1)} %broadcast_in_dim.39), channel_id=1, replica_groups={{0,4,8,12},{1,5,9,13},{2,6,10,14},{3,7,11,15},{16,20,24,28},{17,21,25,2..., dimensions={0} | all-to-all | bytes 163840 | tf_op jit(solution)/shard_map/all_to_all | solution.py:36
  24.2 1.2 fusion.5
  28.3 18.0 %all_to_all.72 = bf16[16,8,2688]{2,1,0:T(8,128)(2,1)S(1)} all-to-all(bf16[16,8,2688]{2,1,0:T(8,128)(2,1)S(1)} %concatenate.16), channel_id=1, replica_groups=mesh['dp'=32,'expert'=16] {'expert'}, dimensions={0} | all-to-all | bytes 1376256 | tf_op jit(solution)/shard_map/all_to_all | solution.py:36
  47.3 25.7 %all_to_all.73 = bf16[4,2,8,1280]{3,2,1,0:T(8,128)(2,1)S(1)} all-to-all(bf16[4,2,8,1280]{3,2,1,0:T(8,128)(2,1)S(1)} %broadcast_in_dim.42), channel_id=1, replica_groups={{0,64,128,192},{16,80,144,208},{32,96,160,224},{48,112,176,240},{256,32..., dimensions={0} | all-to-all | bytes 327680 | tf_op jit(solution)/shard_map/all_to_all | solution.py:36
  73.1 20.3 %all_to_all.74 = bf16[4,4,2,8,1280]{4,3,1,2,0:T(8,128)(2,1)S(1)} all-to-all(bf16[4,4,2,8,1280]{4,3,1,2,0:T(8,128)(2,1)S(1)} %broadcast_in_dim.43), channel_id=1, replica_groups={{0,16,32,48},{64,80,96,112},{128,144,160,176},{192,208,224,240},{256,27..., dimensions={0} | all-to-all | bytes 1310720 | tf_op jit(solution)/shard_map/all_to_all | solution.py:36
  94.6 3.6 %all-to-all-start.5 = ((bf16[2,2,128,1280]{3,2,1,0:T(8,128)(2,1)}), bf16[2,2,128,1280]{3,2,1,0:T(8,128)(2,1)S(1)}, u32[]{:S(2)}, u32[]{:S(2)}) async-start(bf16[2,2,128,1280]{3,2,1,0:T(8,128)(2,1)} %broadcast_in_dim.45), calls=%async_computation.5 | async-start | bytes 2621440 | tf_op jit(solution)/shard_map/all_to_all | solution.py:36
  98.3 13.8 %all-to-all-done.5 = bf16[2,2,128,1280]{3,2,1,0:T(8,128)(2,1)S(1)} async-done(((bf16[2,2,128,1280]{3,2,1,0:T(8,128)(2,1)}), bf16[2,2,128,1280]{3,2,1,0:T(8,128)(2,1)S(1)}, u32[]{:S(2)}, u32[]{:S(2)}) %all-to-all-start.5) | async-done | bytes 1310752 | tf_op jit(solution)/shard_map/all_to_all | solution.py:36
  115.7 15.4 %all_to_all.75 = bf16[2,2,128,1280]{3,2,1,0:T(8,128)(2,1)S(1)} all-to-all(bf16[2,2,128,1280]{3,2,1,0:T(8,128)(2,1)S(1)} %pad_maximum_fusion), channel_id=1, replica_groups={{0,256},{16,272},{32,288},{48,304},{64,320},{80,336},{96,352},{112,368}..., dimensions={0} | all-to-all | bytes 2621440 | tf_op jit(solution)/shard_map/all_to_all | solution.py:36
  131.1 1.2 reduce_sum.153
  133.4 20.2 %all_to_all.76 = bf16[4,2,32,1280]{3,2,1,0:T(8,128)(2,1)S(1)} all-to-all(bf16[4,2,32,1280]{3,2,1,0:T(8,128)(2,1)S(1)} %copy.219), channel_id=1, replica_groups={{0,16,32,48},{64,80,96,112},{128,144,160,176},{192,208,224,240},{256,27..., dimensions={0} | all-to-all | bytes 1310720 | tf_op jit(solution)/shard_map/all_to_all | solution.py:36
  154.4 6.2 %all-to-all-start.8 = ((bf16[4,2,8,1280]{3,2,1,0:T(8,128)(2,1)}), bf16[4,2,8,1280]{3,2,1,0:T(8,128)(2,1)S(1)}, u32[]{:S(2)}, u32[]{:S(2)}) async-start(bf16[4,2,8,1280]{3,2,1,0:T(8,128)(2,1)} %copy.220), calls=%async_computation.8 | async-start | bytes 327680 | tf_op jit(solution)/shard_map/all_to_all | solution.py:36
  161.1 13.3 %all-to-all-done.8 = bf16[4,2,8,1280]{3,2,1,0:T(8,128)(2,1)S(1)} async-done(((bf16[4,2,8,1280]{3,2,1,0:T(8,128)(2,1)}), bf16[4,2,8,1280]{3,2,1,0:T(8,128)(2,1)S(1)}, u32[]{:S(2)}, u32[]{:S(2)}) %all-to-all-start.8) | async-done | bytes 163872 | tf_op jit(solution)/shard_map/all_to_all | solution.py:36
  175.1 19.6 %all_to_all.77 = bf16[16,8,2688]{2,1,0:T(8,128)(2,1)S(1)} all-to-all(bf16[16,8,2688]{2,1,0:T(8,128)(2,1)S(1)} %broadcast_in_dim.47), channel_id=1, replica_groups=mesh['dp'=32,'expert'=16] {'expert'}, dimensions={0} | all-to-all | bytes 1376256 | tf_op jit(solution)/shard_map/all_to_all | solution.py:36
  196.7 1.2 convolution_bitcast_fusion.4
  198.5 7.5 %all_to_all.78 = f32[4,8,1280]{2,1,0:T(8,128)S(1)} all-to-all(f32[4,8,1280]{2,1,0:T(8,128)S(1)} %convolution_bitcast_fusion.2), channel_id=1, replica_groups={{0,4,8,12},{1,5,9,13},{2,6,10,14},{3,7,11,15},{16,20,24,28},{17,21,25,2..., dimensions={0} | all-to-all | bytes 327680 | tf_op jit(solution)/shard_map/all_to_all | solution.py:36
  206.7 4.8 %all-to-all-start.11 = ((f32[4,2,1280]{2,1,0:T(2,128)}), f32[4,2,1280]{2,1,0:T(2,128)S(1)}, u32[]{:S(2)}, u32[]{:S(2)}) async-start(f32[4,2,1280]{2,1,0:T(2,128)} %reshape.380), calls=%async_computation.11 | async-start | bytes 81920 | tf_op jit(solution)/shard_map/all_to_all | solution.py:36
  211.4 1.3 convolution_convert_fusion
  212.7 3.4 %all-to-all-done.11 = f32[4,2,1280]{2,1,0:T(2,128)S(1)} async-done(((f32[4,2,1280]{2,1,0:T(2,128)}), f32[4,2,1280]{2,1,0:T(2,128)S(1)}, u32[]{:S(2)}, u32[]{:S(2)}) %all-to-all-start.11) | async-done | bytes 40992 | tf_op jit(solution)/shard_map/all_to_all | solution.py:36
  216.8 4.1 %all-to-all-start.12 = ((f32[4,2,1280]{2,1,0:T(2,128)}), f32[4,2,1280]{2,1,0:T(2,128)S(1)}, u32[]{:S(2)}, u32[]{:S(2)}) async-start(f32[4,2,1280]{2,1,0:T(2,128)} %broadcast_in_dim.88), calls=%async_computation.12 | async-start | bytes 81920 | tf_op jit(solution)/shard_map/all_to_all | solution.py:36
  220.9 1.3 fusion.4
  222.2 10.6 %all-to-all-done.12 = f32[4,2,1280]{2,1,0:T(2,128)S(1)} async-done(((f32[4,2,1280]{2,1,0:T(2,128)}), f32[4,2,1280]{2,1,0:T(2,128)S(1)}, u32[]{:S(2)}, u32[]{:S(2)}) %all-to-all-start.12) | async-done | bytes 40992 | tf_op jit(solution)/shard_map/all_to_all | solution.py:36
  233.5 3.4 %all-to-all-start.13 = ((f32[8,2,1280]{2,1,0:T(2,128)}), f32[8,2,1280]{2,1,0:T(2,128)S(1)}, u32[]{:S(2)}, u32[]{:S(2)}) async-start(f32[8,2,1280]{2,1,0:T(2,128)} %broadcast_in_dim.89), calls=%async_computation.13 | async-start | bytes 163840 | tf_op jit(solution)/shard_map/all_to_all | solution.py:36
  238.0 4.7 %all-to-all-done.13 = f32[8,2,1280]{2,1,0:T(2,128)S(1)} async-done(((f32[8,2,1280]{2,1,0:T(2,128)}), f32[8,2,1280]{2,1,0:T(2,128)S(1)}, u32[]{:S(2)}, u32[]{:S(2)}) %all-to-all-start.13) | async-done | bytes 81952 | tf_op jit(solution)/shard_map/all_to_all | solution.py:36
  (113 shorter events, 20.8 us)
Async XLA Ops:
  0.6 111.5 %copy-start = (bf16[2,1280,160]{1,2,0:T(8,128)(2,1)S(1)}, bf16[2,1280,160]{1,2,0:T(8,128)(2,1)}, u32[]{:S(2)}) copy-start(bf16[2,1280,160]{1,2,0:T(8,128)(2,1)} %param.8) | copy-start | bytes 2457604
  0.6 24.9 %copy-start.8 = (bf16[4,16,1280]{2,1,0:T(8,128)(2,1)S(1)}, bf16[4,16,1280]{2,1,0:T(8,128)(2,1)}, u32[]{:S(2)}) copy-start(bf16[4,16,1280]{2,1,0:T(8,128)(2,1)} %param.6) | copy-start | bytes 491524
  22.3 1.9 copy-start.2
  94.6 17.5 %all-to-all-start.5 = ((bf16[2,2,128,1280]{3,2,1,0:T(8,128)(2,1)}), bf16[2,2,128,1280]{3,2,1,0:T(8,128)(2,1)S(1)}, u32[]{:S(2)}, u32[]{:S(2)}) async-start(bf16[2,2,128,1280]{3,2,1,0:T(8,128)(2,1)} %broadcast_in_dim.45), calls=%async_computation.5 | async-start | bytes 2621440 | tf_op jit(solution)/shard_map/all_to_all | solution.py:36
  112.1 1.2 copy-start.10
  113.3 1.1 copy-start.4
  114.4 1.1 copy-start.6
  154.4 20.0 %all-to-all-start.8 = ((bf16[4,2,8,1280]{3,2,1,0:T(8,128)(2,1)}), bf16[4,2,8,1280]{3,2,1,0:T(8,128)(2,1)S(1)}, u32[]{:S(2)}, u32[]{:S(2)}) async-start(bf16[4,2,8,1280]{3,2,1,0:T(8,128)(2,1)} %copy.220), calls=%async_computation.8 | async-start | bytes 327680 | tf_op jit(solution)/shard_map/all_to_all | solution.py:36
  194.9 3.0 %copy-start.1 = (bf16[4,16,1280]{2,1,0:T(8,128)(2,1)S(1)}, bf16[4,16,1280]{2,1,0:T(8,128)(2,1)}, u32[]{:S(2)}) copy-start(bf16[4,16,1280]{2,1,0:T(8,128)(2,1)} %param.5) | copy-start | bytes 491524
  195.9 2.2 copy-start.9
  196.6 14.9 %copy-start.5 = (bf16[2,256,160]{1,2,0:T(8,128)(2,1)S(1)}, bf16[2,256,160]{1,2,0:T(8,128)(2,1)}, u32[]{:S(2)}) copy-start(bf16[2,256,160]{1,2,0:T(8,128)(2,1)} %copy-done.4) | copy-start | bytes 491524
  198.5 22.4 %copy-start.7 = (bf16[2,256,160]{1,2,0:T(8,128)(2,1)S(1)}, bf16[2,256,160]{1,2,0:T(8,128)(2,1)}, u32[]{:S(2)}) copy-start(bf16[2,256,160]{1,2,0:T(8,128)(2,1)} %copy-done.6) | copy-start | bytes 491524
  206.7 9.5 %all-to-all-start.11 = ((f32[4,2,1280]{2,1,0:T(2,128)}), f32[4,2,1280]{2,1,0:T(2,128)S(1)}, u32[]{:S(2)}, u32[]{:S(2)}) async-start(f32[4,2,1280]{2,1,0:T(2,128)} %reshape.380), calls=%async_computation.11 | async-start | bytes 81920 | tf_op jit(solution)/shard_map/all_to_all | solution.py:36
  216.8 16.0 %all-to-all-start.12 = ((f32[4,2,1280]{2,1,0:T(2,128)}), f32[4,2,1280]{2,1,0:T(2,128)S(1)}, u32[]{:S(2)}, u32[]{:S(2)}) async-start(f32[4,2,1280]{2,1,0:T(2,128)} %broadcast_in_dim.88), calls=%async_computation.12 | async-start | bytes 81920 | tf_op jit(solution)/shard_map/all_to_all | solution.py:36
  220.9 16.1 %copy-start.3 = (bf16[32,1280,1]{1,0,2:T(8,128)(2,1)S(1)}, bf16[32,1280,1]{1,0,2:T(8,128)(2,1)}, u32[]{:S(2)}) copy-start(bf16[32,1280,1]{1,0,2:T(8,128)(2,1)} %copy-done.2) | copy-start | bytes 245764
  233.5 9.3 %all-to-all-start.13 = ((f32[8,2,1280]{2,1,0:T(2,128)}), f32[8,2,1280]{2,1,0:T(2,128)S(1)}, u32[]{:S(2)}, u32[]{:S(2)}) async-start(f32[8,2,1280]{2,1,0:T(2,128)} %broadcast_in_dim.89), calls=%async_computation.13 | async-start | bytes 163840 | tf_op jit(solution)/shard_map/all_to_all | solution.py:36

commit v3 on v2

--- a/solution.py
+++ b/solution.py
@@ -44,30 +44,20 @@
 
 
 def dp_groups(*inner):
-    depth = lax.axis_size("dp") // 2
-    near = 4 if depth >= 16 else 2
-    return groups_of("dp", (depth // near, near), inner)
-
-
-def expert_groups(*inner):
-    return groups_of("expert", (2, 2), inner)
+    return groups_of("dp", (lax.axis_size("dp") // 4, 2), inner)
 
 
 def gather_dp(own):
     rows, d = own.shape[1:]
     far = everywhere(own, "dp", dp_groups(1))
-    near = everywhere(far, "dp", dp_groups(2))
-    near = jnp.transpose(near, (2, 0, 1, 3, 4)).reshape(2, -1, d)
-    return everywhere(near, "dp", dp_groups(0))
+    far = jnp.transpose(far, (1, 0, 2, 3)).reshape(2, -1, d)
+    return everywhere(far, "dp", dp_groups(0, 2))
 
 
 def reduce_dp(partial, rows):
     d = partial.shape[-1]
-    near, far = len(dp_groups(2)[0]), len(dp_groups(1)[0])
-    total = jnp.sum(exchange(partial, "dp", dp_groups(0)).astype(F32), axis=0).astype(BF16)
-    total = jnp.transpose(total.reshape(2, near, far * rows, d), (1, 0, 2, 3))
-    total = jnp.sum(exchange(total, "dp", dp_groups(2)).astype(F32), axis=0).astype(BF16)
-    total = jnp.transpose(total.reshape(2, far, rows, d), (1, 0, 2, 3))
+    total = jnp.sum(exchange(partial, "dp", dp_groups(0, 2)).astype(F32), axis=0).astype(BF16)
+    total = jnp.transpose(total.reshape(2, -1, rows, d), (1, 0, 2, 3))
     return jnp.sum(exchange(total, "dp", dp_groups(1)).astype(F32), axis=0)
 
 
@@ -105,8 +95,7 @@
     slots = peers * own_slots
     rows = own_slots * imgs
 
-    params = everywhere(slot_params.T, "expert", expert_groups(1, 2))
-    params = everywhere(params, "expert", expert_groups(0)).reshape(slots, d)
+    params = everywhere(slot_params.T, "expert").reshape(slots, d)
     logits = jnp.einsum("sd,bmd->sbm", params, tokens, preferred_element_type=F32)
     combine = jax.nn.softmax(logits, axis=0)
     combine_b = combine.astype(BF16)
@@ -160,10 +149,7 @@
     token_grad = token_grad.astype(BF16)
 
     share_grad = jnp.einsum("sbm,bmd->sd", logit_grad, tokens, preferred_element_type=F32)
-    share_grad = share_grad.reshape(peers // 4, 4 * own_slots, d)
-    share_grad = jnp.sum(exchange(share_grad, "expert", expert_groups(0)), axis=0)
-    share_grad = share_grad.reshape(4, own_slots, d)
-    share_grad = jnp.sum(exchange(share_grad, "expert", expert_groups(1, 2)), axis=0)
+    share_grad = jnp.sum(exchange(share_grad.reshape(peers, own_slots, d), "expert"), axis=0)
     share_grad = jnp.sum(everywhere(share_grad, "dp", dp_groups(1)), axis=0)
     share_grad = jnp.sum(everywhere(share_grad, "dp", dp_groups(0, 2)), axis=0)
     slot_grad = share_grad.T

time: 245 us -> 211 us (0.86)
  blocking collectives: 147 us -> 106 us
  waiting for transfers between devices: 45.8 us -> 54.8 us
    all_to_all x9 -> x5, blocking collectives: 147 us -> 106 us  [exchange(): lax.all_to_all(value, axis, split_axis=0, concat_axis=0, axis_index_group...]
    all_to_all x5, waiting for transfers between devices: 45.8 us -> 54.8 us  [exchange(): lax.all_to_all(value, axis, split_axis=0, concat_axis=0, axis_index_group...]
where the time goes in v3:
time: 211 us; the launch traced here: 209 us
  blocking collectives  106 us (50%)
  waiting for transfers between devices  54.8 us (26%)
  starting transfers between devices  20.6 us (10%)
  local copies, waits for them, and re-layouts  10.9 us (5%)
  matrix products  10.8 us (5%)
  other arithmetic  4.96 us (2%)
    all_to_all x5, blocking collectives, exchange(): lax.all_to_all(value, axis, split_axis=0, concat_axis=0, axis_index_group...  106 us
    all_to_all x5, waiting for transfers between devices, exchange(): lax.all_to_all(value, axis, split_axis=0, concat_axis=0, axis_index_group...  54.8 us
    all_to_all x5, starting transfers between devices, exchange(): lax.all_to_all(value, axis, split_axis=0, concat_axis=0, axis_index_group...  20.6 us
  transfers between devices with their start and end apart: 5, of which 5 were waited for; matrix products, arithmetic and copies ran while one was open for 2% of the time, Pallas kernels for 0%

profile of v3, /device:TPU:1, one launch (start us, length us, event | category | flops | bytes accessed | tf_op | source)
XLA Modules:
  0.0 208.8 jit_solution(490682711992401905)
XLA Ops:
  1.5 16.7 %all_to_all.50 = bf16[16,2,1280]{2,1,0:T(2,128)(2,1)S(1)} all-to-all(bf16[16,2,1280]{2,1,0:T(2,128)(2,1)S(1)} %broadcast_in_dim.34), channel_id=1, replica_groups=mesh['dp'=32,'expert'=16] {'expert'}, dimensions={0} | all-to-all | bytes 163840 | tf_op jit(solution)/shard_map/all_to_all | solution.py:36
  18.3 1.1 fusion.68
  20.1 1.2 fusion.5
  24.2 16.5 %all_to_all.51 = bf16[16,8,2688]{2,1,0:T(8,128)(2,1)S(1)} all-to-all(bf16[16,8,2688]{2,1,0:T(8,128)(2,1)S(1)} %concatenate.16), channel_id=1, replica_groups=mesh['dp'=32,'expert'=16] {'expert'}, dimensions={0} | all-to-all | bytes 1376256 | tf_op jit(solution)/shard_map/all_to_all | solution.py:36
  41.8 34.4 %all_to_all.52 = bf16[8,2,8,1280]{3,2,1,0:T(8,128)(2,1)S(1)} all-to-all(bf16[8,2,8,1280]{3,2,1,0:T(8,128)(2,1)S(1)} %broadcast_in_dim.37), channel_id=1, replica_groups={{0,32,64,96,128,160,192,224},{16,48,80,112,144,176,208,240},{256,288,32..., dimensions={0} | all-to-all | bytes 655360 | tf_op jit(solution)/shard_map/all_to_all | solution.py:36
  76.3 1.1 broadcast_in_dim.39
  77.4 3.5 %all-to-all-start.3 = ((bf16[4,2,64,1280]{3,2,1,0:T(8,128)(2,1)}), bf16[4,2,64,1280]{3,2,1,0:T(8,128)(2,1)S(1)}, u32[]{:S(2)}, u32[]{:S(2)}) async-start(bf16[4,2,64,1280]{3,2,1,0:T(8,128)(2,1)} %broadcast_in_dim.39), calls=%async_computation.3 | async-start | bytes 2621440 | tf_op jit(solution)/shard_map/all_to_all | solution.py:36
  81.0 15.5 %all-to-all-done.3 = bf16[4,2,64,1280]{3,2,1,0:T(8,128)(2,1)S(1)} async-done(((bf16[4,2,64,1280]{3,2,1,0:T(8,128)(2,1)}), bf16[4,2,64,1280]{3,2,1,0:T(8,128)(2,1)S(1)}, u32[]{:S(2)}, u32[]{:S(2)}) %all-to-all-start.3) | async-done | bytes 1310752 | tf_op jit(solution)/shard_map/all_to_all | solution.py:36
  97.7 1.1 fusion.27
  100.1 16.8 %all_to_all.53 = bf16[4,2,64,1280]{3,2,1,0:T(8,128)(2,1)S(1)} all-to-all(bf16[4,2,64,1280]{3,2,1,0:T(8,128)(2,1)S(1)} %pad_maximum_fusion), channel_id=1, replica_groups={{0,16,256,272},{32,48,288,304},{64,80,320,336},{96,112,352,368},{128,14..., dimensions={0} | all-to-all | bytes 2621440 | tf_op jit(solution)/shard_map/all_to_all | solution.py:36
  117.9 1.7 copy.179
  119.6 6.7 %all-to-all-start.5 = ((bf16[8,2,8,1280]{3,2,1,0:T(8,128)(2,1)}), bf16[8,2,8,1280]{3,2,1,0:T(8,128)(2,1)S(1)}, u32[]{:S(2)}, u32[]{:S(2)}) async-start(bf16[8,2,8,1280]{3,2,1,0:T(8,128)(2,1)} %copy.179), calls=%async_computation.5 | async-start | bytes 655360 | tf_op jit(solution)/shard_map/all_to_all | solution.py:36
  126.9 19.2 %all-to-all-done.5 = bf16[8,2,8,1280]{3,2,1,0:T(8,128)(2,1)S(1)} async-done(((bf16[8,2,8,1280]{3,2,1,0:T(8,128)(2,1)}), bf16[8,2,8,1280]{3,2,1,0:T(8,128)(2,1)S(1)}, u32[]{:S(2)}, u32[]{:S(2)}) %all-to-all-start.5) | async-done | bytes 327712 | tf_op jit(solution)/shard_map/all_to_all | solution.py:36
  146.8 21.1 %all_to_all.54 = bf16[16,8,2688]{2,1,0:T(8,128)(2,1)S(1)} all-to-all(bf16[16,8,2688]{2,1,0:T(8,128)(2,1)S(1)} %broadcast_in_dim.73), channel_id=1, replica_groups=mesh['dp'=32,'expert'=16] {'expert'}, dimensions={0} | all-to-all | bytes 1376256 | tf_op jit(solution)/shard_map/all_to_all | solution.py:36
  169.9 1.2 convolution_bitcast_fusion.4
  172.5 3.7 %all-to-all-start.7 = ((f32[16,2,1280]{2,1,0:T(2,128)}), f32[16,2,1280]{2,1,0:T(2,128)S(1)}, u32[]{:S(2)}, u32[]{:S(2)}) async-start(f32[16,2,1280]{2,1,0:T(2,128)} %reshape.370), calls=%async_computation.7 | async-start | bytes 327680 | tf_op jit(solution)/shard_map/all_to_all | solution.py:36
  176.2 1.3 convolution_convert_fusion
  177.5 6.8 %all-to-all-done.7 = f32[16,2,1280]{2,1,0:T(2,128)S(1)} async-done(((f32[16,2,1280]{2,1,0:T(2,128)}), f32[16,2,1280]{2,1,0:T(2,128)S(1)}, u32[]{:S(2)}, u32[]{:S(2)}) %all-to-all-start.7) | async-done | bytes 163872 | tf_op jit(solution)/shard_map/all_to_all | solution.py:36
  185.0 3.4 %all-to-all-start.8 = ((f32[8,2,1280]{2,1,0:T(2,128)}), f32[8,2,1280]{2,1,0:T(2,128)S(1)}, u32[]{:S(2)}, u32[]{:S(2)}) async-start(f32[8,2,1280]{2,1,0:T(2,128)} %broadcast_in_dim.74), calls=%async_computation.8 | async-start | bytes 163840 | tf_op jit(solution)/shard_map/all_to_all | solution.py:36
  188.3 1.3 fusion.4
  189.8 10.9 %all-to-all-done.8 = f32[8,2,1280]{2,1,0:T(2,128)S(1)} async-done(((f32[8,2,1280]{2,1,0:T(2,128)}), f32[8,2,1280]{2,1,0:T(2,128)S(1)}, u32[]{:S(2)}, u32[]{:S(2)}) %all-to-all-start.8) | async-done | bytes 81952 | tf_op jit(solution)/shard_map/all_to_all | solution.py:36
  201.3 3.3 %all-to-all-start.9 = ((f32[4,2,1280]{2,1,0:T(2,128)}), f32[4,2,1280]{2,1,0:T(2,128)S(1)}, u32[]{:S(2)}, u32[]{:S(2)}) async-start(f32[4,2,1280]{2,1,0:T(2,128)} %broadcast_in_dim.75), calls=%async_computation.9 | async-start | bytes 81920 | tf_op jit(solution)/shard_map/all_to_all | solution.py:36
  204.6 1.0 fusion.7
  205.6 2.6 %all-to-all-done.9 = f32[4,2,1280]{2,1,0:T(2,128)S(1)} async-done(((f32[4,2,1280]{2,1,0:T(2,128)}), f32[4,2,1280]{2,1,0:T(2,128)S(1)}, u32[]{:S(2)}, u32[]{:S(2)}) %all-to-all-start.9) | async-done | bytes 40992 | tf_op jit(solution)/shard_map/all_to_all | solution.py:36
  (103 shorter events, 15.6 us)
Async XLA Ops:
  0.6 95.9 %copy-start = (bf16[2,1280,160]{1,2,0:T(8,128)(2,1)S(1)}, bf16[2,1280,160]{1,2,0:T(8,128)(2,1)}, u32[]{:S(2)}) copy-start(bf16[2,1280,160]{1,2,0:T(8,128)(2,1)} %param.8) | copy-start | bytes 2457604
  0.6 20.8 %copy-start.8 = (bf16[4,16,1280]{2,1,0:T(8,128)(2,1)S(1)}, bf16[4,16,1280]{2,1,0:T(8,128)(2,1)}, u32[]{:S(2)}) copy-start(bf16[4,16,1280]{2,1,0:T(8,128)(2,1)} %param.6) | copy-start | bytes 491524
  18.3 1.9 copy-start.2
  77.4 19.0 %all-to-all-start.3 = ((bf16[4,2,64,1280]{3,2,1,0:T(8,128)(2,1)}), bf16[4,2,64,1280]{3,2,1,0:T(8,128)(2,1)S(1)}, u32[]{:S(2)}, u32[]{:S(2)}) async-start(bf16[4,2,64,1280]{3,2,1,0:T(8,128)(2,1)} %broadcast_in_dim.39), calls=%async_computation.3 | async-start | bytes 2621440 | tf_op jit(solution)/shard_map/all_to_all | solution.py:36
  96.6 1.2 copy-start.10
  97.7 1.1 copy-start.4
  98.8 1.1 copy-start.6
  119.6 26.5 %all-to-all-start.5 = ((bf16[8,2,8,1280]{3,2,1,0:T(8,128)(2,1)}), bf16[8,2,8,1280]{3,2,1,0:T(8,128)(2,1)S(1)}, u32[]{:S(2)}, u32[]{:S(2)}) async-start(bf16[8,2,8,1280]{3,2,1,0:T(8,128)(2,1)} %copy.179), calls=%async_computation.5 | async-start | bytes 655360 | tf_op jit(solution)/shard_map/all_to_all | solution.py:36
  168.1 3.0 %copy-start.1 = (bf16[4,16,1280]{2,1,0:T(8,128)(2,1)S(1)}, bf16[4,16,1280]{2,1,0:T(8,128)(2,1)}, u32[]{:S(2)}) copy-start(bf16[4,16,1280]{2,1,0:T(8,128)(2,1)} %param.5) | copy-start | bytes 491524
  169.2 2.2 %copy-start.9 = (f32[32,4,16]{0,2,1:T(8,128)S(1)}, f32[32,4,16]{0,2,1:T(8,128)}, u32[]{:S(2)}) copy-start(f32[32,4,16]{0,2,1:T(8,128)} %get-tuple-element.35) | copy-start | bytes 24580
  169.8 6.4 %copy-start.5 = (bf16[2,256,160]{1,2,0:T(8,128)(2,1)S(1)}, bf16[2,256,160]{1,2,0:T(8,128)(2,1)}, u32[]{:S(2)}) copy-start(bf16[2,256,160]{1,2,0:T(8,128)(2,1)} %copy-done.4) | copy-start | bytes 491524
  171.7 16.6 %copy-start.7 = (bf16[2,256,160]{1,2,0:T(8,128)(2,1)S(1)}, bf16[2,256,160]{1,2,0:T(8,128)(2,1)}, u32[]{:S(2)}) copy-start(bf16[2,256,160]{1,2,0:T(8,128)(2,1)} %copy-done.6) | copy-start | bytes 491524
  172.5 11.7 %all-to-all-start.7 = ((f32[16,2,1280]{2,1,0:T(2,128)}), f32[16,2,1280]{2,1,0:T(2,128)S(1)}, u32[]{:S(2)}, u32[]{:S(2)}) async-start(f32[16,2,1280]{2,1,0:T(2,128)} %reshape.370), calls=%async_computation.7 | async-start | bytes 327680 | tf_op jit(solution)/shard_map/all_to_all | solution.py:36
  185.0 15.7 %all-to-all-start.8 = ((f32[8,2,1280]{2,1,0:T(2,128)}), f32[8,2,1280]{2,1,0:T(2,128)S(1)}, u32[]{:S(2)}, u32[]{:S(2)}) async-start(f32[8,2,1280]{2,1,0:T(2,128)} %broadcast_in_dim.74), calls=%async_computation.8 | async-start | bytes 163840 | tf_op jit(solution)/shard_map/all_to_all | solution.py:36
  188.3 16.3 %copy-start.3 = (bf16[32,1280,1]{1,0,2:T(8,128)(2,1)S(1)}, bf16[32,1280,1]{1,0,2:T(8,128)(2,1)}, u32[]{:S(2)}) copy-start(bf16[32,1280,1]{1,0,2:T(8,128)(2,1)} %copy-done.2) | copy-start | bytes 245764
  201.3 6.9 %all-to-all-start.9 = ((f32[4,2,1280]{2,1,0:T(2,128)}), f32[4,2,1280]{2,1,0:T(2,128)S(1)}, u32[]{:S(2)}, u32[]{:S(2)}) async-start(f32[4,2,1280]{2,1,0:T(2,128)} %broadcast_in_dim.75), calls=%async_computation.9 | async-start | bytes 81920 | tf_op jit(solution)/shard_map/all_to_all | solution.py:36

commit v4 on v3

--- a/solution.py
+++ b/solution.py
@@ -48,30 +48,30 @@
 
 
 def gather_dp(own):
-    rows, d = own.shape[1:]
-    far = everywhere(own, "dp", dp_groups(1))
-    far = jnp.transpose(far, (1, 0, 2, 3)).reshape(2, -1, d)
-    return everywhere(far, "dp", dp_groups(0, 2))
+    return everywhere(everywhere(own, "dp", dp_groups(1)), "dp", dp_groups(0, 2))
 
 
 def reduce_dp(partial, rows):
     d = partial.shape[-1]
     total = jnp.sum(exchange(partial, "dp", dp_groups(0, 2)).astype(F32), axis=0).astype(BF16)
-    total = jnp.transpose(total.reshape(2, -1, rows, d), (1, 0, 2, 3))
-    return jnp.sum(exchange(total, "dp", dp_groups(1)).astype(F32), axis=0)
+    return jnp.sum(exchange(total.reshape(-1, rows, d), "dp", dp_groups(1)).astype(F32), axis=0)
 
 
-def expert_part(gathered, w_in, w_out, imgs):
-    slots, d, width = w_in.shape
-    all_in = gathered[:, 0].reshape(-1, d)
-    all_out_grad = gathered[:, 1].reshape(-1, d)
-    row = lax.broadcasted_iota(jnp.int32, (slots, all_in.shape[0], 1), 1)
-    slot = lax.broadcasted_iota(jnp.int32, (slots, all_in.shape[0], 1), 0)
-    mine = (row // imgs) % slots == slot
+def slot_mask(rows, slots, imgs):
+    row = lax.broadcasted_iota(jnp.int32, (slots, rows, 1), 1)
+    slot = lax.broadcasted_iota(jnp.int32, (slots, rows, 1), 0)
+    return (row // imgs) % slots == slot
+
+
+def expert_forward(all_in, w_in, w_out, mine):
     preact = jnp.einsum("rd,sdh->srh", all_in, w_in, preferred_element_type=F32)
-    activated_wide, pullback = jax.vjp(gelu_exact, preact)
-    activated = jnp.where(mine, activated_wide, 0.0).astype(BF16)
+    activated = jnp.where(mine, gelu_exact(preact), 0.0).astype(BF16)
     slot_out = jnp.einsum("srh,shd->rd", activated, w_out, preferred_element_type=F32)
+    return preact, activated, slot_out.astype(BF16)
+
+
+def expert_backward(all_in, all_out_grad, preact, activated, w_in, w_out, mine):
+    _, pullback = jax.vjp(gelu_exact, preact)
     act_grad = jnp.einsum("rd,shd->srh", all_out_grad, w_out, preferred_element_type=F32)
     preact_grad = jnp.where(mine, pullback(act_grad)[0], 0.0).astype(BF16)
     slot_in_grad = jnp.einsum("srh,sdh->rd", preact_grad, w_in, preferred_element_type=F32)
@@ -81,11 +81,7 @@
     w_in_grad = jnp.einsum(
         "rd,srh->sdh", all_in, preact_grad, preferred_element_type=F32
     ).astype(BF16)
-    shape = (gathered.shape[0], 1) + gathered.shape[2:]
-    partial = jnp.concatenate(
-        [slot_out.astype(BF16).reshape(shape), slot_in_grad.astype(BF16).reshape(shape)], axis=1
-    )
-    return partial, w_in_grad, w_out_grad
+    return slot_in_grad.astype(BF16), w_in_grad, w_out_grad
 
 
 def on_device(tokens, cotangent, slot_params, w_in, w_out):
@@ -117,17 +113,22 @@
     total = jnp.sum(masses * scale, axis=0)
     slot_in_wide = jnp.sum(taken[:, :, :d].astype(F32) * scale, axis=0) / total
     slot_out_grad = jnp.sum(taken[:, :, d + 128 :].astype(F32), axis=0)
-    own = jnp.stack([slot_in_wide.astype(BF16), slot_out_grad.astype(BF16)])
+    squared = len(dp_groups(0, 2)[0])
+    all_in = gather_dp(slot_in_wide.astype(BF16)).reshape(-1, d)
+    all_out_grad = gather_dp(slot_out_grad.astype(BF16)).reshape(-1, d)
+    mine = slot_mask(all_in.shape[0], own_slots, imgs)
+    preact, activated, out_partial = expert_forward(all_in, w_in, w_out, mine)
+    owned_out = reduce_dp(out_partial.reshape(squared, -1, d), rows).astype(BF16)
+    in_partial, w_in_grad, w_out_grad = expert_backward(
+        all_in, all_out_grad, preact, activated, w_in, w_out, mine
+    )
+    owned_in = reduce_dp(in_partial.reshape(squared, -1, d), rows).astype(BF16)
 
-    gathered = gather_dp(own)
-    partial, w_in_grad, w_out_grad = expert_part(gathered, w_in, w_out, imgs)
-    owned_b = reduce_dp(partial, rows).astype(BF16)
-
-    col = jnp.sum(owned_b[1].astype(F32) * slot_in_wide, axis=1, keepdims=True)
+    col = jnp.sum(owned_in.astype(F32) * slot_in_wide, axis=1, keepdims=True)
     stats = jnp.concatenate(
         split3(top) + split3(total) + split3(col) + [jnp.zeros((rows, 119), BF16)], axis=1
     )
-    back = everywhere(jnp.concatenate([owned_b[0], owned_b[1], stats], axis=1), "expert")
+    back = everywhere(jnp.concatenate([owned_out, owned_in, stats], axis=1), "expert")
     back = back.reshape(slots, imgs, 2 * d + 128)
     slot_out, slot_in_grad = back[:, :, :d], back[:, :, d : 2 * d]
     top = join3(back[:, :, 2 * d : 2 * d + 3])

time: 211 us -> 238 us (1.13)
  starting transfers between devices: 20.6 us -> 45.8 us
  waiting for transfers between devices: 54.8 us -> 75.7 us
  blocking collectives: 106 us -> 85.7 us
    all_to_all x5 -> x9, starting transfers between devices: 20.6 us -> 45.8 us  [exchange(): lax.all_to_all(value, axis, split_axis=0, concat_axis=0, axis_index_group...]
    all_to_all x5 -> x9, waiting for transfers between devices: 54.8 us -> 75.7 us  [exchange(): lax.all_to_all(value, axis, split_axis=0, concat_axis=0, axis_index_group...]
    all_to_all x5, blocking collectives: 106 us -> 85.7 us  [exchange(): lax.all_to_all(value, axis, split_axis=0, concat_axis=0, axis_index_group...]
    dot_general x5, matrix products: 4.69 us -> 8.73 us  [the longest x1 2.57 us: expert_forward(): jnp.einsum('srh,shd->rd', activated, w_out, preferred_element_type=F32)]
  transfers between devices with their start and end apart: 5 -> 9, of which waited for: 5 -> 9; matrix products, arithmetic and copies ran while one was open for 2% -> 4% of each run, Pallas kernels for 0% -> 0%
where the time goes in v4:
time: 238 us; the launch traced here: 235 us
  blocking collectives  85.7 us (36%)
  waiting for transfers between devices  75.7 us (32%)
  starting transfers between devices  45.8 us (19%)
  matrix products  12.9 us (5%)
  local copies, waits for them, and re-layouts  8.74 us (4%)
  other arithmetic  5.43 us (2%)
    all_to_all x5, blocking collectives, exchange(): lax.all_to_all(value, axis, split_axis=0, concat_axis=0, axis_index_group...  85.7 us
    all_to_all x9, waiting for transfers between devices, exchange(): lax.all_to_all(value, axis, split_axis=0, concat_axis=0, axis_index_group...  75.7 us
    all_to_all x9, starting transfers between devices, exchange(): lax.all_to_all(value, axis, split_axis=0, concat_axis=0, axis_index_group...  45.8 us
  transfers between devices with their start and end apart: 9, of which 9 were waited for; matrix products, arithmetic and copies ran while one was open for 4% of the time, Pallas kernels for 0%

profile of v4, /device:TPU:1, one launch (start us, length us, event | category | flops | bytes accessed | tf_op | source)
XLA Modules:
  0.0 235.4 jit_solution(11613483322246793152)
XLA Ops:
  1.5 16.7 %all_to_all.70 = bf16[16,2,1280]{2,1,0:T(2,128)(2,1)S(1)} all-to-all(bf16[16,2,1280]{2,1,0:T(2,128)(2,1)S(1)} %broadcast_in_dim.36), channel_id=1, replica_groups=mesh['dp'=32,'expert'=16] {'expert'}, dimensions={0} | all-to-all | bytes 163840 | tf_op jit(solution)/shard_map/all_to_all | solution.py:36
  23.4 16.5 %all_to_all.71 = bf16[16,8,2688]{2,1,0:T(8,128)(2,1)S(1)} all-to-all(bf16[16,8,2688]{2,1,0:T(8,128)(2,1)S(1)} %concatenate.13), channel_id=1, replica_groups=mesh['dp'=32,'expert'=16] {'expert'}, dimensions={0} | all-to-all | bytes 1376256 | tf_op jit(solution)/shard_map/all_to_all | solution.py:36
  41.5 13.7 %all-to-all-start.2 = ((bf16[8,8,1280]{2,1,0:T(8,128)(2,1)}), bf16[8,8,1280]{2,1,0:T(8,128)(2,1)S(1)}, u32[]{:S(2)}, u32[]{:S(2)}) async-start(bf16[8,8,1280]{2,1,0:T(8,128)(2,1)} %broadcast_in_dim.39), calls=%async_computation.2 | async-start | bytes 327680 | tf_op jit(solution)/shard_map/all_to_all | solution.py:36
  55.2 14.4 %all-to-all-done.2 = bf16[8,8,1280]{2,1,0:T(8,128)(2,1)S(1)} async-done(((bf16[8,8,1280]{2,1,0:T(8,128)(2,1)}), bf16[8,8,1280]{2,1,0:T(8,128)(2,1)S(1)}, u32[]{:S(2)}, u32[]{:S(2)}) %all-to-all-start.2) | async-done | bytes 163872 | tf_op jit(solution)/shard_map/all_to_all | solution.py:36
  69.7 19.3 %all_to_all.72 = bf16[8,8,1280]{2,1,0:T(8,128)(2,1)S(1)} all-to-all(bf16[8,8,1280]{2,1,0:T(8,128)(2,1)S(1)} %broadcast_in_dim.41), channel_id=1, replica_groups={{0,32,64,96,128,160,192,224},{16,48,80,112,144,176,208,240},{256,288,32..., dimensions={0} | all-to-all | bytes 327680 | tf_op jit(solution)/shard_map/all_to_all | solution.py:36
  89.1 9.2 %all_to_all.73 = bf16[4,8,8,1280]{3,2,1,0:T(8,128)(2,1)S(1)} all-to-all(bf16[4,8,8,1280]{3,2,1,0:T(8,128)(2,1)S(1)} %broadcast_in_dim.40), channel_id=1, replica_groups={{0,16,256,272},{32,48,288,304},{64,80,320,336},{96,112,352,368},{128,14..., dimensions={0} | all-to-all | bytes 1310720 | tf_op jit(solution)/shard_map/all_to_all | solution.py:36
  99.2 3.5 %all-to-all-start.7 = ((bf16[4,8,8,1280]{3,2,1,0:T(8,128)(2,1)}), bf16[4,8,8,1280]{3,2,1,0:T(8,128)(2,1)S(1)}, u32[]{:S(2)}, u32[]{:S(2)}) async-start(bf16[4,8,8,1280]{3,2,1,0:T(8,128)(2,1)} %broadcast_in_dim.42), calls=%async_computation.7 | async-start | bytes 1310720 | tf_op jit(solution)/shard_map/all_to_all | solution.py:36
  103.1 5.7 %all-to-all-done.7 = bf16[4,8,8,1280]{3,2,1,0:T(8,128)(2,1)S(1)} async-done(((bf16[4,8,8,1280]{3,2,1,0:T(8,128)(2,1)}), bf16[4,8,8,1280]{3,2,1,0:T(8,128)(2,1)S(1)}, u32[]{:S(2)}, u32[]{:S(2)}) %all-to-all-start.7) | async-done | bytes 655392 | tf_op jit(solution)/shard_map/all_to_all | solution.py:36
  112.4 3.5 %all-to-all-start.8 = ((bf16[4,64,1280]{2,1,0:T(8,128)(2,1)}), bf16[4,64,1280]{2,1,0:T(8,128)(2,1)S(1)}, u32[]{:S(2)}, u32[]{:S(2)}) async-start(bf16[4,64,1280]{2,1,0:T(8,128)(2,1)} %bitcast.162), calls=%async_computation.8 | async-start | bytes 1310720 | tf_op jit(solution)/shard_map/all_to_all | solution.py:36
  116.7 2.6 %fusion.2 = bf16[256,1280]{1,0:T(8,128)(2,1)} fusion(bf16[2,256,160]{1,2,0:T(8,128)(2,1)S(1)} %fusion.20, bf16[2,160,1280]{2,1,0:T(8,128)(2,1)} %param.9), kind=kOutput, calls=%fused_computation.6 | convolution fusion | flops 210042880 | bytes 1638400 | tf_op jit(solution)/shard_map/srh,shd->rd/dot_general | solution.py:69
  119.2 2.8 %all-to-all-done.8 = bf16[4,64,1280]{2,1,0:T(8,128)(2,1)S(1)} async-done(((bf16[4,64,1280]{2,1,0:T(8,128)(2,1)}), bf16[4,64,1280]{2,1,0:T(8,128)(2,1)S(1)}, u32[]{:S(2)}, u32[]{:S(2)}) %all-to-all-start.8) | async-done | bytes 655392 | tf_op jit(solution)/shard_map/all_to_all | solution.py:36
  122.1 3.5 %all-to-all-start.4 = ((bf16[4,64,1280]{2,1,0:T(8,128)(2,1)}), bf16[4,64,1280]{2,1,0:T(8,128)(2,1)S(1)}, u32[]{:S(2)}, u32[]{:S(2)}) async-start(bf16[4,64,1280]{2,1,0:T(8,128)(2,1)} %bitcast.161), calls=%async_computation.4 | async-start | bytes 1310720 | tf_op jit(solution)/shard_map/all_to_all | solution.py:36
  126.3 6.2 %all-to-all-done.4 = bf16[4,64,1280]{2,1,0:T(8,128)(2,1)S(1)} async-done(((bf16[4,64,1280]{2,1,0:T(8,128)(2,1)}), bf16[4,64,1280]{2,1,0:T(8,128)(2,1)S(1)}, u32[]{:S(2)}, u32[]{:S(2)}) %all-to-all-start.4) | async-done | bytes 655392 | tf_op jit(solution)/shard_map/all_to_all | solution.py:36
  132.6 8.0 %all-to-all-start.9 = ((bf16[8,8,1280]{2,1,0:T(8,128)(2,1)}), bf16[8,8,1280]{2,1,0:T(8,128)(2,1)S(1)}, u32[]{:S(2)}, u32[]{:S(2)}) async-start(bf16[8,8,1280]{2,1,0:T(8,128)(2,1)} %bitcast.163), calls=%async_computation.9 | async-start | bytes 327680 | tf_op jit(solution)/shard_map/all_to_all | solution.py:36
  141.3 13.7 %all-to-all-done.9 = bf16[8,8,1280]{2,1,0:T(8,128)(2,1)S(1)} async-done(((bf16[8,8,1280]{2,1,0:T(8,128)(2,1)}), bf16[8,8,1280]{2,1,0:T(8,128)(2,1)S(1)}, u32[]{:S(2)}, u32[]{:S(2)}) %all-to-all-start.9) | async-done | bytes 163872 | tf_op jit(solution)/shard_map/all_to_all | solution.py:36
  155.0 3.4 %all-to-all-start.5 = ((bf16[8,8,1280]{2,1,0:T(8,128)(2,1)}), bf16[8,8,1280]{2,1,0:T(8,128)(2,1)S(1)}, u32[]{:S(2)}, u32[]{:S(2)}) async-start(bf16[8,8,1280]{2,1,0:T(8,128)(2,1)} %bitcast.13), calls=%async_computation.5 | async-start | bytes 327680 | tf_op jit(solution)/shard_map/all_to_all | solution.py:36
  158.9 13.0 %all-to-all-done.5 = bf16[8,8,1280]{2,1,0:T(8,128)(2,1)S(1)} async-done(((bf16[8,8,1280]{2,1,0:T(8,128)(2,1)}), bf16[8,8,1280]{2,1,0:T(8,128)(2,1)S(1)}, u32[]{:S(2)}, u32[]{:S(2)}) %all-to-all-start.5) | async-done | bytes 163872 | tf_op jit(solution)/shard_map/all_to_all | solution.py:36
  172.1 23.9 %all_to_all.74 = bf16[16,8,2688]{2,1,0:T(8,128)(2,1)S(1)} all-to-all(bf16[16,8,2688]{2,1,0:T(8,128)(2,1)S(1)} %broadcast_in_dim.44), channel_id=1, replica_groups=mesh['dp'=32,'expert'=16] {'expert'}, dimensions={0} | all-to-all | bytes 1376256 | tf_op jit(solution)/shard_map/all_to_all | solution.py:36
  199.3 3.7 %all-to-all-start.11 = ((f32[16,2,1280]{2,1,0:T(2,128)}), f32[16,2,1280]{2,1,0:T(2,128)S(1)}, u32[]{:S(2)}, u32[]{:S(2)}) async-start(f32[16,2,1280]{2,1,0:T(2,128)} %reshape.370), calls=%async_computation.11 | async-start | bytes 327680 | tf_op jit(solution)/shard_map/all_to_all | solution.py:36
  204.3 6.7 %all-to-all-done.11 = f32[16,2,1280]{2,1,0:T(2,128)S(1)} async-done(((f32[16,2,1280]{2,1,0:T(2,128)}), f32[16,2,1280]{2,1,0:T(2,128)S(1)}, u32[]{:S(2)}, u32[]{:S(2)}) %all-to-all-start.11) | async-done | bytes 163872 | tf_op jit(solution)/shard_map/all_to_all | solution.py:36
  211.8 3.4 %all-to-all-start.12 = ((f32[8,2,1280]{2,1,0:T(2,128)}), f32[8,2,1280]{2,1,0:T(2,128)S(1)}, u32[]{:S(2)}, u32[]{:S(2)}) async-start(f32[8,2,1280]{2,1,0:T(2,128)} %broadcast_in_dim.45), calls=%async_computation.12 | async-start | bytes 163840 | tf_op jit(solution)/shard_map/all_to_all | solution.py:36
  216.6 10.6 %all-to-all-done.12 = f32[8,2,1280]{2,1,0:T(2,128)S(1)} async-done(((f32[8,2,1280]{2,1,0:T(2,128)}), f32[8,2,1280]{2,1,0:T(2,128)S(1)}, u32[]{:S(2)}, u32[]{:S(2)}) %all-to-all-start.12) | async-done | bytes 81952 | tf_op jit(solution)/shard_map/all_to_all | solution.py:36
  227.9 3.3 %all-to-all-start.13 = ((f32[4,2,1280]{2,1,0:T(2,128)}), f32[4,2,1280]{2,1,0:T(2,128)S(1)}, u32[]{:S(2)}, u32[]{:S(2)}) async-start(f32[4,2,1280]{2,1,0:T(2,128)} %broadcast_in_dim.46), calls=%async_computation.13 | async-start | bytes 81920 | tf_op jit(solution)/shard_map/all_to_all | solution.py:36
  232.2 2.6 %all-to-all-done.13 = f32[4,2,1280]{2,1,0:T(2,128)S(1)} async-done(((f32[4,2,1280]{2,1,0:T(2,128)}), f32[4,2,1280]{2,1,0:T(2,128)S(1)}, u32[]{:S(2)}, u32[]{:S(2)}) %all-to-all-start.13) | async-done | bytes 40992 | tf_op jit(solution)/shard_map/all_to_all | solution.py:36
  (104 shorter events, 24.5 us)
Async XLA Ops:
  0.6 102.1 %copy-start = (bf16[2,1280,160]{1,2,0:T(8,128)(2,1)S(1)}, bf16[2,1280,160]{1,2,0:T(8,128)(2,1)}, u32[]{:S(2)}) copy-start(bf16[2,1280,160]{1,2,0:T(8,128)(2,1)} %param.8) | copy-start | bytes 2457604
  0.6 19.6 %copy-start.1 = (bf16[4,16,1280]{2,1,0:T(8,128)(2,1)S(1)}, bf16[4,16,1280]{2,1,0:T(8,128)(2,1)}, u32[]{:S(2)}) copy-start(bf16[4,16,1280]{2,1,0:T(8,128)(2,1)} %param.5) | copy-start | bytes 491524
  18.3 1.3 copy-start.3
  20.5 1.7 copy-start.9
  41.5 28.1 %all-to-all-start.2 = ((bf16[8,8,1280]{2,1,0:T(8,128)(2,1)}), bf16[8,8,1280]{2,1,0:T(8,128)(2,1)S(1)}, u32[]{:S(2)}, u32[]{:S(2)}) async-start(bf16[8,8,1280]{2,1,0:T(8,128)(2,1)} %broadcast_in_dim.39), calls=%async_computation.2 | async-start | bytes 327680 | tf_op jit(solution)/shard_map/all_to_all | solution.py:36
  99.2 9.6 %all-to-all-start.7 = ((bf16[4,8,8,1280]{3,2,1,0:T(8,128)(2,1)}), bf16[4,8,8,1280]{3,2,1,0:T(8,128)(2,1)S(1)}, u32[]{:S(2)}, u32[]{:S(2)}) async-start(bf16[4,8,8,1280]{3,2,1,0:T(8,128)(2,1)} %broadcast_in_dim.42), calls=%async_computation.7 | async-start | bytes 1310720 | tf_op jit(solution)/shard_map/all_to_all | solution.py:36
  111.0 1.4 copy-start.7
  112.4 9.6 %all-to-all-start.8 = ((bf16[4,64,1280]{2,1,0:T(8,128)(2,1)}), bf16[4,64,1280]{2,1,0:T(8,128)(2,1)S(1)}, u32[]{:S(2)}, u32[]{:S(2)}) async-start(bf16[4,64,1280]{2,1,0:T(8,128)(2,1)} %bitcast.162), calls=%async_computation.8 | async-start | bytes 1310720 | tf_op jit(solution)/shard_map/all_to_all | solution.py:36
  116.6 2.6 %copy-start.5 = (bf16[2,256,160]{1,2,0:T(8,128)(2,1)}, bf16[2,256,160]{1,2,0:T(8,128)(2,1)S(1)}, u32[]{:S(2)}) copy-start(bf16[2,256,160]{1,2,0:T(8,128)(2,1)S(1)} %fusion.20) | copy-start | bytes 491524
  122.1 10.5 %all-to-all-start.4 = ((bf16[4,64,1280]{2,1,0:T(8,128)(2,1)}), bf16[4,64,1280]{2,1,0:T(8,128)(2,1)S(1)}, u32[]{:S(2)}, u32[]{:S(2)}) async-start(bf16[4,64,1280]{2,1,0:T(8,128)(2,1)} %bitcast.161), calls=%async_computation.4 | async-start | bytes 1310720 | tf_op jit(solution)/shard_map/all_to_all | solution.py:36
  132.6 22.5 %all-to-all-start.9 = ((bf16[8,8,1280]{2,1,0:T(8,128)(2,1)}), bf16[8,8,1280]{2,1,0:T(8,128)(2,1)S(1)}, u32[]{:S(2)}, u32[]{:S(2)}) async-start(bf16[8,8,1280]{2,1,0:T(8,128)(2,1)} %bitcast.163), calls=%async_computation.9 | async-start | bytes 327680 | tf_op jit(solution)/shard_map/all_to_all | solution.py:36
  155.0 16.8 %all-to-all-start.5 = ((bf16[8,8,1280]{2,1,0:T(8,128)(2,1)}), bf16[8,8,1280]{2,1,0:T(8,128)(2,1)S(1)}, u32[]{:S(2)}, u32[]{:S(2)}) async-start(bf16[8,8,1280]{2,1,0:T(8,128)(2,1)} %bitcast.13), calls=%async_computation.5 | async-start | bytes 327680 | tf_op jit(solution)/shard_map/all_to_all | solution.py:36
  196.1 0.9 copy-start.10
  196.5 1.5 copy-start.2
  197.2 1.0 copy-start.11
  198.0 5.0 %copy-start.6 = (bf16[2,256,160]{1,2,0:T(8,128)(2,1)S(1)}, bf16[2,256,160]{1,2,0:T(8,128)(2,1)}, u32[]{:S(2)}) copy-start(bf16[2,256,160]{1,2,0:T(8,128)(2,1)} %copy-done.5) | copy-start | bytes 491524
  199.3 11.7 %all-to-all-start.11 = ((f32[16,2,1280]{2,1,0:T(2,128)}), f32[16,2,1280]{2,1,0:T(2,128)S(1)}, u32[]{:S(2)}, u32[]{:S(2)}) async-start(f32[16,2,1280]{2,1,0:T(2,128)} %reshape.370), calls=%async_computation.11 | async-start | bytes 327680 | tf_op jit(solution)/shard_map/all_to_all | solution.py:36
  203.0 12.1 %copy-start.8 = (bf16[2,256,160]{1,2,0:T(8,128)(2,1)S(1)}, bf16[2,256,160]{1,2,0:T(8,128)(2,1)}, u32[]{:S(2)}) copy-start(bf16[2,256,160]{1,2,0:T(8,128)(2,1)} %copy-done.7) | copy-start | bytes 491524
  211.8 15.4 %all-to-all-start.12 = ((f32[8,2,1280]{2,1,0:T(2,128)}), f32[8,2,1280]{2,1,0:T(2,128)S(1)}, u32[]{:S(2)}, u32[]{:S(2)}) async-start(f32[8,2,1280]{2,1,0:T(2,128)} %broadcast_in_dim.45), calls=%async_computation.12 | async-start | bytes 163840 | tf_op jit(solution)/shard_map/all_to_all | solution.py:36
  216.4 14.7 %copy-start.4 = (bf16[32,1280,1]{1,0,2:T(8,128)(2,1)S(1)}, bf16[32,1280,1]{1,0,2:T(8,128)(2,1)}, u32[]{:S(2)}) copy-start(bf16[32,1280,1]{1,0,2:T(8,128)(2,1)} %copy-done.3) | copy-start | bytes 245764
  227.9 6.9 %all-to-all-start.13 = ((f32[4,2,1280]{2,1,0:T(2,128)}), f32[4,2,1280]{2,1,0:T(2,128)S(1)}, u32[]{:S(2)}, u32[]{:S(2)}) async-start(f32[4,2,1280]{2,1,0:T(2,128)} %broadcast_in_dim.46), calls=%async_computation.13 | async-start | bytes 81920 | tf_op jit(solution)/shard_map/all_to_all | solution.py:36

commit v5 on v3

v5 whole, which is shorter than its diff:
```python
import functools

import jax
import jax.numpy as jnp
import numpy as np
from jax import lax
from jax.experimental import pallas as pl
from jax.experimental.pallas import tpu as pltpu
from jax.sharding import PartitionSpec as P

F32 = jnp.float32
BF16 = jnp.bfloat16


def gelu_exact(value):
    return jax.nn.gelu(value, approximate=False)


def split3(value):
    high = lax.reduce_precision(value, 8, 7)
    middle = lax.reduce_precision(value - high, 8, 7)
    low = value - high - middle
    return [high.astype(BF16), middle.astype(BF16), low.astype(BF16)]


def join3(terms):
    wide = terms.astype(F32)
    return wide[..., 0:1] + wide[..., 1:2] + wide[..., 2:3]


def groups_of(axis, sizes, inner):
    shape = [lax.axis_size(axis) // sizes[0] // sizes[1], sizes[0], sizes[1]]
    ids = np.arange(lax.axis_size(axis)).reshape(shape)
    outer = [part for part in range(3) if part not in inner]
    width = int(np.prod([shape[part] for part in inner]))
    return ids.transpose(outer + list(inner)).reshape(-1, width).tolist()


def exchange(value, axis, groups=None):
    return lax.all_to_all(
        value, axis, split_axis=0, concat_axis=0, axis_index_groups=groups, tiled=True
    )


def everywhere(value, axis, groups=None):
    peers = lax.axis_size(axis) if groups is None else len(groups[0])
    return exchange(jnp.broadcast_to(value[None], (peers,) + value.shape), axis, groups)


def dp_groups(*inner):
    return groups_of("dp", (lax.axis_size("dp") // 4, 2), inner)


def plane_groups():
    peers, depth = lax.axis_size("expert"), lax.axis_size("dp") // 2
    ids = np.arange(2 * depth * peers).reshape(2, depth, peers)
    return ids.transpose(1, 0, 2).reshape(depth, 2 * peers).tolist()


def gather_dp(own):
    far = everywhere(own, "dp", dp_groups(1))
    return everywhere(far.reshape(-1, own.shape[1]), "dp", dp_groups(0, 2))


def reduce_dp(partial, rows):
    d = partial.shape[-1]
    total = jnp.sum(exchange(partial, "dp", dp_groups(0, 2)).astype(F32), axis=0).astype(BF16)
    return jnp.sum(exchange(total.reshape(-1, rows, d), "dp", dp_groups(1)).astype(F32), axis=0)


def dot(left, right, left_dim=1, right_dim=0):
    return lax.dot_general(
        left, right, (((left_dim,), (right_dim,)), ((), ())), preferred_element_type=F32
    )


def own_image(rows, columns, imgs, own_slots, share):
    row = lax.broadcasted_iota(jnp.int32, (rows, columns), 0)
    column = lax.broadcasted_iota(jnp.int32, (rows, columns), 1)
    return (row // own_slots) % imgs == column // share


def slot_rows(rows, slots, imgs, own_slots):
    row = lax.broadcasted_iota(jnp.int32, (rows, slots), 0)
    column = lax.broadcasted_iota(jnp.int32, (rows, slots), 1)
    slot = (row // (imgs * own_slots)) * own_slots + row % own_slots
    return jnp.where(slot == column, 1.0, 0.0).astype(BF16)


def lanes_of(columns, rows):
    lane = lax.broadcasted_iota(jnp.int32, (rows, 128), 1)
    block = jnp.zeros((rows, 128), F32)
    at = 0
    for value in columns:
        high = value.astype(BF16).astype(F32)
        middle = (value - high).astype(BF16).astype(F32)
        for term in (high, middle, value - high - middle):
            block = jnp.where(lane == at, term, block)
            at += 1
    return block.astype(BF16)


def column_of(block, at):
    lane = lax.broadcasted_iota(jnp.int32, block.shape, 1)
    inside = (lane >= 3 * at) & (lane < 3 * at + 3)
    return jnp.sum(jnp.where(inside, block, 0.0), axis=1, keepdims=True)


def route(imgs, own_slots, params_ref, tok_ref, cot_ref, sent_ref, logits_ref, combine_ref):
    tokens, cotangent = tok_ref[...], cot_ref[...]
    slots, d = params_ref.shape
    rows, columns = logits_ref.shape
    spread = dot(slot_rows(rows, slots, imgs, own_slots), params_ref[...]).astype(BF16)
    logits = dot(spread, tokens, 1, 1)
    mine = own_image(rows, columns, imgs, own_slots, columns // imgs)
    logits = jnp.where(mine, logits, jnp.finfo(F32).min)
    logits_ref[...] = logits
    raised = jnp.exp(logits - jnp.max(logits, axis=0, keepdims=True))
    combine = raised / jnp.sum(raised, axis=0, keepdims=True)
    combine_ref[...] = combine
    peak = jnp.max(logits, axis=1, keepdims=True)
    weight = jnp.exp(logits - peak)
    mass = jnp.sum(weight, axis=1, keepdims=True)
    sent_ref[:, :d] = dot(weight.astype(BF16), tokens).astype(BF16)
    sent_ref[:, d : d + 128] = lanes_of([peak, mass], rows)
    sent_ref[:, d + 128 :] = dot(combine.astype(BF16), cotangent).astype(BF16)


def finish(
    imgs, own_slots, back_ref, logits_ref, combine_ref, params_ref, tok_ref, cot_ref,
    token_grad_ref, share_ref,
):
    tokens, cotangent = tok_ref[...], cot_ref[...]
    slots, d = params_ref.shape
    rows = logits_ref.shape[0]
    slot_out, slot_in_grad = back_ref[:, :d], back_ref[:, d : 2 * d]
    stats = back_ref[:, 2 * d :].astype(F32)
    top, total, col = [column_of(stats, at) for at in range(3)]
    combine = combine_ref[...]
    dispatch = jnp.exp(logits_ref[...] - top) / total
    combine_grad = dot(slot_out, cotangent, 1, 1)
    dispatch_grad = dot(slot_in_grad, tokens, 1, 1)
    row_sums = jnp.sum(combine * combine_grad, axis=0, keepdims=True)
    logit_grad = dispatch * (dispatch_grad - col) + combine * (combine_grad - row_sums)
    members = slot_rows(rows, slots, imgs, own_slots)
    by_slot = dot(members, logit_grad.astype(BF16), 0, 0).astype(BF16)
    share_ref[...] = dot(by_slot, tokens).astype(BF16)
    token_grad = dot(dispatch.astype(BF16), slot_in_grad, 0, 0)
    token_grad = token_grad + dot(by_slot, params_ref[...], 0, 0)
    token_grad_ref[...] = token_grad.astype(BF16)


def call(kernel, out_shape, *operands):
    shapes = [jax.ShapeDtypeStruct(shape, dtype) for shape, dtype in out_shape]
    return pl.pallas_call(
        kernel,
        out_shape=shapes,
        compiler_params=pltpu.CompilerParams(vmem_limit_bytes=32 * 1024 * 1024),
        cost_estimate=pl.CostEstimate(flops=120_000_000, bytes_accessed=2_000_000, transcendentals=16384),
    )(*operands)


def expert_part(gathered, w_in, w_out, imgs):
    slots, d, _ = w_in.shape
    rows = slots * imgs
    blocks = (gathered.shape[0], gathered.shape[1] // (2 * rows), rows, d)
    halves = gathered.reshape(blocks[:2] + (2 * rows, d))
    all_in = halves[:, :, :rows].reshape(-1, d)
    all_out_grad = halves[:, :, rows:].reshape(-1, d)
    row = lax.broadcasted_iota(jnp.int32, (slots, all_in.shape[0], 1), 1)
    slot = lax.broadcasted_iota(jnp.int32, (slots, all_in.shape[0], 1), 0)
    mine = row % slots == slot
    preact = jnp.einsum("rd,sdh->srh", all_in, w_in, preferred_element_type=F32)
    activated_wide, pullback = jax.vjp(gelu_exact, preact)
    activated = jnp.where(mine, activated_wide, 0.0).astype(BF16)
    slot_out = jnp.einsum("srh,shd->rd", activated, w_out, preferred_element_type=F32)
    act_grad = jnp.einsum("rd,shd->srh", all_out_grad, w_out, preferred_element_type=F32)
    preact_grad = jnp.where(mine, pullback(act_grad)[0], 0.0).astype(BF16)
    slot_in_grad = jnp.einsum("srh,sdh->rd", preact_grad, w_in, preferred_element_type=F32)
    w_out_grad = jnp.einsum(
        "srh,rd->shd", activated, all_out_grad, preferred_element_type=F32
    ).astype(BF16)
    w_in_grad = jnp.einsum(
        "rd,srh->sdh", all_in, preact_grad, preferred_element_type=F32
    ).astype(BF16)
    pair = [value.astype(BF16).reshape(blocks) for value in (slot_out, slot_in_grad)]
    partial = jnp.concatenate(pair, axis=2).reshape(gathered.shape)
    return partial, w_in_grad, w_out_grad


def on_device(tokens, cotangent, slot_params, w_in, w_out):
    imgs, share, d = tokens.shape
    peers = lax.axis_size("expert")
    own_slots = slot_params.shape[1]
    slots = peers * own_slots
    rows = own_slots * imgs

    params = everywhere(slot_params.T, "expert").reshape(slots, d)
    flat_tok, flat_cot = tokens.reshape(-1, d), cotangent.reshape(-1, d)
    pairs = (peers * rows, imgs * share)
    sent, logits, combine = call(
        functools.partial(route, imgs, own_slots),
        [((peers * rows, 2 * d + 128), BF16), (pairs, F32), (pairs, F32)],
        params, flat_tok, flat_cot,
    )
    taken = exchange(sent.reshape(peers, rows, 2 * d + 128), "expert")

    peaks = join3(taken[:, :, d : d + 3])
    masses = join3(taken[:, :, d + 3 : d + 6])
    top = jnp.max(peaks, axis=0)
    scale = jnp.exp(peaks - top[None])
    total = jnp.sum(masses * scale, axis=0)
    slot_in_wide = jnp.sum(taken[:, :, :d].astype(F32) * scale, axis=0) / total
    slot_out_grad = jnp.sum(taken[:, :, d + 128 :].astype(F32), axis=0)
    own = jnp.concatenate([slot_in_wide.astype(BF16), slot_out_grad.astype(BF16)], axis=0)

    gathered = gather_dp(own)
    partial, w_in_grad, w_out_grad = expert_part(gathered, w_in, w_out, imgs)
    owned_b = reduce_dp(partial, 2 * rows).astype(BF16).reshape(2, rows, d)

    col = jnp.sum(owned_b[1].astype(F32) * slot_in_wide, axis=1, keepdims=True)
    stats = jnp.concatenate(
        split3(top) + split3(total) + split3(col) + [jnp.zeros((rows, 119), BF16)], axis=1
    )
    back = everywhere(jnp.concatenate([owned_b[0], owned_b[1], stats], axis=1), "expert")
    token_grad, share_grad = call(
        functools.partial(finish, imgs, own_slots),
        [(flat_tok.shape, BF16), ((slots, d), BF16)],
        back.reshape(peers * rows, 2 * d + 128), logits, combine, params, flat_tok, flat_cot,
    )
    token_grad = token_grad.reshape(tokens.shape)

    share_grad = jnp.broadcast_to(share_grad.reshape(1, peers, own_slots, d), (2, peers, own_slots, d))
    share_grad = exchange(
        share_grad.reshape(2 * peers, own_slots, d), ("dp", "expert"), plane_groups()
    )
    share_grad = jnp.sum(share_grad.astype(F32), axis=0).astype(BF16)
    share_grad = everywhere(share_grad, "dp", dp_groups(1, 2))
    share_grad = jnp.sum(share_grad.astype(F32), axis=0)
    slot_grad = share_grad.T
    return (token_grad, slot_grad, w_in_grad, w_out_grad)


def solution(mesh):
    placed = (
        P("dp", "expert", None),
        P("dp", "expert", None),
        P(None, "expert"),
        P("expert", None, "dp"),
        P("expert", "dp", None),
    )
    return jax.shard_map(
        on_device,
        mesh=mesh,
        in_specs=placed,
        out_specs=(
            P("dp", "expert", None),
            P(None, "expert"),
            P("expert", None, "dp"),
            P("expert", "dp", None),
        ),
        check_vma=False,
    )
```

time: 211 us -> 193 us (0.915)
  blocking collectives: 106 us -> 117 us
  waiting for transfers between devices: 54.8 us -> 43.8 us
  starting transfers between devices: 20.6 us -> 13.8 us
  matrix products: 10.8 us -> 5.12 us
  local copies, waits for them, and re-layouts: 10.9 us -> 6.4 us
  Pallas kernels: 0 us -> 2.26 us
    all_to_all x5 -> x3, waiting for transfers between devices: 54.8 us -> 43.8 us  [exchange(): lax.all_to_all(value, axis, split_axis=0, concat_axis=0, axis_index_group...]
    all_to_all x5 -> x6, blocking collectives: 106 us -> 117 us  [exchange(): lax.all_to_all(value, axis, split_axis=0, concat_axis=0, axis_index_group...]
    all_to_all x5 -> x3, starting transfers between devices: 20.6 us -> 13.8 us  [exchange(): lax.all_to_all(value, axis, split_axis=0, concat_axis=0, axis_index_group...]
    dot_general x8 -> x0, matrix products: 5.74 us -> none  [the longest x1 1.21 us: on_device(): jnp.einsum('bmd,sbd->sbm', cotangent, slot_out, preferred_element_type=F32)]
    unnamed x22 -> x18, local copies, waits for them, and re-layouts: 0.06 us -> 2.35 us
    pallas_call x0 -> x2, Pallas kernels: none -> 2.26 us  [call(): pl.pallas_call(kernel, out_shape=shapes, compiler_params=pltpu.CompilerPa...]
  transfers between devices with their start and end apart: 5 -> 3, of which waited for: 5 -> 3; matrix products, arithmetic and copies ran while one was open for 2% -> 2% of each run, Pallas kernels for 0% -> 0%
where the time goes in v5:
time: 193 us; the launch traced here: 192 us
  blocking collectives  117 us (61%)
  waiting for transfers between devices  43.8 us (23%)
  starting transfers between devices  13.8 us (7%)
  local copies, waits for them, and re-layouts  6.4 us (3%)
  matrix products  5.12 us (3%)
  other arithmetic  3.48 us (2%)
  Pallas kernels  2.26 us (1%)
    all_to_all x6, blocking collectives, exchange(): lax.all_to_all(value, axis, split_axis=0, concat_axis=0, axis_index_group...  117 us
    all_to_all x3, waiting for transfers between devices, exchange(): lax.all_to_all(value, axis, split_axis=0, concat_axis=0, axis_index_group...  43.8 us
    all_to_all x3, starting transfers between devices, exchange(): lax.all_to_all(value, axis, split_axis=0, concat_axis=0, axis_index_group...  13.8 us
  transfers between devices with their start and end apart: 3, of which 3 were waited for; matrix products, arithmetic and copies ran while one was open for 2% of the time, Pallas kernels for 0%

profile of v5, /device:TPU:1, one launch (start us, length us, event | category | flops | bytes accessed | tf_op | source)
XLA Modules:
  0.0 192.3 jit_solution(7345366036997208114)
XLA Ops:
  0.6 0.8 broadcast_in_dim.60
  1.5 16.7 %all_to_all.45 = bf16[16,2,1280]{2,1,0:T(2,128)(2,1)S(1)} all-to-all(bf16[16,2,1280]{2,1,0:T(2,128)(2,1)S(1)} %broadcast_in_dim.60), channel_id=1, replica_groups=mesh['dp'=32,'expert'=16] {'expert'}, dimensions={0} | all-to-all | bytes 163840 | tf_op jit(solution)/shard_map/all_to_all | solution.py:40
  18.2 0.9 copy-done.1
  19.1 0.9 copy-done.3
  20.1 0.8 shard_map.84
  20.9 16.5 %all_to_all.46 = bf16[16,8,2688]{2,1,0:T(8,128)(2,1)S(1)} all-to-all(bf16[16,8,2688]{2,1,0:T(8,128)(2,1)S(1)} %bitcast.155), channel_id=1, replica_groups=mesh['dp'=32,'expert'=16] {'expert'}, dimensions={0} | all-to-all | bytes 1376256 | tf_op jit(solution)/shard_map/all_to_all | solution.py:40
  38.5 34.4 %all_to_all.47 = bf16[8,16,1280]{2,1,0:T(8,128)(2,1)S(1)} all-to-all(bf16[8,16,1280]{2,1,0:T(8,128)(2,1)S(1)} %broadcast_in_dim.61), channel_id=1, replica_groups={{0,32,64,96,128,160,192,224},{16,48,80,112,144,176,208,240},{256,288,32..., dimensions={0} | all-to-all | bytes 655360 | tf_op jit(solution)/shard_map/all_to_all | solution.py:40
  73.0 1.1 broadcast_in_dim.63
  74.1 3.5 %all-to-all-start.3 = ((bf16[4,128,1280]{2,1,0:T(8,128)(2,1)}), bf16[4,128,1280]{2,1,0:T(8,128)(2,1)S(1)}, u32[]{:S(2)}, u32[]{:S(2)}) async-start(bf16[4,128,1280]{2,1,0:T(8,128)(2,1)} %broadcast_in_dim.63), calls=%async_computation.3 | async-start | bytes 2621440 | tf_op jit(solution)/shard_map/all_to_all | solution.py:40
  77.7 15.5 %all-to-all-done.3 = bf16[4,128,1280]{2,1,0:T(8,128)(2,1)S(1)} async-done(((bf16[4,128,1280]{2,1,0:T(8,128)(2,1)}), bf16[4,128,1280]{2,1,0:T(8,128)(2,1)S(1)}, u32[]{:S(2)}, u32[]{:S(2)}) %all-to-all-start.3) | async-done | bytes 1310752 | tf_op jit(solution)/shard_map/all_to_all | solution.py:40
  93.7 0.7 fusion.6
  94.6 1.1 fusion.13
  96.9 16.9 %all_to_all.48 = bf16[4,128,1280]{2,1,0:T(8,128)(2,1)S(1)} all-to-all(bf16[4,128,1280]{2,1,0:T(8,128)(2,1)S(1)} %bitcast.163), channel_id=1, replica_groups={{0,16,256,272},{32,48,288,304},{64,80,320,336},{96,112,352,368},{128,14..., dimensions={0} | all-to-all | bytes 2621440 | tf_op jit(solution)/shard_map/all_to_all | solution.py:40
  113.8 1.0 reduce_sum.91
  114.8 6.7 %all-to-all-start.5 = ((bf16[8,16,1280]{2,1,0:T(8,128)(2,1)}), bf16[8,16,1280]{2,1,0:T(8,128)(2,1)S(1)}, u32[]{:S(2)}, u32[]{:S(2)}) async-start(bf16[8,16,1280]{2,1,0:T(8,128)(2,1)} %bitcast.21), calls=%async_computation.5 | async-start | bytes 655360 | tf_op jit(solution)/shard_map/all_to_all | solution.py:40
  122.1 19.2 %all-to-all-done.5 = bf16[8,16,1280]{2,1,0:T(8,128)(2,1)S(1)} async-done(((bf16[8,16,1280]{2,1,0:T(8,128)(2,1)}), bf16[8,16,1280]{2,1,0:T(8,128)(2,1)S(1)}, u32[]{:S(2)}, u32[]{:S(2)}) %all-to-all-start.5) | async-done | bytes 327712 | tf_op jit(solution)/shard_map/all_to_all | solution.py:40
  142.0 21.1 %all_to_all.49 = bf16[16,8,2688]{2,1,0:T(8,128)(2,1)S(1)} all-to-all(bf16[16,8,2688]{2,1,0:T(8,128)(2,1)S(1)} %broadcast_in_dim.65), channel_id=1, replica_groups=mesh['dp'=32,'expert'=16] {'expert'}, dimensions={0} | all-to-all | bytes 1376256 | tf_op jit(solution)/shard_map/all_to_all | solution.py:40
  163.1 1.4 shard_map.85
  164.7 10.9 %all_to_all.50 = bf16[32,2,1280]{2,1,0:T(2,128)(2,1)S(1)} all-to-all(bf16[32,2,1280]{2,1,0:T(2,128)(2,1)S(1)} %bitcast.171), channel_id=1, replica_groups={{0,1,2,3,4,5,6,7,8,9,10,11,12,13,14,15,256,257,258,259,260,261,262,263,..., dimensions={0} | all-to-all | bytes 327680 | tf_op jit(solution)/shard_map/all_to_all | solution.py:40
  175.8 0.7 broadcast_in_dim.68
  176.5 3.5 %all-to-all-start.8 = ((bf16[16,2,1280]{2,1,0:T(2,128)(2,1)}), bf16[16,2,1280]{2,1,0:T(2,128)(2,1)S(1)}, u32[]{:S(2)}, u32[]{:S(2)}) async-start(bf16[16,2,1280]{2,1,0:T(2,128)(2,1)} %broadcast_in_dim.68), calls=%async_computation.8 | async-start | bytes 163840 | tf_op jit(solution)/shard_map/all_to_all | solution.py:40
  180.0 1.3 convolution_convert_fusion
  181.3 1.3 fusion.2
  182.5 9.1 %all-to-all-done.8 = bf16[16,2,1280]{2,1,0:T(2,128)(2,1)S(1)} async-done(((bf16[16,2,1280]{2,1,0:T(2,128)(2,1)}), bf16[16,2,1280]{2,1,0:T(2,128)(2,1)S(1)}, u32[]{:S(2)}, u32[]{:S(2)}) %all-to-all-start.8) | async-done | bytes 81952 | tf_op jit(solution)/shard_map/all_to_all | solution.py:40
  (58 shorter events, 5.2 us)
Async XLA Ops:
  0.6 92.6 %copy-start = (bf16[2,1280,160]{1,2,0:T(8,128)(2,1)S(1)}, bf16[2,1280,160]{1,2,0:T(8,128)(2,1)}, u32[]{:S(2)}) copy-start(bf16[2,1280,160]{1,2,0:T(8,128)(2,1)} %param.8) | copy-start | bytes 2457604
  18.2 0.9 copy-start.1
  19.1 0.9 copy-start.3
  74.1 19.1 %all-to-all-start.3 = ((bf16[4,128,1280]{2,1,0:T(8,128)(2,1)}), bf16[4,128,1280]{2,1,0:T(8,128)(2,1)S(1)}, u32[]{:S(2)}, u32[]{:S(2)}) async-start(bf16[4,128,1280]{2,1,0:T(8,128)(2,1)} %broadcast_in_dim.63), calls=%async_computation.3 | async-start | bytes 2621440 | tf_op jit(solution)/shard_map/all_to_all | solution.py:40
  93.2 2.5 %copy-start.5 = (bf16[4,8,8,1280]{3,2,1,0:T(8,128)(2,1)}, bf16[4,8,8,1280]{3,2,1,0:T(8,128)(2,1)S(1)}, u32[]{:S(2)}) copy-start(bf16[4,8,8,1280]{3,2,1,0:T(8,128)(2,1)S(1)} %get-tuple-element.17) | copy-start | bytes 1966084
  93.3 1.4 copy-start.7
  114.8 26.5 %all-to-all-start.5 = ((bf16[8,16,1280]{2,1,0:T(8,128)(2,1)}), bf16[8,16,1280]{2,1,0:T(8,128)(2,1)S(1)}, u32[]{:S(2)}, u32[]{:S(2)}) async-start(bf16[8,16,1280]{2,1,0:T(8,128)(2,1)} %bitcast.21), calls=%async_computation.5 | async-start | bytes 655360 | tf_op jit(solution)/shard_map/all_to_all | solution.py:40
  122.1 41.0 %copy-start.2 = (bf16[4,16,1280]{2,1,0:T(8,128)(2,1)S(1)}, bf16[4,16,1280]{2,1,0:T(8,128)(2,1)}, u32[]{:S(2)}) copy-start(bf16[4,16,1280]{2,1,0:T(8,128)(2,1)} %param.5) | copy-start | bytes 491524
  122.1 41.0 %copy-start.4 = (bf16[4,16,1280]{2,1,0:T(8,128)(2,1)S(1)}, bf16[4,16,1280]{2,1,0:T(8,128)(2,1)}, u32[]{:S(2)}) copy-start(bf16[4,16,1280]{2,1,0:T(8,128)(2,1)} %param.6) | copy-start | bytes 491524
  163.1 16.8 %copy-start.6 = (bf16[4,8,8,1280]{3,2,1,0:T(8,128)(2,1)S(1)}, bf16[4,8,8,1280]{3,2,1,0:T(8,128)(2,1)}, u32[]{:S(2)}) copy-start(bf16[4,8,8,1280]{3,2,1,0:T(8,128)(2,1)} %copy-done.5) | copy-start | bytes 1966084
  176.5 15.2 %all-to-all-start.8 = ((bf16[16,2,1280]{2,1,0:T(2,128)(2,1)}), bf16[16,2,1280]{2,1,0:T(2,128)(2,1)S(1)}, u32[]{:S(2)}, u32[]{:S(2)}) async-start(bf16[16,2,1280]{2,1,0:T(2,128)(2,1)} %broadcast_in_dim.68), calls=%async_computation.8 | async-start | bytes 163840 | tf_op jit(solution)/shard_map/all_to_all | solution.py:40

commit v6 on v5

--- a/solution.py
+++ b/solution.py
@@ -5,7 +5,6 @@
 import numpy as np
 from jax import lax
 from jax.experimental import pallas as pl
-from jax.experimental.pallas import tpu as pltpu
 from jax.sharding import PartitionSpec as P
 
 F32 = jnp.float32
@@ -57,14 +56,21 @@
     return ids.transpose(1, 0, 2).reshape(depth, 2 * peers).tolist()
 
 
-def gather_dp(own):
-    far = everywhere(own, "dp", dp_groups(1))
-    return everywhere(far.reshape(-1, own.shape[1]), "dp", dp_groups(0, 2))
-
-
-def reduce_dp(partial, rows):
+def across_y(value):
+    depth = lax.axis_size("dp") // 2
+    pairs = [(y * depth + z, (1 - y) * depth + z) for y in range(2) for z in range(depth)]
+    return lax.ppermute(value, "dp", pairs)
+
+
+def gather_z(own, beside):
+    far = everywhere(own, "dp", dp_groups(1)).reshape(-1, own.shape[1])
+    far, beside = lax.optimization_barrier((far, beside))
+    return everywhere(far, "dp", dp_groups(2)), beside
+
+
+def reduce_z(partial, rows):
     d = partial.shape[-1]
-    total = jnp.sum(exchange(partial, "dp", dp_groups(0, 2)).astype(F32), axis=0).astype(BF16)
+    total = jnp.sum(exchange(partial, "dp", dp_groups(2)).astype(F32), axis=0).astype(BF16)
     return jnp.sum(exchange(total.reshape(-1, rows, d), "dp", dp_groups(1)).astype(F32), axis=0)
 
 
@@ -155,37 +161,55 @@
     return pl.pallas_call(
         kernel,
         out_shape=shapes,
-        compiler_params=pltpu.CompilerParams(vmem_limit_bytes=32 * 1024 * 1024),
         cost_estimate=pl.CostEstimate(flops=120_000_000, bytes_accessed=2_000_000, transcendentals=16384),
     )(*operands)
 
 
-def expert_part(gathered, w_in, w_out, imgs):
-    slots, d, _ = w_in.shape
-    rows = slots * imgs
-    blocks = (gathered.shape[0], gathered.shape[1] // (2 * rows), rows, d)
-    halves = gathered.reshape(blocks[:2] + (2 * rows, d))
-    all_in = halves[:, :, :rows].reshape(-1, d)
-    all_out_grad = halves[:, :, rows:].reshape(-1, d)
-    row = lax.broadcasted_iota(jnp.int32, (slots, all_in.shape[0], 1), 1)
-    slot = lax.broadcasted_iota(jnp.int32, (slots, all_in.shape[0], 1), 0)
-    mine = row % slots == slot
-    preact = jnp.einsum("rd,sdh->srh", all_in, w_in, preferred_element_type=F32)
-    activated_wide, pullback = jax.vjp(gelu_exact, preact)
-    activated = jnp.where(mine, activated_wide, 0.0).astype(BF16)
-    slot_out = jnp.einsum("srh,shd->rd", activated, w_out, preferred_element_type=F32)
+def halves_of(gathered, rows):
+    d = gathered.shape[-1]
+    blocks = gathered.reshape(-1, 2 * rows, d)
+    return blocks[:, :rows].reshape(-1, d), blocks[:, rows:].reshape(-1, d)
+
+
+def own_slot(rows, slots):
+    row = lax.broadcasted_iota(jnp.int32, (slots, rows, 1), 1)
+    slot = lax.broadcasted_iota(jnp.int32, (slots, rows, 1), 0)
+    return row % slots == slot
+
+
+def hidden_forward(all_in, w_in, mine):
+    preact = jnp.einsum("rd,shd->srh", all_in, w_in, preferred_element_type=F32)
+    return preact, jnp.where(mine, gelu_exact(preact), 0.0).astype(BF16)
+
+
+def hidden_backward(all_out_grad, preact, w_out, mine):
+    _, pullback = jax.vjp(gelu_exact, preact)
     act_grad = jnp.einsum("rd,shd->srh", all_out_grad, w_out, preferred_element_type=F32)
-    preact_grad = jnp.where(mine, pullback(act_grad)[0], 0.0).astype(BF16)
-    slot_in_grad = jnp.einsum("srh,sdh->rd", preact_grad, w_in, preferred_element_type=F32)
-    w_out_grad = jnp.einsum(
-        "srh,rd->shd", activated, all_out_grad, preferred_element_type=F32
-    ).astype(BF16)
-    w_in_grad = jnp.einsum(
-        "rd,srh->sdh", all_in, preact_grad, preferred_element_type=F32
-    ).astype(BF16)
+    return jnp.where(mine, pullback(act_grad)[0], 0.0).astype(BF16)
+
+
+def expert_part(gathered, weights, rows):
+    all_in, all_out_grad = halves_of(gathered, rows)
+    mine = own_slot(all_in.shape[0], weights[0].shape[1])
+    slot_out, slot_in_grad = 0.0, 0.0
+    for w_in, w_out in weights:
+        preact, activated = hidden_forward(all_in, w_in, mine)
+        preact_grad = hidden_backward(all_out_grad, preact, w_out, mine)
+        slot_out += jnp.einsum("srh,shd->rd", activated, w_out, preferred_element_type=F32)
+        slot_in_grad += jnp.einsum("srh,shd->rd", preact_grad, w_in, preferred_element_type=F32)
+    blocks = (gathered.shape[0], -1, rows, gathered.shape[2])
     pair = [value.astype(BF16).reshape(blocks) for value in (slot_out, slot_in_grad)]
-    partial = jnp.concatenate(pair, axis=2).reshape(gathered.shape)
-    return partial, w_in_grad, w_out_grad
+    return jnp.concatenate(pair, axis=2).reshape(gathered.shape)
+
+
+def weight_grads(gathered, w_in, w_out, rows):
+    all_in, all_out_grad = halves_of(gathered, rows)
+    mine = own_slot(all_in.shape[0], w_in.shape[0])
+    preact, activated = hidden_forward(all_in, w_in, mine)
+    preact_grad = hidden_backward(all_out_grad, preact, w_out, mine)
+    w_out_grad = jnp.einsum("srh,rd->shd", activated, all_out_grad, preferred_element_type=F32)
+    w_in_grad = jnp.einsum("rd,srh->sdh", all_in, preact_grad, preferred_element_type=F32)
+    return w_in_grad.astype(BF16), w_out_grad.astype(BF16)
 
 
 def on_device(tokens, cotangent, slot_params, w_in, w_out):
@@ -204,6 +228,9 @@
         params, flat_tok, flat_cot,
     )
     taken = exchange(sent.reshape(peers, rows, 2 * d + 128), "expert")
+    weights = jnp.stack([jnp.swapaxes(w_in, 1, 2), w_out])
+    weights, taken = lax.optimization_barrier((weights, taken))
+    weights_y = across_y(weights)
 
     peaks = join3(taken[:, :, d : d + 3])
     masses = join3(taken[:, :, d + 3 : d + 6])
@@ -214,9 +241,13 @@
     slot_out_grad = jnp.sum(taken[:, :, d + 128 :].astype(F32), axis=0)
     own = jnp.concatenate([slot_in_wide.astype(BF16), slot_out_grad.astype(BF16)], axis=0)
 
-    gathered = gather_dp(own)
-    partial, w_in_grad, w_out_grad = expert_part(gathered, w_in, w_out, imgs)
-    owned_b = reduce_dp(partial, 2 * rows).astype(BF16).reshape(2, rows, d)
+    gathered, weights_y = gather_z(own, weights_y)
+    partial = expert_part(gathered, (weights, weights_y), rows)
+    gathered, partial = lax.optimization_barrier((gathered, partial))
+    gathered_y = across_y(gathered)
+    owned_b = reduce_z(partial, 2 * rows).astype(BF16)
+    owned_b, gathered_y = lax.optimization_barrier((owned_b, gathered_y))
+    owned_b = owned_b.reshape(2, rows, d)
 
     col = jnp.sum(owned_b[1].astype(F32) * slot_in_wide, axis=1, keepdims=True)
     stats = jnp.concatenate(
@@ -230,6 +261,9 @@
     )
     token_grad = token_grad.reshape(tokens.shape)
 
+    share_grad, gathered, gathered_y = lax.optimization_barrier((share_grad, gathered, gathered_y))
+    both = jnp.concatenate([gathered, gathered_y], axis=0)
+    w_in_grad, w_out_grad = weight_grads(both, weights[0], weights[1], rows)
     share_grad = jnp.broadcast_to(share_grad.reshape(1, peers, own_slots, d), (2, peers, own_slots, d))
     share_grad = exchange(
         share_grad.reshape(2 * peers, own_slots, d), ("dp", "expert"), plane_groups()

time: 193 us -> 215 us (1.11)
  blocking collectives: 117 us -> 56.7 us
  starting transfers between devices: 13.8 us -> 53 us
  waiting for transfers between devices: 43.8 us -> 60.5 us
  matrix products: 5.12 us -> 17.4 us
  local copies, waits for them, and re-layouts: 6.4 us -> 14 us
  Pallas kernels: 2.26 us -> 5.41 us
  other arithmetic: 3.48 us -> 6.06 us
    all_to_all x6 -> x3, blocking collectives: 117 us -> 56.7 us  [exchange(): lax.all_to_all(value, axis, split_axis=0, concat_axis=0, axis_index_group...]
    all_to_all x3 -> x6, starting transfers between devices: 13.8 us -> 48.8 us  [exchange(): lax.all_to_all(value, axis, split_axis=0, concat_axis=0, axis_index_group...]
    all_to_all x3 -> x6, waiting for transfers between devices: 43.8 us -> 56.3 us  [exchange(): lax.all_to_all(value, axis, split_axis=0, concat_axis=0, axis_index_group...]
    dot_general x4 -> x7, matrix products: 4.19 us -> 14 us  [the longest x2 4.79 us: expert_part(): jnp.einsum('srh,shd->rd', preact_grad, w_in, preferred_element_type=F32)]
    optimization_barrier x0 -> x1, local copies, waits for them, and re-layouts: none -> 5.27 us  [on_device(): weights, taken = lax.optimization_barrier((weights, taken))]
    ppermute x0 -> x2, starting transfers between devices: none -> 4.22 us  [across_y(): return lax.ppermute(value, 'dp', pairs)]
    ppermute x0 -> x2, waiting for transfers between devices: none -> 4.16 us  [across_y(): return lax.ppermute(value, 'dp', pairs)]
    pallas_call x2, Pallas kernels: 2.26 us -> 5.41 us  [call(): pl.pallas_call(kernel, out_shape=shapes, cost_estimate=pl.CostEstimate(fl...]
  transfers between devices with their start and end apart: 3 -> 8, of which waited for: 3 -> 7; matrix products, arithmetic and copies ran while one was open for 2% -> 4% of each run, Pallas kernels for 0% -> 0%
where the time goes in v6:
time: 215 us; the launch traced here: 214 us
  waiting for transfers between devices  60.5 us (28%)
  blocking collectives  56.7 us (26%)
  starting transfers between devices  53 us (25%)
  matrix products  17.4 us (8%)
  local copies, waits for them, and re-layouts  14 us (7%)
  other arithmetic  6.06 us (3%)
  Pallas kernels  5.41 us (3%)
    all_to_all x3, blocking collectives, exchange(): lax.all_to_all(value, axis, split_axis=0, concat_axis=0, axis_index_group...  56.7 us
    all_to_all x6, waiting for transfers between devices, exchange(): lax.all_to_all(value, axis, split_axis=0, concat_axis=0, axis_index_group...  56.3 us
    all_to_all x6, starting transfers between devices, exchange(): lax.all_to_all(value, axis, split_axis=0, concat_axis=0, axis_index_group...  48.8 us
    pallas_call x2, Pallas kernels, call(): pl.pallas_call(kernel, out_shape=shapes, cost_estimate=pl.CostEstimate(fl...  5.41 us
    optimization_barrier x1, local copies, waits for them, and re-layouts, on_device(): weights, taken = lax.optimization_barrier((weights, taken))  5.27 us
    dot_general x2, matrix products, expert_part(): jnp.einsum('srh,shd->rd', preact_grad, w_in, preferred_element_type=F32)  4.79 us
  transfers between devices with their start and end apart: 8, of which 7 were waited for; matrix products, arithmetic and copies ran while one was open for 4% of the time, Pallas kernels for 0%

profile of v6, /device:TPU:1, one launch (start us, length us, event | category | flops | bytes accessed | tf_op | source)
XLA Modules:
  0.0 214.1 jit_solution(8470562337978125360)
XLA Ops:
  1.4 16.7 %all_to_all.45 = bf16[16,2,1280]{2,1,0:T(2,128)(2,1)S(1)} all-to-all(bf16[16,2,1280]{2,1,0:T(2,128)(2,1)S(1)} %broadcast_in_dim.86), channel_id=1, replica_groups=mesh['dp'=32,'expert'=16] {'expert'}, dimensions={0} | all-to-all | bytes 163840 | tf_op jit(solution)/shard_map/all_to_all | solution.py:39
  18.8 2.7 %shard_map.84 = (bf16[128,2688]{1,0:T(8,128)(2,1)}, f32[128,64]{1,0:T(8,128)}, f32[128,64]{1,0:T(8,128)}) custom-call(bf16[32,1280]{1,0:T(8,128)(2,1)} %reshape.277.params_ref, bf16[64,1280]{1,0:T(8,128)(2,1)} %bitcast.423, bf16[64,1280]{1,0:T(8,128)(2,1)} %bitcast.425), custom_call_target="tpu_custom_call" | custom-call | flops 120000000 | bytes 2000000 | tf_op jit(solution)/shard_map/pallas_call | solution.py:161
  21.5 3.8 %all-to-all-start.1 = ((bf16[16,8,2688]{2,1,0:T(8,128)(2,1)}), bf16[16,8,2688]{2,1,0:T(8,128)(2,1)S(1)}, u32[]{:S(2)}, u32[]{:S(2)}) async-start(bf16[16,8,2688]{2,1,0:T(8,128)(2,1)} %bitcast.420), calls=%async_computation.1 | async-start | bytes 1376256 | tf_op jit(solution)/shard_map/all_to_all | solution.py:39
  26.9 11.3 %all-to-all-done.1 = bf16[16,8,2688]{2,1,0:T(8,128)(2,1)S(1)} async-done(((bf16[16,8,2688]{2,1,0:T(8,128)(2,1)}), bf16[16,8,2688]{2,1,0:T(8,128)(2,1)S(1)}, u32[]{:S(2)}, u32[]{:S(2)}) %all-to-all-start.1) | async-done | bytes 688160 | tf_op jit(solution)/shard_map/all_to_all | solution.py:39
  38.2 5.3 %copy.81 = bf16[16,8,2688]{0,1,2:T(8,128)(2,1)} copy(bf16[16,8,2688]{2,1,0:T(8,128)(2,1)S(1)} %all-to-all-done.1) | data formatting | bytes 1376256 | tf_op jit(solution)/shard_map/optimization_barrier | solution.py:232
  46.8 31.5 %all_to_all.46 = bf16[8,16,1280]{2,1,0:T(8,128)(2,1)S(1)} all-to-all(bf16[8,16,1280]{2,1,0:T(8,128)(2,1)S(1)} %broadcast_in_dim.87), channel_id=1, replica_groups={{0,32,64,96,128,160,192,224},{16,48,80,112,144,176,208,240},{256,288,32..., dimensions={0} | all-to-all | bytes 655360 | tf_op jit(solution)/shard_map/all_to_all | solution.py:39
  78.3 4.2 %collective-permute-done = bf16[2,2,160,1280]{3,2,1,0:T(8,128)(2,1)S(1)} collective-permute-done((bf16[2,2,160,1280]{3,2,1,0:T(8,128)(2,1)S(1)}, bf16[2,2,160,1280]{3,2,1,0:T(8,128)(2,1)S(1)}, u32[]{:S(2)}, u32[]{:S(2)}) %collective-permute-start) | collective-permute-done | bytes 1638432 | tf_op jit(solution)/shard_map/ppermute | solution.py:62
  84.5 3.5 %all-to-all-start.3 = ((bf16[2,128,1280]{2,1,0:T(8,128)(2,1)}), bf16[2,128,1280]{2,1,0:T(8,128)(2,1)S(1)}, u32[]{:S(2)}, u32[]{:S(2)}) async-start(bf16[2,128,1280]{2,1,0:T(8,128)(2,1)} %broadcast_in_dim.88), calls=%async_computation.3 | async-start | bytes 1310720 | tf_op jit(solution)/shard_map/all_to_all | solution.py:39
  88.0 6.1 %all-to-all-done.3 = bf16[2,128,1280]{2,1,0:T(8,128)(2,1)S(1)} async-done(((bf16[2,128,1280]{2,1,0:T(8,128)(2,1)}), bf16[2,128,1280]{2,1,0:T(8,128)(2,1)S(1)}, u32[]{:S(2)}, u32[]{:S(2)}) %all-to-all-start.3) | async-done | bytes 655392 | tf_op jit(solution)/shard_map/all_to_all | solution.py:39
  96.0 2.0 convolution_bitcast_fusion.1
  101.5 2.8 %fusion.4 = bf16[128,1280]{1,0:T(8,128)(2,1)S(1)} fusion(f32[128,1280]{1,0:T(8,128)} %convolution_bitcast_fusion.1, bf16[2,2,160,1280]{3,2,1,0:T(8,128)(2,1)} %copy-done.4, bf16[16,16,1280]{2,1,0:T(8,128)(2,1)S(1)} %bitcast.412, f32[2,160,128]{2,1,0:T(8,128)S(1)} %fusion.8, pred[2,128]{1,0:T(4,128)(4,1)S(1)} %iota_compare_fusion.1), kind=kOutput, calls=%fused_computation.10 | convolution fusion | flops 213032960 | bytes 3113472 | tf_op jit(solution)/shard_map/srh,shd->rd/dot_general | solution.py:199
  104.3 8.6 %all_to_all.47 = bf16[2,128,1280]{2,1,0:T(8,128)(2,1)S(1)} all-to-all(bf16[2,128,1280]{2,1,0:T(8,128)(2,1)S(1)} %bitcast.413), channel_id=1, replica_groups={{0,16},{32,48},{64,80},{96,112},{128,144},{160,176},{192,208},{224,240}..., dimensions={0} | all-to-all | bytes 1310720 | tf_op jit(solution)/shard_map/all_to_all | solution.py:39
  113.8 14.5 %all-to-all-start.5 = ((bf16[8,16,1280]{2,1,0:T(8,128)(2,1)}), bf16[8,16,1280]{2,1,0:T(8,128)(2,1)S(1)}, u32[]{:S(2)}, u32[]{:S(2)}) async-start(bf16[8,16,1280]{2,1,0:T(8,128)(2,1)} %bitcast.33), calls=%async_computation.5 | async-start | bytes 655360 | tf_op jit(solution)/shard_map/all_to_all | solution.py:39
  128.3 2.3 %collective-permute-start.1 = (bf16[2,128,1280]{2,1,0:T(8,128)(2,1)S(1)}, bf16[2,128,1280]{2,1,0:T(8,128)(2,1)S(1)}, u32[]{:S(2)}, u32[]{:S(2)}) collective-permute-start(bf16[2,128,1280]{2,1,0:T(8,128)(2,1)S(1)} %all-to-all-done.3), channel_id=1, source_target_pairs={{0,256},{16,272},{32,288},{48,304},{64,320},{80,336},{96,352},{112... | collective-permute-start | bytes 1966088 | tf_op jit(solution)/shard_map/ppermute | solution.py:62
  131.2 13.5 %all-to-all-done.5 = bf16[8,16,1280]{2,1,0:T(8,128)(2,1)S(1)} async-done(((bf16[8,16,1280]{2,1,0:T(8,128)(2,1)}), bf16[8,16,1280]{2,1,0:T(8,128)(2,1)S(1)}, u32[]{:S(2)}, u32[]{:S(2)}) %all-to-all-start.5) | async-done | bytes 327712 | tf_op jit(solution)/shard_map/all_to_all | solution.py:39
  146.3 15.9 %all-to-all-start.6 = ((bf16[16,8,2688]{2,1,0:T(8,128)(2,1)}), bf16[16,8,2688]{2,1,0:T(8,128)(2,1)S(1)}, u32[]{:S(2)}, u32[]{:S(2)}) async-start(bf16[16,8,2688]{2,1,0:T(8,128)(2,1)} %broadcast_in_dim.91), calls=%async_computation.6 | async-start | bytes 1376256 | tf_op jit(solution)/shard_map/all_to_all | solution.py:39
  162.2 12.7 %all-to-all-done.6 = bf16[16,8,2688]{2,1,0:T(8,128)(2,1)S(1)} async-done(((bf16[16,8,2688]{2,1,0:T(8,128)(2,1)}), bf16[16,8,2688]{2,1,0:T(8,128)(2,1)S(1)}, u32[]{:S(2)}, u32[]{:S(2)}) %all-to-all-start.6) | async-done | bytes 688160 | tf_op jit(solution)/shard_map/all_to_all | solution.py:39
  175.8 2.7 %shard_map.85 = (bf16[64,1280]{1,0:T(8,128)(2,1)}, bf16[32,1280]{1,0:T(8,128)(2,1)}) custom-call(bf16[128,2688]{1,0:T(8,128)(2,1)} %bitcast.408, f32[128,64]{1,0:T(8,128)} %get-tuple-element.28.logits_ref, f32[128,64]{1,0:T(8,128)} %get-tuple-element.29.combine_ref, bf16[32,1280]{1,0:T(8,128)(2,1)} %reshape.277.params_ref, bf16[64,1280]{1,0:T(8,128)(2,1)} %bitcast.424, ...), custom_call_target="tpu_custom_call" | custom-call | flops 120000000 | bytes 2000000 | tf_op jit(solution)/shard_map/pallas_call | solution.py:161
  181.9 5.0 %all-to-all-start.7 = ((bf16[32,2,1280]{2,1,0:T(2,128)(2,1)}), bf16[32,2,1280]{2,1,0:T(2,128)(2,1)S(1)}, u32[]{:S(2)}, u32[]{:S(2)}) async-start(bf16[32,2,1280]{2,1,0:T(2,128)(2,1)} %bitcast.39), calls=%async_computation.7 | async-start | bytes 327680 | tf_op jit(solution)/shard_map/all_to_all | solution.py:39
  187.0 3.9 %fusion = bf16[2,1280,160]{1,2,0:T(8,128)(2,1)} fusion(bf16[32,16,1280]{2,1,0:T(8,128)(2,1)} %bitcast.415, bf16[2,2,160,1280]{3,2,1,0:T(8,128)(2,1)S(1)} %pad_maximum_fusion, f32[2,160,256]{2,1,0:T(8,128)S(1)} %fusion.13, pred[2,256]{1,0:T(4,128)(4,1)S(1)} %iota_compare_fusion), kind=kOutput, calls=%fused_computation.2 | convolution fusion | flops 425820160 | bytes 3277824 | tf_op jit(solution)/shard_map/rd,srh->sdh/dot_general | solution.py:211
  190.8 4.0 %all-to-all-done.7 = bf16[32,2,1280]{2,1,0:T(2,128)(2,1)S(1)} async-done(((bf16[32,2,1280]{2,1,0:T(2,128)(2,1)}), bf16[32,2,1280]{2,1,0:T(2,128)(2,1)S(1)}, u32[]{:S(2)}, u32[]{:S(2)}) %all-to-all-start.7) | async-done | bytes 163872 | tf_op jit(solution)/shard_map/all_to_all | solution.py:39
  195.7 6.0 %all-to-all-start.8 = ((bf16[16,2,1280]{2,1,0:T(2,128)(2,1)}), bf16[16,2,1280]{2,1,0:T(2,128)(2,1)S(1)}, u32[]{:S(2)}, u32[]{:S(2)}) async-start(bf16[16,2,1280]{2,1,0:T(2,128)(2,1)} %broadcast_in_dim.94), calls=%async_computation.8 | async-start | bytes 163840 | tf_op jit(solution)/shard_map/all_to_all | solution.py:39
  201.7 3.0 %convolution_convert_fusion = bf16[2,160,1280]{2,1,0:T(8,128)(2,1)} fusion(bf16[32,16,1280]{2,1,0:T(8,128)(2,1)} %bitcast.416, f32[2,160,256]{2,1,0:T(8,128)S(1)} %fusion.13, pred[2,256]{1,0:T(4,128)(4,1)S(1)} %iota_compare_fusion), kind=kOutput, calls=%fused_computation | convolution fusion | flops 215531520 | bytes 1802752 | tf_op jit(solution)/shard_map/srh,rd->shd/dot_general | solution.py:210
  204.7 8.8 %all-to-all-done.8 = bf16[16,2,1280]{2,1,0:T(2,128)(2,1)S(1)} async-done(((bf16[16,2,1280]{2,1,0:T(2,128)(2,1)}), bf16[16,2,1280]{2,1,0:T(2,128)(2,1)S(1)}, u32[]{:S(2)}, u32[]{:S(2)}) %all-to-all-start.8) | async-done | bytes 81952 | tf_op jit(solution)/shard_map/all_to_all | solution.py:39
  (62 shorter events, 22.5 us)
Async XLA Ops:
  21.5 16.7 %all-to-all-start.1 = ((bf16[16,8,2688]{2,1,0:T(8,128)(2,1)}), bf16[16,8,2688]{2,1,0:T(8,128)(2,1)S(1)}, u32[]{:S(2)}, u32[]{:S(2)}) async-start(bf16[16,8,2688]{2,1,0:T(8,128)(2,1)} %bitcast.420), calls=%async_computation.1 | async-start | bytes 1376256 | tf_op jit(solution)/shard_map/all_to_all | solution.py:39
  44.7 37.7 %collective-permute-start = (bf16[2,2,160,1280]{3,2,1,0:T(8,128)(2,1)S(1)}, bf16[2,2,160,1280]{3,2,1,0:T(8,128)(2,1)S(1)}, u32[]{:S(2)}, u32[]{:S(2)}) collective-permute-start(bf16[2,2,160,1280]{3,2,1,0:T(8,128)(2,1)S(1)} %pad_maximum_fusion), channel_id=1, source_target_pairs={{0,256},{16,272},{32,288},{48,304},{64,320},{80,336},{96,352},{112... | collective-permute-start | bytes 4915208 | tf_op jit(solution)/shard_map/ppermute | solution.py:62
  82.4 1.2 copy-start.4
  84.5 9.6 %all-to-all-start.3 = ((bf16[2,128,1280]{2,1,0:T(8,128)(2,1)}), bf16[2,128,1280]{2,1,0:T(8,128)(2,1)S(1)}, u32[]{:S(2)}, u32[]{:S(2)}) async-start(bf16[2,128,1280]{2,1,0:T(8,128)(2,1)} %broadcast_in_dim.88), calls=%async_computation.3 | async-start | bytes 1310720 | tf_op jit(solution)/shard_map/all_to_all | solution.py:39
  113.8 30.9 %all-to-all-start.5 = ((bf16[8,16,1280]{2,1,0:T(8,128)(2,1)}), bf16[8,16,1280]{2,1,0:T(8,128)(2,1)S(1)}, u32[]{:S(2)}, u32[]{:S(2)}) async-start(bf16[8,16,1280]{2,1,0:T(8,128)(2,1)} %bitcast.33), calls=%async_computation.5 | async-start | bytes 655360 | tf_op jit(solution)/shard_map/all_to_all | solution.py:39
  128.3 16.4 %collective-permute-start.1 = (bf16[2,128,1280]{2,1,0:T(8,128)(2,1)S(1)}, bf16[2,128,1280]{2,1,0:T(8,128)(2,1)S(1)}, u32[]{:S(2)}, u32[]{:S(2)}) collective-permute-start(bf16[2,128,1280]{2,1,0:T(8,128)(2,1)S(1)} %all-to-all-done.3), channel_id=1, source_target_pairs={{0,256},{16,272},{32,288},{48,304},{64,320},{80,336},{96,352},{112... | collective-permute-start | bytes 1966088 | tf_op jit(solution)/shard_map/ppermute | solution.py:62
  144.7 1.5 copy-start.2
  146.3 28.7 %all-to-all-start.6 = ((bf16[16,8,2688]{2,1,0:T(8,128)(2,1)}), bf16[16,8,2688]{2,1,0:T(8,128)(2,1)S(1)}, u32[]{:S(2)}, u32[]{:S(2)}) async-start(bf16[16,8,2688]{2,1,0:T(8,128)(2,1)} %broadcast_in_dim.91), calls=%async_computation.6 | async-start | bytes 1376256 | tf_op jit(solution)/shard_map/all_to_all | solution.py:39
  174.9 0.8 copy-start
  179.7 1.1 copy-start.1
  179.7 1.5 copy-start.3
  181.9 12.9 %all-to-all-start.7 = ((bf16[32,2,1280]{2,1,0:T(2,128)(2,1)}), bf16[32,2,1280]{2,1,0:T(2,128)(2,1)S(1)}, u32[]{:S(2)}, u32[]{:S(2)}) async-start(bf16[32,2,1280]{2,1,0:T(2,128)(2,1)} %bitcast.39), calls=%async_computation.7 | async-start | bytes 327680 | tf_op jit(solution)/shard_map/all_to_all | solution.py:39
  195.7 17.8 %all-to-all-start.8 = ((bf16[16,2,1280]{2,1,0:T(2,128)(2,1)}), bf16[16,2,1280]{2,1,0:T(2,128)(2,1)S(1)}, u32[]{:S(2)}, u32[]{:S(2)}) async-start(bf16[16,2,1280]{2,1,0:T(2,128)(2,1)} %broadcast_in_dim.94), calls=%async_computation.8 | async-start | bytes 163840 | tf_op jit(solution)/shard_map/all_to_all | solution.py:39

commit v7 on v5

--- a/solution.py
+++ b/solution.py
@@ -12,8 +12,10 @@
 BF16 = jnp.bfloat16
 
 
-def gelu_exact(value):
-    return jax.nn.gelu(value, approximate=False)
+def gelu_and_slope(value):
+    below = 0.5 * (1.0 + lax.erf(value * 0.5**0.5))
+    density = jnp.exp(-0.5 * value * value) * (1.0 / (2.0 * np.pi) ** 0.5)
+    return value * below, below + value * density
 
 
 def split3(value):
@@ -57,15 +59,24 @@
     return ids.transpose(1, 0, 2).reshape(depth, 2 * peers).tolist()
 
 
-def gather_dp(own):
-    far = everywhere(own, "dp", dp_groups(1))
-    return everywhere(far.reshape(-1, own.shape[1]), "dp", dp_groups(0, 2))
-
-
-def reduce_dp(partial, rows):
+def across_y(value):
+    depth = lax.axis_size("dp") // 2
+    pairs = [(y * depth + z, (1 - y) * depth + z) for y in range(2) for z in range(depth)]
+    return lax.ppermute(value, "dp", pairs)
+
+
+def gather_z(own, beside):
+    far = everywhere(own, "dp", dp_groups(1)).reshape(-1, own.shape[1])
+    far, beside = lax.optimization_barrier((far, beside))
+    return everywhere(far, "dp", dp_groups(2)), beside
+
+
+def reduce_z(partial, rows, beside):
     d = partial.shape[-1]
-    total = jnp.sum(exchange(partial, "dp", dp_groups(0, 2)).astype(F32), axis=0).astype(BF16)
-    return jnp.sum(exchange(total.reshape(-1, rows, d), "dp", dp_groups(1)).astype(F32), axis=0)
+    total = jnp.sum(exchange(partial, "dp", dp_groups(2)).astype(F32), axis=0).astype(BF16)
+    total, beside = lax.optimization_barrier((total, beside))
+    total = jnp.sum(exchange(total.reshape(-1, rows, d), "dp", dp_groups(1)).astype(F32), axis=0)
+    return total, beside
 
 
 def dot(left, right, left_dim=1, right_dim=0):
@@ -150,42 +161,68 @@
     token_grad_ref[...] = token_grad.astype(BF16)
 
 
-def call(kernel, out_shape, *operands):
+def call(kernel, out_shape, flops, *operands):
     shapes = [jax.ShapeDtypeStruct(shape, dtype) for shape, dtype in out_shape]
+    size = sum(value.size * value.dtype.itemsize for value in list(operands) + shapes)
     return pl.pallas_call(
         kernel,
         out_shape=shapes,
         compiler_params=pltpu.CompilerParams(vmem_limit_bytes=32 * 1024 * 1024),
-        cost_estimate=pl.CostEstimate(flops=120_000_000, bytes_accessed=2_000_000, transcendentals=16384),
+        cost_estimate=pl.CostEstimate(flops=flops, bytes_accessed=size, transcendentals=16384),
     )(*operands)
 
 
-def expert_part(gathered, w_in, w_out, imgs):
-    slots, d, _ = w_in.shape
-    rows = slots * imgs
-    blocks = (gathered.shape[0], gathered.shape[1] // (2 * rows), rows, d)
-    halves = gathered.reshape(blocks[:2] + (2 * rows, d))
-    all_in = halves[:, :, :rows].reshape(-1, d)
-    all_out_grad = halves[:, :, rows:].reshape(-1, d)
-    row = lax.broadcasted_iota(jnp.int32, (slots, all_in.shape[0], 1), 1)
-    slot = lax.broadcasted_iota(jnp.int32, (slots, all_in.shape[0], 1), 0)
-    mine = row % slots == slot
-    preact = jnp.einsum("rd,sdh->srh", all_in, w_in, preferred_element_type=F32)
-    activated_wide, pullback = jax.vjp(gelu_exact, preact)
-    activated = jnp.where(mine, activated_wide, 0.0).astype(BF16)
-    slot_out = jnp.einsum("srh,shd->rd", activated, w_out, preferred_element_type=F32)
-    act_grad = jnp.einsum("rd,shd->srh", all_out_grad, w_out, preferred_element_type=F32)
-    preact_grad = jnp.where(mine, pullback(act_grad)[0], 0.0).astype(BF16)
-    slot_in_grad = jnp.einsum("srh,sdh->rd", preact_grad, w_in, preferred_element_type=F32)
-    w_out_grad = jnp.einsum(
-        "srh,rd->shd", activated, all_out_grad, preferred_element_type=F32
-    ).astype(BF16)
-    w_in_grad = jnp.einsum(
-        "rd,srh->sdh", all_in, preact_grad, preferred_element_type=F32
-    ).astype(BF16)
-    pair = [value.astype(BF16).reshape(blocks) for value in (slot_out, slot_in_grad)]
-    partial = jnp.concatenate(pair, axis=2).reshape(gathered.shape)
-    return partial, w_in_grad, w_out_grad
+def picked(gathered, half, block):
+    total = gathered.shape[0]
+    row = lax.broadcasted_iota(jnp.int32, (total // 2, total), 0)
+    column = lax.broadcasted_iota(jnp.int32, (total // 2, total), 1)
+    here = (row // block) * (2 * block) + half * block + row % block == column
+    select = jnp.where(here, 1.0, 0.0).astype(BF16)
+    return dot(select, gathered).astype(BF16), select
+
+
+def hidden(all_in, all_out_grad, w_in, w_out, own_slots):
+    shape = (all_in.shape[0], w_in.shape[0])
+    row = lax.broadcasted_iota(jnp.int32, shape, 0)
+    column = lax.broadcasted_iota(jnp.int32, shape, 1)
+    mine = row % own_slots == column // (shape[1] // own_slots)
+    activated, slope = gelu_and_slope(dot(all_in, w_in, 1, 1))
+    preact_grad = dot(all_out_grad, w_out, 1, 1) * slope
+    return (
+        jnp.where(mine, activated, 0.0).astype(BF16),
+        jnp.where(mine, preact_grad, 0.0).astype(BF16),
+    )
+
+
+def experts(block, own_slots, gathered_ref, own_ref, other_ref, partial_ref):
+    gathered = gathered_ref[...]
+    all_in, first = picked(gathered, 0, block)
+    all_out_grad, second = picked(gathered, 1, block)
+    slot_out = jnp.zeros(all_in.shape, F32)
+    slot_in_grad = jnp.zeros(all_in.shape, F32)
+    for weights_ref in (own_ref, other_ref):
+        w_in, w_out = weights_ref[0], weights_ref[1]
+        activated, preact_grad = hidden(all_in, all_out_grad, w_in, w_out, own_slots)
+        slot_out += dot(activated, w_out)
+        slot_in_grad += dot(preact_grad, w_in)
+    partial = dot(first, slot_out.astype(BF16), 0, 0) + dot(second, slot_in_grad.astype(BF16), 0, 0)
+    partial_ref[...] = partial.astype(BF16)
+
+
+def weight_grads(
+    block, own_slots, gathered_ref, other_ref, weights_ref, w_in_grad_ref, w_out_grad_ref
+):
+    w_in, w_out = weights_ref[0], weights_ref[1]
+    w_in_grad = jnp.zeros(w_in.shape, F32)
+    w_out_grad = jnp.zeros(w_out.shape, F32)
+    for rows_ref in (gathered_ref, other_ref):
+        rows = rows_ref[...]
+        all_in, all_out_grad = picked(rows, 0, block)[0], picked(rows, 1, block)[0]
+        activated, preact_grad = hidden(all_in, all_out_grad, w_in, w_out, own_slots)
+        w_in_grad += dot(preact_grad, all_in, 0, 0)
+        w_out_grad += dot(activated, all_out_grad, 0, 0)
+    w_in_grad_ref[...] = w_in_grad.astype(BF16)
+    w_out_grad_ref[...] = w_out_grad.astype(BF16)
 
 
 def on_device(tokens, cotangent, slot_params, w_in, w_out):
@@ -201,12 +238,15 @@
     sent, logits, combine = call(
         functools.partial(route, imgs, own_slots),
         [((peers * rows, 2 * d + 128), BF16), (pairs, F32), (pairs, F32)],
-        params, flat_tok, flat_cot,
+        100_000_000, params, flat_tok, flat_cot,
     )
     taken = exchange(sent.reshape(peers, rows, 2 * d + 128), "expert")
-
-    peaks = join3(taken[:, :, d : d + 3])
-    masses = join3(taken[:, :, d + 3 : d + 6])
+    weights = jnp.stack([jnp.swapaxes(w_in, 1, 2).reshape(-1, d), w_out.reshape(-1, d)])
+    weights, head = lax.optimization_barrier((weights, taken[:, :, d : d + 128]))
+    weights_y = across_y(weights)
+
+    peaks = join3(head[:, :, :3])
+    masses = join3(head[:, :, 3:6])
     top = jnp.max(peaks, axis=0)
     scale = jnp.exp(peaks - top[None])
     total = jnp.sum(masses * scale, axis=0)
@@ -214,9 +254,21 @@
     slot_out_grad = jnp.sum(taken[:, :, d + 128 :].astype(F32), axis=0)
     own = jnp.concatenate([slot_in_wide.astype(BF16), slot_out_grad.astype(BF16)], axis=0)
 
-    gathered = gather_dp(own)
-    partial, w_in_grad, w_out_grad = expert_part(gathered, w_in, w_out, imgs)
-    owned_b = reduce_dp(partial, 2 * rows).astype(BF16).reshape(2, rows, d)
+    gathered, weights_y = gather_z(own, weights_y)
+    gathered_y = across_y(gathered)
+    flat = gathered.reshape(-1, d)
+    (partial,) = call(
+        functools.partial(experts, rows, own_slots), [(flat.shape, BF16)], 1_400_000_000,
+        flat, weights, weights_y,
+    )
+    owned_b, gathered_y = reduce_z(partial.reshape(gathered.shape), 2 * rows, gathered_y)
+    owned_b = owned_b.astype(BF16).reshape(2, rows, d)
+    w_in_grad, w_out_grad = call(
+        functools.partial(weight_grads, rows, own_slots), [(weights.shape[1:], BF16)] * 2,
+        1_400_000_000, flat, gathered_y.reshape(-1, d), weights,
+    )
+    w_in_grad = jnp.swapaxes(w_in_grad.reshape(own_slots, -1, d), 1, 2)
+    w_out_grad = w_out_grad.reshape(w_out.shape)
 
     col = jnp.sum(owned_b[1].astype(F32) * slot_in_wide, axis=1, keepdims=True)
     stats = jnp.concatenate(
@@ -226,7 +278,7 @@
     token_grad, share_grad = call(
         functools.partial(finish, imgs, own_slots),
         [(flat_tok.shape, BF16), ((slots, d), BF16)],
-        back.reshape(peers * rows, 2 * d + 128), logits, combine, params, flat_tok, flat_cot,
+        100_000_000, back.reshape(peers * rows, 2 * d + 128), logits, combine, params, flat_tok, flat_cot,
     )
     token_grad = token_grad.reshape(tokens.shape)
 

time: 193 us -> 200 us (1.036)
  blocking collectives: 117 us -> 98.3 us
  starting transfers between devices: 13.8 us -> 32 us
  Pallas kernels: 2.26 us -> 11.1 us
  matrix products: 5.12 us -> 0 us
  waiting for transfers between devices: 43.8 us -> 47 us
    all_to_all x6 -> x5, blocking collectives: 117 us -> 98.3 us  [exchange(): lax.all_to_all(value, axis, split_axis=0, concat_axis=0, axis_index_group...]
    all_to_all x3 -> x4, starting transfers between devices: 13.8 us -> 27.9 us  [exchange(): lax.all_to_all(value, axis, split_axis=0, concat_axis=0, axis_index_group...]
    ppermute x0 -> x2, waiting for transfers between devices: none -> 9.08 us  [across_y(): return lax.ppermute(value, 'dp', pairs)]
    pallas_call x2 -> x4, Pallas kernels: 2.26 us -> 11.1 us  [call(): pl.pallas_call(kernel, out_shape=shapes, compiler_params=pltpu.CompilerPa...]
    all_to_all x3 -> x4, waiting for transfers between devices: 43.8 us -> 38 us  [exchange(): lax.all_to_all(value, axis, split_axis=0, concat_axis=0, axis_index_group...]
    dot_general x5 -> x0, matrix products: 4.71 us -> none  [the longest x1 1.28 us: expert_part(): jnp.einsum('rd,srh->sdh', all_in, preact_grad, preferred_element_type=F32)]
    ppermute x0 -> x2, starting transfers between devices: none -> 4.12 us  [across_y(): return lax.ppermute(value, 'dp', pairs)]
  transfers between devices with their start and end apart: 3 -> 6, of which waited for: 3 -> 6; matrix products, arithmetic and copies ran while one was open for 2% -> 2% of each run, Pallas kernels for 0% -> 2%
where the time goes in v7:
time: 200 us; the launch traced here: 199 us
  blocking collectives  98.3 us (49%)
  waiting for transfers between devices  47 us (24%)
  starting transfers between devices  32 us (16%)
  Pallas kernels  11.1 us (6%)
  other arithmetic  5.18 us (3%)
  local copies, waits for them, and re-layouts  4.74 us (2%)
    all_to_all x5, blocking collectives, exchange(): lax.all_to_all(value, axis, split_axis=0, concat_axis=0, axis_index_group...  98.3 us
    all_to_all x4, waiting for transfers between devices, exchange(): lax.all_to_all(value, axis, split_axis=0, concat_axis=0, axis_index_group...  38 us
    all_to_all x4, starting transfers between devices, exchange(): lax.all_to_all(value, axis, split_axis=0, concat_axis=0, axis_index_group...  27.9 us
    pallas_call x4, Pallas kernels, call(): pl.pallas_call(kernel, out_shape=shapes, compiler_params=pltpu.CompilerPa...  11.1 us
    ppermute x2, waiting for transfers between devices, across_y(): return lax.ppermute(value, 'dp', pairs)  9.08 us
    ppermute x2, starting transfers between devices, across_y(): return lax.ppermute(value, 'dp', pairs)  4.12 us
  transfers between devices with their start and end apart: 6, of which 6 were waited for; matrix products, arithmetic and copies ran while one was open for 2% of the time, Pallas kernels for 2%

profile of v7, /device:TPU:1, one launch (start us, length us, event | category | flops | bytes accessed | tf_op | source)
XLA Modules:
  0.0 199.2 jit_solution(6941230599719703089)
XLA Ops:
  1.4 16.7 %all_to_all.45 = bf16[16,2,1280]{2,1,0:T(2,128)(2,1)S(1)} all-to-all(bf16[16,2,1280]{2,1,0:T(2,128)(2,1)S(1)} %broadcast_in_dim.16), channel_id=1, replica_groups=mesh['dp'=32,'expert'=16] {'expert'}, dimensions={0} | all-to-all | bytes 163840 | tf_op jit(solution)/shard_map/all_to_all | solution.py:42
  19.1 0.9 copy-done.2
  20.0 1.7 shard_map.84
  21.7 3.9 %all-to-all-start.1 = ((bf16[16,8,2688]{2,1,0:T(8,128)(2,1)}), bf16[16,8,2688]{2,1,0:T(8,128)(2,1)S(1)}, u32[]{:S(2)}, u32[]{:S(2)}) async-start(bf16[16,8,2688]{2,1,0:T(8,128)(2,1)} %bitcast.3), calls=%async_computation.1 | async-start | bytes 1376256 | tf_op jit(solution)/shard_map/all_to_all | solution.py:42
  25.5 1.5 pad_maximum_fusion.own_ref.weights_ref
  27.1 11.3 %all-to-all-done.1 = bf16[16,8,2688]{2,1,0:T(8,128)(2,1)S(1)} async-done(((bf16[16,8,2688]{2,1,0:T(8,128)(2,1)}), bf16[16,8,2688]{2,1,0:T(8,128)(2,1)S(1)}, u32[]{:S(2)}, u32[]{:S(2)}) %all-to-all-start.1) | async-done | bytes 688160 | tf_op jit(solution)/shard_map/all_to_all | solution.py:42
  39.0 1.9 collective-permute-start
  41.2 31.5 %all_to_all.46 = bf16[8,16,1280]{2,1,0:T(8,128)(2,1)S(1)} all-to-all(bf16[8,16,1280]{2,1,0:T(8,128)(2,1)S(1)} %broadcast_in_dim.17), channel_id=1, replica_groups={{0,32,64,96,128,160,192,224},{16,48,80,112,144,176,208,240},{256,288,32..., dimensions={0} | all-to-all | bytes 655360 | tf_op jit(solution)/shard_map/all_to_all | solution.py:42
  72.7 4.0 %collective-permute-done.other_ref = bf16[2,320,1280]{2,1,0:T(8,128)(2,1)S(1)} collective-permute-done((bf16[2,320,1280]{2,1,0:T(8,128)(2,1)S(1)}, bf16[2,320,1280]{2,1,0:T(8,128)(2,1)S(1)}, u32[]{:S(2)}, u32[]{:S(2)}) %collective-permute-start) | collective-permute-done | bytes 1638432 | tf_op jit(solution)/shard_map/ppermute | solution.py:65
  76.7 8.6 %all_to_all.47 = bf16[2,128,1280]{2,1,0:T(8,128)(2,1)S(1)} all-to-all(bf16[2,128,1280]{2,1,0:T(8,128)(2,1)S(1)} %broadcast_in_dim.18), channel_id=1, replica_groups={{0,16},{32,48},{64,80},{96,112},{128,144},{160,176},{192,208},{224,240}..., dimensions={0} | all-to-all | bytes 1310720 | tf_op jit(solution)/shard_map/all_to_all | solution.py:42
  85.3 3.4 %shard_map.85 = bf16[256,1280]{1,0:T(8,128)(2,1)} custom-call(bf16[256,1280]{1,0:T(8,128)(2,1)S(1)} %bitcast.49, bf16[2,320,1280]{2,1,0:T(8,128)(2,1)S(1)} %pad_maximum_fusion.own_ref.weights_ref, bf16[2,320,1280]{2,1,0:T(8,128)(2,1)S(1)} %collective-permute-done.other_ref), custom_call_target="tpu_custom_call" | custom-call | flops 1400000000 | bytes 4587520 | tf_op jit(solution)/shard_map/pallas_call | solution.py:167
  88.7 4.3 %all-to-all-start.4 = ((bf16[2,128,1280]{2,1,0:T(8,128)(2,1)}), bf16[2,128,1280]{2,1,0:T(8,128)(2,1)}, u32[]{:S(2)}, u32[]{:S(2)}) async-start(bf16[2,128,1280]{2,1,0:T(8,128)(2,1)} %bitcast.10), calls=%async_computation.4 | async-start | bytes 1310720 | tf_op jit(solution)/shard_map/all_to_all | solution.py:42
  93.0 2.2 %collective-permute-start.1 = (bf16[2,128,1280]{2,1,0:T(8,128)(2,1)S(1)}, bf16[2,128,1280]{2,1,0:T(8,128)(2,1)}, u32[]{:S(2)}, u32[]{:S(2)}) collective-permute-start(bf16[2,128,1280]{2,1,0:T(8,128)(2,1)S(1)} %all_to_all.47), channel_id=1, source_target_pairs={{0,256},{16,272},{32,288},{48,304},{64,320},{80,336},{96,352},{112... | collective-permute-start | bytes 1966088 | tf_op jit(solution)/shard_map/ppermute | solution.py:65
  95.2 4.0 %all-to-all-done.4 = bf16[2,128,1280]{2,1,0:T(8,128)(2,1)} async-done(((bf16[2,128,1280]{2,1,0:T(8,128)(2,1)}), bf16[2,128,1280]{2,1,0:T(8,128)(2,1)}, u32[]{:S(2)}, u32[]{:S(2)}) %all-to-all-start.4) | async-done | bytes 655392 | tf_op jit(solution)/shard_map/all_to_all | solution.py:42
  99.2 2.0 %reduce_sum.91 = bf16[128,1280]{1,0:T(8,128)(2,1)} reduce(bf16[2,128,1280]{2,1,0:T(8,128)(2,1)} %all-to-all-done.4, bf16[]{:T(256)} %constant.9.clone.1), dimensions={0}, to_apply=%region_4.0 | reduce | flops 163840 | bytes 983042 | tf_op jit(solution)/shard_map/reduce_sum | solution.py:76
  101.2 5.1 %collective-permute-done.1 = bf16[2,128,1280]{2,1,0:T(8,128)(2,1)} collective-permute-done((bf16[2,128,1280]{2,1,0:T(8,128)(2,1)S(1)}, bf16[2,128,1280]{2,1,0:T(8,128)(2,1)}, u32[]{:S(2)}, u32[]{:S(2)}) %collective-permute-start.1) | collective-permute-done | bytes 655392 | tf_op jit(solution)/shard_map/ppermute | solution.py:65
  106.3 16.3 %all-to-all-start.5 = ((bf16[8,16,1280]{2,1,0:T(8,128)(2,1)}), bf16[8,16,1280]{2,1,0:T(8,128)(2,1)S(1)}, u32[]{:S(2)}, u32[]{:S(2)}) async-start(bf16[8,16,1280]{2,1,0:T(8,128)(2,1)} %bitcast.11), calls=%async_computation.5 | async-start | bytes 655360 | tf_op jit(solution)/shard_map/all_to_all | solution.py:42
  123.1 15.5 %all-to-all-done.5 = bf16[8,16,1280]{2,1,0:T(8,128)(2,1)S(1)} async-done(((bf16[8,16,1280]{2,1,0:T(8,128)(2,1)}), bf16[8,16,1280]{2,1,0:T(8,128)(2,1)S(1)}, u32[]{:S(2)}, u32[]{:S(2)}) %all-to-all-start.5) | async-done | bytes 327712 | tf_op jit(solution)/shard_map/all_to_all | solution.py:42
  139.4 30.6 %all_to_all.48 = bf16[16,8,2688]{2,1,0:T(8,128)(2,1)S(1)} all-to-all(bf16[16,8,2688]{2,1,0:T(8,128)(2,1)S(1)} %broadcast_in_dim.20), channel_id=1, replica_groups=mesh['dp'=32,'expert'=16] {'expert'}, dimensions={0} | all-to-all | bytes 1376256 | tf_op jit(solution)/shard_map/all_to_all | solution.py:42
  170.0 1.4 shard_map.86
  171.6 10.9 %all_to_all.49 = bf16[32,2,1280]{2,1,0:T(2,128)(2,1)S(1)} all-to-all(bf16[32,2,1280]{2,1,0:T(2,128)(2,1)S(1)} %bitcast.54), channel_id=1, replica_groups={{0,1,2,3,4,5,6,7,8,9,10,11,12,13,14,15,256,257,258,259,260,261,262,263,..., dimensions={0} | all-to-all | bytes 327680 | tf_op jit(solution)/shard_map/all_to_all | solution.py:42
  183.3 3.5 %all-to-all-start.8 = ((bf16[16,2,1280]{2,1,0:T(2,128)(2,1)}), bf16[16,2,1280]{2,1,0:T(2,128)(2,1)S(1)}, u32[]{:S(2)}, u32[]{:S(2)}) async-start(bf16[16,2,1280]{2,1,0:T(2,128)(2,1)} %broadcast_in_dim.23), calls=%async_computation.8 | async-start | bytes 163840 | tf_op jit(solution)/shard_map/all_to_all | solution.py:42
  186.8 4.6 %shard_map.87 = (bf16[320,1280]{1,0:T(8,128)(2,1)}, bf16[320,1280]{1,0:T(8,128)(2,1)}) custom-call(bf16[256,1280]{1,0:T(8,128)(2,1)S(1)} %bitcast.50, bf16[256,1280]{1,0:T(8,128)(2,1)} %bitcast.19.other_ref, bf16[2,320,1280]{2,1,0:T(8,128)(2,1)S(1)} %pad_maximum_fusion.own_ref.weights_ref), custom_call_target="tpu_custom_call" | custom-call | flops 1400000000 | bytes 4587520 | tf_op jit(solution)/shard_map/pallas_call | solution.py:167
  191.4 7.1 %all-to-all-done.8 = bf16[16,2,1280]{2,1,0:T(2,128)(2,1)S(1)} async-done(((bf16[16,2,1280]{2,1,0:T(2,128)(2,1)}), bf16[16,2,1280]{2,1,0:T(2,128)(2,1)S(1)}, u32[]{:S(2)}, u32[]{:S(2)}) %all-to-all-start.8) | async-done | bytes 81952 | tf_op jit(solution)/shard_map/all_to_all | solution.py:42
  (44 shorter events, 5.5 us)
Async XLA Ops:
  18.1 0.9 copy-start
  19.1 0.9 copy-start.2
  21.7 16.7 %all-to-all-start.1 = ((bf16[16,8,2688]{2,1,0:T(8,128)(2,1)}), bf16[16,8,2688]{2,1,0:T(8,128)(2,1)S(1)}, u32[]{:S(2)}, u32[]{:S(2)}) async-start(bf16[16,8,2688]{2,1,0:T(8,128)(2,1)} %bitcast.3), calls=%async_computation.1 | async-start | bytes 1376256 | tf_op jit(solution)/shard_map/all_to_all | solution.py:42
  39.0 37.7 %collective-permute-start = (bf16[2,320,1280]{2,1,0:T(8,128)(2,1)S(1)}, bf16[2,320,1280]{2,1,0:T(8,128)(2,1)S(1)}, u32[]{:S(2)}, u32[]{:S(2)}) collective-permute-start(bf16[2,320,1280]{2,1,0:T(8,128)(2,1)S(1)} %pad_maximum_fusion.own_ref.weights_ref), channel_id=1, source_target_pairs={{0,256},{16,272},{32,288},{48,304},{64,320},{80,336},{96,352},{112... | collective-permute-start | bytes 4915208 | tf_op jit(solution)/shard_map/ppermute | solution.py:65
  88.7 10.5 %all-to-all-start.4 = ((bf16[2,128,1280]{2,1,0:T(8,128)(2,1)}), bf16[2,128,1280]{2,1,0:T(8,128)(2,1)}, u32[]{:S(2)}, u32[]{:S(2)}) async-start(bf16[2,128,1280]{2,1,0:T(8,128)(2,1)} %bitcast.10), calls=%async_computation.4 | async-start | bytes 1310720 | tf_op jit(solution)/shard_map/all_to_all | solution.py:42
  93.0 13.3 %collective-permute-start.1 = (bf16[2,128,1280]{2,1,0:T(8,128)(2,1)S(1)}, bf16[2,128,1280]{2,1,0:T(8,128)(2,1)}, u32[]{:S(2)}, u32[]{:S(2)}) collective-permute-start(bf16[2,128,1280]{2,1,0:T(8,128)(2,1)S(1)} %all_to_all.47), channel_id=1, source_target_pairs={{0,256},{16,272},{32,288},{48,304},{64,320},{80,336},{96,352},{112... | collective-permute-start | bytes 1966088 | tf_op jit(solution)/shard_map/ppermute | solution.py:65
  106.3 63.8 %copy-start.1 = (bf16[4,16,1280]{2,1,0:T(8,128)(2,1)S(1)}, bf16[4,16,1280]{2,1,0:T(8,128)(2,1)}, u32[]{:S(2)}) copy-start(bf16[4,16,1280]{2,1,0:T(8,128)(2,1)} %param.5) | copy-start | bytes 491524
  106.3 63.8 %copy-start.3 = (bf16[4,16,1280]{2,1,0:T(8,128)(2,1)S(1)}, bf16[4,16,1280]{2,1,0:T(8,128)(2,1)}, u32[]{:S(2)}) copy-start(bf16[4,16,1280]{2,1,0:T(8,128)(2,1)} %param.6) | copy-start | bytes 491524
  106.3 32.4 %all-to-all-start.5 = ((bf16[8,16,1280]{2,1,0:T(8,128)(2,1)}), bf16[8,16,1280]{2,1,0:T(8,128)(2,1)S(1)}, u32[]{:S(2)}, u32[]{:S(2)}) async-start(bf16[8,16,1280]{2,1,0:T(8,128)(2,1)} %bitcast.11), calls=%async_computation.5 | async-start | bytes 655360 | tf_op jit(solution)/shard_map/all_to_all | solution.py:42
  183.3 15.2 %all-to-all-start.8 = ((bf16[16,2,1280]{2,1,0:T(2,128)(2,1)}), bf16[16,2,1280]{2,1,0:T(2,128)(2,1)S(1)}, u32[]{:S(2)}, u32[]{:S(2)}) async-start(bf16[16,2,1280]{2,1,0:T(2,128)(2,1)} %broadcast_in_dim.23), calls=%async_computation.8 | async-start | bytes 163840 | tf_op jit(solution)/shard_map/all_to_all | solution.py:42

commit v8 on v7

--- a/solution.py
+++ b/solution.py
@@ -75,8 +75,9 @@
     d = partial.shape[-1]
     total = jnp.sum(exchange(partial, "dp", dp_groups(2)).astype(F32), axis=0).astype(BF16)
     total, beside = lax.optimization_barrier((total, beside))
+    beside = across_y(beside)
     total = jnp.sum(exchange(total.reshape(-1, rows, d), "dp", dp_groups(1)).astype(F32), axis=0)
-    return total, beside
+    return lax.optimization_barrier((total, beside))
 
 
 def dot(left, right, left_dim=1, right_dim=0):
@@ -117,8 +118,8 @@
     return jnp.sum(jnp.where(inside, block, 0.0), axis=1, keepdims=True)
 
 
-def route(imgs, own_slots, params_ref, tok_ref, cot_ref, sent_ref, logits_ref, combine_ref):
-    tokens, cotangent = tok_ref[...], cot_ref[...]
+def route(imgs, own_slots, params_ref, both_ref, sent_ref, logits_ref, combine_ref):
+    tokens, cotangent = both_ref[0], both_ref[1]
     slots, d = params_ref.shape
     rows, columns = logits_ref.shape
     spread = dot(slot_rows(rows, slots, imgs, own_slots), params_ref[...]).astype(BF16)
@@ -138,10 +139,10 @@
 
 
 def finish(
-    imgs, own_slots, back_ref, logits_ref, combine_ref, params_ref, tok_ref, cot_ref,
+    imgs, own_slots, back_ref, logits_ref, combine_ref, params_ref, both_ref,
     token_grad_ref, share_ref,
 ):
-    tokens, cotangent = tok_ref[...], cot_ref[...]
+    tokens, cotangent = both_ref[0], both_ref[1]
     slots, d = params_ref.shape
     rows = logits_ref.shape[0]
     slot_out, slot_in_grad = back_ref[:, :d], back_ref[:, d : 2 * d]
@@ -194,14 +195,17 @@
     )
 
 
-def experts(block, own_slots, gathered_ref, own_ref, other_ref, partial_ref):
+def experts(
+    block, own_slots, gathered_ref, w_in_ref, w_out_ref, early_ref, late_ref, partial_ref
+):
     gathered = gathered_ref[...]
     all_in, first = picked(gathered, 0, block)
     all_out_grad, second = picked(gathered, 1, block)
     slot_out = jnp.zeros(all_in.shape, F32)
     slot_in_grad = jnp.zeros(all_in.shape, F32)
-    for weights_ref in (own_ref, other_ref):
-        w_in, w_out = weights_ref[0], weights_ref[1]
+    rest = w_in_ref.shape[0] - early_ref.shape[0]
+    other_in = jnp.concatenate([early_ref[...], late_ref[:rest]], axis=0)
+    for w_in, w_out in ((w_in_ref[...], w_out_ref[...]), (other_in, late_ref[rest:])):
         activated, preact_grad = hidden(all_in, all_out_grad, w_in, w_out, own_slots)
         slot_out += dot(activated, w_out)
         slot_in_grad += dot(preact_grad, w_in)
@@ -210,9 +214,9 @@
 
 
 def weight_grads(
-    block, own_slots, gathered_ref, other_ref, weights_ref, w_in_grad_ref, w_out_grad_ref
+    block, own_slots, gathered_ref, other_ref, w_in_ref, w_out_ref, w_in_grad_ref, w_out_grad_ref
 ):
-    w_in, w_out = weights_ref[0], weights_ref[1]
+    w_in, w_out = w_in_ref[...], w_out_ref[...]
     w_in_grad = jnp.zeros(w_in.shape, F32)
     w_out_grad = jnp.zeros(w_out.shape, F32)
     for rows_ref in (gathered_ref, other_ref):
@@ -232,18 +236,23 @@
     slots = peers * own_slots
     rows = own_slots * imgs
 
+    flat_in, flat_out = jnp.swapaxes(w_in, 1, 2).reshape(-1, d), w_out.reshape(-1, d)
+    early = flat_in.shape[0] * 3 // 5 // 16 * 16
+    early_y = across_y(flat_in[:early])
+
     params = everywhere(slot_params.T, "expert").reshape(slots, d)
-    flat_tok, flat_cot = tokens.reshape(-1, d), cotangent.reshape(-1, d)
+    both = jnp.stack([tokens.reshape(-1, d), cotangent.reshape(-1, d)])
     pairs = (peers * rows, imgs * share)
     sent, logits, combine = call(
         functools.partial(route, imgs, own_slots),
         [((peers * rows, 2 * d + 128), BF16), (pairs, F32), (pairs, F32)],
-        100_000_000, params, flat_tok, flat_cot,
-    )
+        100_000_000, params, both,
+    )
+    sent, early_y = lax.optimization_barrier((sent, early_y))
     taken = exchange(sent.reshape(peers, rows, 2 * d + 128), "expert")
-    weights = jnp.stack([jnp.swapaxes(w_in, 1, 2).reshape(-1, d), w_out.reshape(-1, d)])
-    weights, head = lax.optimization_barrier((weights, taken[:, :, d : d + 128]))
-    weights_y = across_y(weights)
+    late = jnp.concatenate([flat_in[early:], flat_out], axis=0)
+    late, head = lax.optimization_barrier((late, taken[:, :, d : d + 128]))
+    late_y = across_y(late)
 
     peaks = join3(head[:, :, :3])
     masses = join3(head[:, :, 3:6])
@@ -254,18 +263,17 @@
     slot_out_grad = jnp.sum(taken[:, :, d + 128 :].astype(F32), axis=0)
     own = jnp.concatenate([slot_in_wide.astype(BF16), slot_out_grad.astype(BF16)], axis=0)
 
-    gathered, weights_y = gather_z(own, weights_y)
-    gathered_y = across_y(gathered)
+    gathered, late_y = gather_z(own, late_y)
     flat = gathered.reshape(-1, d)
     (partial,) = call(
         functools.partial(experts, rows, own_slots), [(flat.shape, BF16)], 1_400_000_000,
-        flat, weights, weights_y,
-    )
-    owned_b, gathered_y = reduce_z(partial.reshape(gathered.shape), 2 * rows, gathered_y)
+        flat, flat_in, flat_out, early_y, late_y,
+    )
+    owned_b, gathered_y = reduce_z(partial.reshape(gathered.shape), 2 * rows, gathered)
     owned_b = owned_b.astype(BF16).reshape(2, rows, d)
     w_in_grad, w_out_grad = call(
-        functools.partial(weight_grads, rows, own_slots), [(weights.shape[1:], BF16)] * 2,
-        1_400_000_000, flat, gathered_y.reshape(-1, d), weights,
+        functools.partial(weight_grads, rows, own_slots), [(flat_in.shape, BF16)] * 2,
+        1_400_000_000, flat, gathered_y.reshape(-1, d), flat_in, flat_out,
     )
     w_in_grad = jnp.swapaxes(w_in_grad.reshape(own_slots, -1, d), 1, 2)
     w_out_grad = w_out_grad.reshape(w_out.shape)
@@ -277,8 +285,8 @@
     back = everywhere(jnp.concatenate([owned_b[0], owned_b[1], stats], axis=1), "expert")
     token_grad, share_grad = call(
         functools.partial(finish, imgs, own_slots),
-        [(flat_tok.shape, BF16), ((slots, d), BF16)],
-        100_000_000, back.reshape(peers * rows, 2 * d + 128), logits, combine, params, flat_tok, flat_cot,
+        [(both.shape[1:], BF16), ((slots, d), BF16)],
+        100_000_000, back.reshape(peers * rows, 2 * d + 128), logits, combine, params, both,
     )
     token_grad = token_grad.reshape(tokens.shape)
 

time: 200 us -> 199 us (level)
  blocking collectives: 98.3 us -> 57.4 us
  starting transfers between devices: 32 us -> 51 us
  waiting for transfers between devices: 47 us -> 66 us
    all_to_all x5 -> x4, blocking collectives: 98.3 us -> 57.4 us  [exchange(): lax.all_to_all(value, axis, split_axis=0, concat_axis=0, axis_index_group...]
    all_to_all x4 -> x5, waiting for transfers between devices: 38 us -> 55.9 us  [exchange(): lax.all_to_all(value, axis, split_axis=0, concat_axis=0, axis_index_group...]
    all_to_all x4 -> x5, starting transfers between devices: 27.9 us -> 43 us  [exchange(): lax.all_to_all(value, axis, split_axis=0, concat_axis=0, axis_index_group...]
    ppermute x2 -> x3, starting transfers between devices: 4.12 us -> 7.95 us  [across_y(): return lax.ppermute(value, 'dp', pairs)]
    ppermute x2 -> x3, waiting for transfers between devices: 9.08 us -> 10.1 us  [across_y(): return lax.ppermute(value, 'dp', pairs)]
  transfers between devices with their start and end apart: 6 -> 8, of which waited for: 6 -> 6; matrix products, arithmetic and copies ran while one was open for 2% -> 2% of each run, Pallas kernels for 2% -> 3%
where the time goes in v8:
time: 199 us; the launch traced here: 198 us
  waiting for transfers between devices  66 us (33%)
  blocking collectives  57.4 us (29%)
  starting transfers between devices  51 us (26%)
  Pallas kernels  11.5 us (6%)
  local copies, waits for them, and re-layouts  6.12 us (3%)
  other arithmetic  5.46 us (3%)
    all_to_all x4, blocking collectives, exchange(): lax.all_to_all(value, axis, split_axis=0, concat_axis=0, axis_index_group...  57.4 us
    all_to_all x5, waiting for transfers between devices, exchange(): lax.all_to_all(value, axis, split_axis=0, concat_axis=0, axis_index_group...  55.9 us
    all_to_all x5, starting transfers between devices, exchange(): lax.all_to_all(value, axis, split_axis=0, concat_axis=0, axis_index_group...  43 us
    pallas_call x4, Pallas kernels, call(): pl.pallas_call(kernel, out_shape=shapes, compiler_params=pltpu.CompilerPa...  11.5 us
    ppermute x3, waiting for transfers between devices, across_y(): return lax.ppermute(value, 'dp', pairs)  10.1 us
    ppermute x3, starting transfers between devices, across_y(): return lax.ppermute(value, 'dp', pairs)  7.95 us
  transfers between devices with their start and end apart: 8, of which 6 were waited for; matrix products, arithmetic and copies ran while one was open for 2% of the time, Pallas kernels for 3%

profile of v8, /device:TPU:1, one launch (start us, length us, event | category | flops | bytes accessed | tf_op | source)
XLA Modules:
  0.0 198.3 jit_solution(16432960247290803446)
XLA Ops:
  1.8 4.0 %collective-permute-start = (bf16[192,1280]{1,0:T(8,128)(2,1)S(1)}, bf16[192,1280]{1,0:T(8,128)(2,1)S(1)}, u32[]{:S(2)}, u32[]{:S(2)}) collective-permute-start(bf16[192,1280]{1,0:T(8,128)(2,1)S(1)} %slice.63), channel_id=1, source_target_pairs={{0,256},{16,272},{32,288},{48,304},{64,320},{80,336},{96,352},{112... | collective-permute-start | bytes 1474568 | tf_op jit(solution)/shard_map/ppermute | solution.py:65
  5.8 1.4 broadcast_in_dim.16
  7.2 8.1 %all-to-all-start = ((bf16[16,2,1280]{2,1,0:T(2,128)(2,1)}), bf16[16,2,1280]{2,1,0:T(2,128)(2,1)S(1)}, u32[]{:S(2)}, u32[]{:S(2)}) async-start(bf16[16,2,1280]{2,1,0:T(2,128)(2,1)} %broadcast_in_dim.16), calls=%async_computation | async-start | bytes 163840 | tf_op jit(solution)/shard_map/all_to_all | solution.py:42
  15.3 7.4 %all-to-all-done = bf16[16,2,1280]{2,1,0:T(2,128)(2,1)S(1)} async-done(((bf16[16,2,1280]{2,1,0:T(2,128)(2,1)}), bf16[16,2,1280]{2,1,0:T(2,128)(2,1)S(1)}, u32[]{:S(2)}, u32[]{:S(2)}) %all-to-all-start) | async-done | bytes 81952 | tf_op jit(solution)/shard_map/all_to_all | solution.py:42
  22.7 1.7 shard_map.84
  24.4 3.9 %all-to-all-start.1 = ((bf16[16,8,2688]{2,1,0:T(8,128)(2,1)}), bf16[16,8,2688]{2,1,0:T(8,128)(2,1)S(1)}, u32[]{:S(2)}, u32[]{:S(2)}) async-start(bf16[16,8,2688]{2,1,0:T(8,128)(2,1)} %bitcast.5), calls=%async_computation.1 | async-start | bytes 1376256 | tf_op jit(solution)/shard_map/all_to_all | solution.py:42
  29.4 11.7 %all-to-all-done.1 = bf16[16,8,2688]{2,1,0:T(8,128)(2,1)S(1)} async-done(((bf16[16,8,2688]{2,1,0:T(8,128)(2,1)}), bf16[16,8,2688]{2,1,0:T(8,128)(2,1)S(1)}, u32[]{:S(2)}, u32[]{:S(2)}) %all-to-all-start.1) | async-done | bytes 688160 | tf_op jit(solution)/shard_map/all_to_all | solution.py:42
  44.1 14.2 %all-to-all-start.2 = ((bf16[8,16,1280]{2,1,0:T(8,128)(2,1)}), bf16[8,16,1280]{2,1,0:T(8,128)(2,1)S(1)}, u32[]{:S(2)}, u32[]{:S(2)}) async-start(bf16[8,16,1280]{2,1,0:T(8,128)(2,1)} %broadcast_in_dim.17), calls=%async_computation.2 | async-start | bytes 655360 | tf_op jit(solution)/shard_map/all_to_all | solution.py:42
  58.4 1.9 collective-permute-start.1
  60.3 15.2 %all-to-all-done.2 = bf16[8,16,1280]{2,1,0:T(8,128)(2,1)S(1)} async-done(((bf16[8,16,1280]{2,1,0:T(8,128)(2,1)}), bf16[8,16,1280]{2,1,0:T(8,128)(2,1)S(1)}, u32[]{:S(2)}, u32[]{:S(2)}) %all-to-all-start.2) | async-done | bytes 327712 | tf_op jit(solution)/shard_map/all_to_all | solution.py:42
  75.5 10.1 %collective-permute-done.1.late_ref = bf16[448,1280]{1,0:T(8,128)(2,1)} collective-permute-done((bf16[448,1280]{1,0:T(8,128)(2,1)}, bf16[448,1280]{1,0:T(8,128)(2,1)}, u32[]{:S(2)}, u32[]{:S(2)}) %collective-permute-start.1) | collective-permute-done | bytes 1146912 | tf_op jit(solution)/shard_map/ppermute | solution.py:65
  85.6 9.2 %all_to_all.45 = bf16[2,128,1280]{2,1,0:T(8,128)(2,1)S(1)} all-to-all(bf16[2,128,1280]{2,1,0:T(8,128)(2,1)S(1)} %broadcast_in_dim.18), channel_id=1, replica_groups={{0,16},{32,48},{64,80},{96,112},{128,144},{160,176},{192,208},{224,240}..., dimensions={0} | all-to-all | bytes 1310720 | tf_op jit(solution)/shard_map/all_to_all | solution.py:42
  94.8 3.8 %shard_map.85 = bf16[256,1280]{1,0:T(8,128)(2,1)S(1)} custom-call(bf16[256,1280]{1,0:T(8,128)(2,1)S(1)} %bitcast.52, bf16[320,1280]{1,0:T(8,128)(2,1)S(1)} %bitcast.50, bf16[320,1280]{1,0:T(8,128)(2,1)S(1)} %bitcast.46, bf16[192,1280]{1,0:T(8,128)(2,1)S(1)} %collective-permute-done.early_ref, bf16[448,1280]{1,0:T(8,128)(2,1)} %collective-permute-done.1.late_ref), custom_call_target="tpu_custom_call" | custom-call | flops 1400000000 | bytes 4587520 | tf_op jit(solution)/shard_map/pallas_call | solution.py:168
  98.6 9.3 %all_to_all.46 = bf16[2,128,1280]{2,1,0:T(8,128)(2,1)} all-to-all(bf16[2,128,1280]{2,1,0:T(8,128)(2,1)S(1)} %bitcast.54), channel_id=1, replica_groups={{0,16},{32,48},{64,80},{96,112},{128,144},{160,176},{192,208},{224,240}..., dimensions={0} | all-to-all | bytes 1310720 | tf_op jit(solution)/shard_map/all_to_all | solution.py:42
  107.9 2.0 %reduce_sum.88 = bf16[128,1280]{1,0:T(8,128)(2,1)} reduce(bf16[2,128,1280]{2,1,0:T(8,128)(2,1)} %all_to_all.46, bf16[]{:T(256)} %constant.8.clone.1), dimensions={0}, to_apply=%region_4.0 | reduce | flops 163840 | bytes 983042 | tf_op jit(solution)/shard_map/reduce_sum | solution.py:76
  109.9 10.9 %all-to-all-start.5 = ((bf16[8,16,1280]{2,1,0:T(8,128)(2,1)}), bf16[8,16,1280]{2,1,0:T(8,128)(2,1)S(1)}, u32[]{:S(2)}, u32[]{:S(2)}) async-start(bf16[8,16,1280]{2,1,0:T(8,128)(2,1)} %bitcast.12), calls=%async_computation.5 | async-start | bytes 655360 | tf_op jit(solution)/shard_map/all_to_all | solution.py:42
  120.8 2.0 %collective-permute-start.2 = (bf16[2,128,1280]{2,1,0:T(8,128)(2,1)S(1)}, bf16[2,128,1280]{2,1,0:T(8,128)(2,1)}, u32[]{:S(2)}, u32[]{:S(2)}) collective-permute-start(bf16[2,128,1280]{2,1,0:T(8,128)(2,1)S(1)} %all_to_all.45), channel_id=1, source_target_pairs={{0,256},{16,272},{32,288},{48,304},{64,320},{80,336},{96,352},{112... | collective-permute-start | bytes 1966088 | tf_op jit(solution)/shard_map/ppermute | solution.py:65
  123.4 14.4 %all-to-all-done.5 = bf16[8,16,1280]{2,1,0:T(8,128)(2,1)S(1)} async-done(((bf16[8,16,1280]{2,1,0:T(8,128)(2,1)}), bf16[8,16,1280]{2,1,0:T(8,128)(2,1)S(1)}, u32[]{:S(2)}, u32[]{:S(2)}) %all-to-all-start.5) | async-done | bytes 327712 | tf_op jit(solution)/shard_map/all_to_all | solution.py:42
  138.5 28.1 %all_to_all.47 = bf16[16,8,2688]{2,1,0:T(8,128)(2,1)S(1)} all-to-all(bf16[16,8,2688]{2,1,0:T(8,128)(2,1)S(1)} %broadcast_in_dim.20), channel_id=1, replica_groups=mesh['dp'=32,'expert'=16] {'expert'}, dimensions={0} | all-to-all | bytes 1376256 | tf_op jit(solution)/shard_map/all_to_all | solution.py:42
  166.6 1.4 shard_map.86
  168.1 10.9 %all_to_all.48 = bf16[32,2,1280]{2,1,0:T(2,128)(2,1)S(1)} all-to-all(bf16[32,2,1280]{2,1,0:T(2,128)(2,1)S(1)} %bitcast.56), channel_id=1, replica_groups={{0,1,2,3,4,5,6,7,8,9,10,11,12,13,14,15,256,257,258,259,260,261,262,263,..., dimensions={0} | all-to-all | bytes 327680 | tf_op jit(solution)/shard_map/all_to_all | solution.py:42
  179.9 6.0 %all-to-all-start.8 = ((bf16[16,2,1280]{2,1,0:T(2,128)(2,1)}), bf16[16,2,1280]{2,1,0:T(2,128)(2,1)S(1)}, u32[]{:S(2)}, u32[]{:S(2)}) async-start(bf16[16,2,1280]{2,1,0:T(2,128)(2,1)} %broadcast_in_dim.23), calls=%async_computation.8 | async-start | bytes 163840 | tf_op jit(solution)/shard_map/all_to_all | solution.py:42
  185.9 4.6 %shard_map.87 = (bf16[320,1280]{1,0:T(8,128)(2,1)}, bf16[320,1280]{1,0:T(8,128)(2,1)}) custom-call(bf16[256,1280]{1,0:T(8,128)(2,1)S(1)} %bitcast.53, bf16[256,1280]{1,0:T(8,128)(2,1)} %bitcast.20.other_ref, bf16[320,1280]{1,0:T(8,128)(2,1)S(1)} %bitcast.51, bf16[320,1280]{1,0:T(8,128)(2,1)S(1)} %bitcast.47), custom_call_target="tpu_custom_call" | custom-call | flops 1400000000 | bytes 4587520 | tf_op jit(solution)/shard_map/pallas_call | solution.py:168
  190.5 7.2 %all-to-all-done.8 = bf16[16,2,1280]{2,1,0:T(2,128)(2,1)S(1)} async-done(((bf16[16,2,1280]{2,1,0:T(2,128)(2,1)}), bf16[16,2,1280]{2,1,0:T(2,128)(2,1)S(1)}, u32[]{:S(2)}, u32[]{:S(2)}) %all-to-all-start.8) | async-done | bytes 81952 | tf_op jit(solution)/shard_map/all_to_all | solution.py:42
  (50 shorter events, 8.2 us)
Async XLA Ops:
  0.6 14.6 %copy-start.3 = (bf16[4,16,1280]{2,1,0:T(8,128)(2,1)S(1)}, bf16[4,16,1280]{2,1,0:T(8,128)(2,1)}, u32[]{:S(2)}) copy-start(bf16[4,16,1280]{2,1,0:T(8,128)(2,1)} %param.5) | copy-start | bytes 491524
  0.6 14.6 %copy-start.2 = (bf16[4,16,1280]{2,1,0:T(8,128)(2,1)S(1)}, bf16[4,16,1280]{2,1,0:T(8,128)(2,1)}, u32[]{:S(2)}) copy-start(bf16[4,16,1280]{2,1,0:T(8,128)(2,1)} %param.6) | copy-start | bytes 491524
  1.8 22.7 %collective-permute-start = (bf16[192,1280]{1,0:T(8,128)(2,1)S(1)}, bf16[192,1280]{1,0:T(8,128)(2,1)S(1)}, u32[]{:S(2)}, u32[]{:S(2)}) collective-permute-start(bf16[192,1280]{1,0:T(8,128)(2,1)S(1)} %slice.63), channel_id=1, source_target_pairs={{0,256},{16,272},{32,288},{48,304},{64,320},{80,336},{96,352},{112... | collective-permute-start | bytes 1474568 | tf_op jit(solution)/shard_map/ppermute | solution.py:65
  7.2 15.5 %all-to-all-start = ((bf16[16,2,1280]{2,1,0:T(2,128)(2,1)}), bf16[16,2,1280]{2,1,0:T(2,128)(2,1)S(1)}, u32[]{:S(2)}, u32[]{:S(2)}) async-start(bf16[16,2,1280]{2,1,0:T(2,128)(2,1)} %broadcast_in_dim.16), calls=%async_computation | async-start | bytes 163840 | tf_op jit(solution)/shard_map/all_to_all | solution.py:42
  15.3 13.0 %copy-start.1 = (bf16[2,1280,160]{1,2,0:T(8,128)(2,1)S(1)}, bf16[2,1280,160]{1,2,0:T(8,128)(2,1)}, u32[]{:S(2)}) copy-start(bf16[2,1280,160]{1,2,0:T(8,128)(2,1)} %param.8) | copy-start | bytes 2457604
  22.7 5.6 %copy-start = (bf16[2,160,1280]{2,1,0:T(8,128)(2,1)S(1)}, bf16[2,160,1280]{2,1,0:T(8,128)(2,1)}, u32[]{:S(2)}) copy-start(bf16[2,160,1280]{2,1,0:T(8,128)(2,1)} %param.9) | copy-start | bytes 2457604
  24.4 16.7 %all-to-all-start.1 = ((bf16[16,8,2688]{2,1,0:T(8,128)(2,1)}), bf16[16,8,2688]{2,1,0:T(8,128)(2,1)S(1)}, u32[]{:S(2)}, u32[]{:S(2)}) async-start(bf16[16,8,2688]{2,1,0:T(8,128)(2,1)} %bitcast.5), calls=%async_computation.1 | async-start | bytes 1376256 | tf_op jit(solution)/shard_map/all_to_all | solution.py:42
  44.1 31.4 %all-to-all-start.2 = ((bf16[8,16,1280]{2,1,0:T(8,128)(2,1)}), bf16[8,16,1280]{2,1,0:T(8,128)(2,1)S(1)}, u32[]{:S(2)}, u32[]{:S(2)}) async-start(bf16[8,16,1280]{2,1,0:T(8,128)(2,1)} %broadcast_in_dim.17), calls=%async_computation.2 | async-start | bytes 655360 | tf_op jit(solution)/shard_map/all_to_all | solution.py:42
  58.4 27.2 %collective-permute-start.1 = (bf16[448,1280]{1,0:T(8,128)(2,1)}, bf16[448,1280]{1,0:T(8,128)(2,1)}, u32[]{:S(2)}, u32[]{:S(2)}) collective-permute-start(bf16[448,1280]{1,0:T(8,128)(2,1)} %pad_maximum_fusion), channel_id=1, source_target_pairs={{0,256},{16,272},{32,288},{48,304},{64,320},{80,336},{96,352},{112... | collective-permute-start | bytes 3440648 | tf_op jit(solution)/shard_map/ppermute | solution.py:65
  109.9 27.9 %all-to-all-start.5 = ((bf16[8,16,1280]{2,1,0:T(8,128)(2,1)}), bf16[8,16,1280]{2,1,0:T(8,128)(2,1)S(1)}, u32[]{:S(2)}, u32[]{:S(2)}) async-start(bf16[8,16,1280]{2,1,0:T(8,128)(2,1)} %bitcast.12), calls=%async_computation.5 | async-start | bytes 655360 | tf_op jit(solution)/shard_map/all_to_all | solution.py:42
  120.8 17.0 %collective-permute-start.2 = (bf16[2,128,1280]{2,1,0:T(8,128)(2,1)S(1)}, bf16[2,128,1280]{2,1,0:T(8,128)(2,1)}, u32[]{:S(2)}, u32[]{:S(2)}) collective-permute-start(bf16[2,128,1280]{2,1,0:T(8,128)(2,1)S(1)} %all_to_all.45), channel_id=1, source_target_pairs={{0,256},{16,272},{32,288},{48,304},{64,320},{80,336},{96,352},{112... | collective-permute-start | bytes 1966088 | tf_op jit(solution)/shard_map/ppermute | solution.py:65
  179.9 17.8 %all-to-all-start.8 = ((bf16[16,2,1280]{2,1,0:T(2,128)(2,1)}), bf16[16,2,1280]{2,1,0:T(2,128)(2,1)S(1)}, u32[]{:S(2)}, u32[]{:S(2)}) async-start(bf16[16,2,1280]{2,1,0:T(2,128)(2,1)} %broadcast_in_dim.23), calls=%async_computation.8 | async-start | bytes 163840 | tf_op jit(solution)/shard_map/all_to_all | solution.py:42

commit v9 on v5

--- a/solution.py
+++ b/solution.py
@@ -58,12 +58,13 @@
 
 
 def gather_dp(own):
-    far = everywhere(own, "dp", dp_groups(1))
-    return everywhere(far.reshape(-1, own.shape[1]), "dp", dp_groups(0, 2))
+    whole = lax.all_gather(own, "dp", axis=0, tiled=True)
+    return whole.reshape(2, -1, 2 * own.shape[0], own.shape[1])
 
 
 def reduce_dp(partial, rows):
     d = partial.shape[-1]
+    partial = jnp.transpose(partial.reshape(2, -1, 2, rows, d), (0, 2, 1, 3, 4)).reshape(4, -1, d)
     total = jnp.sum(exchange(partial, "dp", dp_groups(0, 2)).astype(F32), axis=0).astype(BF16)
     return jnp.sum(exchange(total.reshape(-1, rows, d), "dp", dp_groups(1)).astype(F32), axis=0)
 
@@ -106,8 +107,8 @@
     return jnp.sum(jnp.where(inside, block, 0.0), axis=1, keepdims=True)
 
 
-def route(imgs, own_slots, params_ref, tok_ref, cot_ref, sent_ref, logits_ref, combine_ref):
-    tokens, cotangent = tok_ref[...], cot_ref[...]
+def route(imgs, own_slots, params_ref, both_ref, sent_ref, logits_ref, combine_ref):
+    tokens, cotangent = both_ref[0], both_ref[1]
     slots, d = params_ref.shape
     rows, columns = logits_ref.shape
     spread = dot(slot_rows(rows, slots, imgs, own_slots), params_ref[...]).astype(BF16)
@@ -127,10 +128,10 @@
 
 
 def finish(
-    imgs, own_slots, back_ref, logits_ref, combine_ref, params_ref, tok_ref, cot_ref,
+    imgs, own_slots, back_ref, logits_ref, combine_ref, params_ref, both_ref,
     token_grad_ref, share_ref,
 ):
-    tokens, cotangent = tok_ref[...], cot_ref[...]
+    tokens, cotangent = both_ref[0], both_ref[1]
     slots, d = params_ref.shape
     rows = logits_ref.shape[0]
     slot_out, slot_in_grad = back_ref[:, :d], back_ref[:, d : 2 * d]
@@ -163,7 +164,7 @@
 def expert_part(gathered, w_in, w_out, imgs):
     slots, d, _ = w_in.shape
     rows = slots * imgs
-    blocks = (gathered.shape[0], gathered.shape[1] // (2 * rows), rows, d)
+    blocks = (gathered.shape[0], 2 * gathered.shape[1], rows, d)
     halves = gathered.reshape(blocks[:2] + (2 * rows, d))
     all_in = halves[:, :, :rows].reshape(-1, d)
     all_out_grad = halves[:, :, rows:].reshape(-1, d)
@@ -196,12 +197,12 @@
     rows = own_slots * imgs
 
     params = everywhere(slot_params.T, "expert").reshape(slots, d)
-    flat_tok, flat_cot = tokens.reshape(-1, d), cotangent.reshape(-1, d)
+    both = jnp.stack([tokens.reshape(-1, d), cotangent.reshape(-1, d)])
     pairs = (peers * rows, imgs * share)
     sent, logits, combine = call(
         functools.partial(route, imgs, own_slots),
         [((peers * rows, 2 * d + 128), BF16), (pairs, F32), (pairs, F32)],
-        params, flat_tok, flat_cot,
+        params, both,
     )
     taken = exchange(sent.reshape(peers, rows, 2 * d + 128), "expert")
 
@@ -225,8 +226,8 @@
     back = everywhere(jnp.concatenate([owned_b[0], owned_b[1], stats], axis=1), "expert")
     token_grad, share_grad = call(
         functools.partial(finish, imgs, own_slots),
-        [(flat_tok.shape, BF16), ((slots, d), BF16)],
-        back.reshape(peers * rows, 2 * d + 128), logits, combine, params, flat_tok, flat_cot,
+        [(both.shape[1:], BF16), ((slots, d), BF16)],
+        back.reshape(peers * rows, 2 * d + 128), logits, combine, params, both,
     )
     token_grad = token_grad.reshape(tokens.shape)
 

time: 193 us -> 282 us (1.46)
  waiting for transfers between devices: 43.8 us -> 144 us
  blocking collectives: 117 us -> 87.5 us
  between operations: 0.87 us -> 14.3 us
  starting transfers between devices: 13.8 us -> 18 us
    all_gather x0 -> x1, waiting for transfers between devices: none -> 109 us  [gather_dp(): whole = lax.all_gather(own, 'dp', axis=0, tiled=True)]
    all_to_all x6 -> x4, blocking collectives: 117 us -> 87.5 us  [exchange(): lax.all_to_all(value, axis, split_axis=0, concat_axis=0, axis_index_group...]
    all_to_all x3, waiting for transfers between devices: 43.8 us -> 35 us  [exchange(): lax.all_to_all(value, axis, split_axis=0, concat_axis=0, axis_index_group...]
    all_to_all x3, starting transfers between devices: 13.8 us -> 18 us  [exchange(): lax.all_to_all(value, axis, split_axis=0, concat_axis=0, axis_index_group...]
  transfers between devices with their start and end apart: 3 -> 4, of which waited for: 3 -> 4; matrix products, arithmetic and copies ran while one was open for 2% -> 1% of each run, Pallas kernels for 0% -> 0%
where the time goes in v9:
time: 282 us
  waiting for transfers between devices  144 us (51%)
  blocking collectives  87.5 us (31%)
  starting transfers between devices  18 us (6%)
  between operations  14.3 us (5%)
  local copies, waits for them, and re-layouts  5.44 us (2%)
  other arithmetic  5.15 us (2%)
  matrix products  5.11 us (2%)
    all_gather x1, waiting for transfers between devices, gather_dp(): whole = lax.all_gather(own, 'dp', axis=0, tiled=True)  109 us
    all_to_all x4, blocking collectives, exchange(): lax.all_to_all(value, axis, split_axis=0, concat_axis=0, axis_index_group...  87.5 us
    all_to_all x3, waiting for transfers between devices, exchange(): lax.all_to_all(value, axis, split_axis=0, concat_axis=0, axis_index_group...  35 us
    all_to_all x3, starting transfers between devices, exchange(): lax.all_to_all(value, axis, split_axis=0, concat_axis=0, axis_index_group...  18 us
  transfers between devices with their start and end apart: 4, of which 4 were waited for; matrix products, arithmetic and copies ran while one was open for 1% of the time, Pallas kernels for 0%

profile of v9, /device:TPU:1, one launch (start us, length us, event | category | flops | bytes accessed | tf_op | source)
XLA Modules:
  0.0 281.6 jit_solution(7679545836649408952)
XLA Ops:
  7.2 1.4 broadcast_in_dim.47
  8.6 10.2 %all-to-all-start = ((bf16[16,2,1280]{2,1,0:T(2,128)(2,1)}), bf16[16,2,1280]{2,1,0:T(2,128)(2,1)S(1)}, u32[]{:S(2)}, u32[]{:S(2)}) async-start(bf16[16,2,1280]{2,1,0:T(2,128)(2,1)} %broadcast_in_dim.47), calls=%async_computation | async-start | bytes 163840 | tf_op jit(solution)/shard_map/all_to_all | solution.py:40
  18.8 1.0 pad_maximum_fusion.1.both_ref
  19.9 6.4 %all-to-all-done = bf16[16,2,1280]{2,1,0:T(2,128)(2,1)S(1)} async-done(((bf16[16,2,1280]{2,1,0:T(2,128)(2,1)}), bf16[16,2,1280]{2,1,0:T(2,128)(2,1)S(1)}, u32[]{:S(2)}, u32[]{:S(2)}) %all-to-all-start) | async-done | bytes 81952 | tf_op jit(solution)/shard_map/all_to_all | solution.py:40
  26.3 0.8 shard_map.84
  27.1 16.5 %all_to_all.35 = bf16[16,8,2688]{2,1,0:T(8,128)(2,1)S(1)} all-to-all(bf16[16,8,2688]{2,1,0:T(8,128)(2,1)S(1)} %bitcast.156), channel_id=1, replica_groups=mesh['dp'=32,'expert'=16] {'expert'}, dimensions={0} | all-to-all | bytes 1376256 | tf_op jit(solution)/shard_map/all_to_all | solution.py:40
  44.7 0.6 pad_maximum_fusion.2
  45.4 108.8 %all-gather.2.cloned.1.call-done = bf16[512,1280]{1,0:T(8,128)(2,1)} async-done(((bf16[16,1280]{1,0:T(8,128)(2,1)}), bf16[512,1280]{1,0:T(8,128)(2,1)}) %all-gather.2.cloned.1.call-update) | async-done | bytes 1310736 | tf_op jit(solution)/shard_map/all_gather | solution.py:61
  154.2 1.4 fusion.35
  156.0 0.7 fusion.6
  157.0 1.1 fusion.13
  159.4 13.1 %all_to_all.36 = bf16[4,128,1280]{2,1,0:T(8,128)(2,1)S(1)} all-to-all(bf16[4,128,1280]{2,1,0:T(8,128)(2,1)S(1)} %bitcast.159), channel_id=1, replica_groups={{0,16,256,272},{32,48,288,304},{64,80,320,336},{96,112,352,368},{128,14..., dimensions={0} | all-to-all | bytes 2621440 | tf_op jit(solution)/shard_map/all_to_all | solution.py:40
  172.5 1.0 reduce_sum.91
  173.5 4.3 %all-to-all-start.3 = ((bf16[8,16,1280]{2,1,0:T(8,128)(2,1)}), bf16[8,16,1280]{2,1,0:T(8,128)(2,1)S(1)}, u32[]{:S(2)}, u32[]{:S(2)}) async-start(bf16[8,16,1280]{2,1,0:T(8,128)(2,1)} %bitcast.165), calls=%async_computation.3 | async-start | bytes 655360 | tf_op jit(solution)/shard_map/all_to_all | solution.py:40
  178.4 19.5 %all-to-all-done.3 = bf16[8,16,1280]{2,1,0:T(8,128)(2,1)S(1)} async-done(((bf16[8,16,1280]{2,1,0:T(8,128)(2,1)}), bf16[8,16,1280]{2,1,0:T(8,128)(2,1)S(1)}, u32[]{:S(2)}, u32[]{:S(2)}) %all-to-all-start.3) | async-done | bytes 327712 | tf_op jit(solution)/shard_map/all_to_all | solution.py:40
  198.6 47.0 %all_to_all.37 = bf16[16,8,2688]{2,1,0:T(8,128)(2,1)S(1)} all-to-all(bf16[16,8,2688]{2,1,0:T(8,128)(2,1)S(1)} %broadcast_in_dim.49), channel_id=1, replica_groups=mesh['dp'=32,'expert'=16] {'expert'}, dimensions={0} | all-to-all | bytes 1376256 | tf_op jit(solution)/shard_map/all_to_all | solution.py:40
  245.6 1.4 shard_map.85
  247.2 10.9 %all_to_all.38 = bf16[32,2,1280]{2,1,0:T(2,128)(2,1)S(1)} all-to-all(bf16[32,2,1280]{2,1,0:T(2,128)(2,1)S(1)} %bitcast.168), channel_id=1, replica_groups={{0,1,2,3,4,5,6,7,8,9,10,11,12,13,14,15,256,257,258,259,260,261,262,263,..., dimensions={0} | all-to-all | bytes 327680 | tf_op jit(solution)/shard_map/all_to_all | solution.py:40
  258.2 0.7 broadcast_in_dim.52
  258.9 3.5 %all-to-all-start.6 = ((bf16[16,2,1280]{2,1,0:T(2,128)(2,1)}), bf16[16,2,1280]{2,1,0:T(2,128)(2,1)S(1)}, u32[]{:S(2)}, u32[]{:S(2)}) async-start(bf16[16,2,1280]{2,1,0:T(2,128)(2,1)} %broadcast_in_dim.52), calls=%async_computation.6 | async-start | bytes 163840 | tf_op jit(solution)/shard_map/all_to_all | solution.py:40
  262.4 1.3 convolution_convert_fusion
  263.7 1.3 fusion.2
  265.0 9.1 %all-to-all-done.6 = bf16[16,2,1280]{2,1,0:T(2,128)(2,1)S(1)} async-done(((bf16[16,2,1280]{2,1,0:T(2,128)(2,1)}), bf16[16,2,1280]{2,1,0:T(2,128)(2,1)S(1)}, u32[]{:S(2)}, u32[]{:S(2)}) %all-to-all-start.6) | async-done | bytes 81952 | tf_op jit(solution)/shard_map/all_to_all | solution.py:40
  274.1 0.6 convert_reduce_fusion
  (55 shorter events, 4.6 us)
Async XLA Ops:
  7.2 148.4 %copy-start = (bf16[2,1280,160]{1,2,0:T(8,128)(2,1)S(1)}, bf16[2,1280,160]{1,2,0:T(8,128)(2,1)}, u32[]{:S(2)}) copy-start(bf16[2,1280,160]{1,2,0:T(8,128)(2,1)} %param.8) | copy-start | bytes 2457604
  8.6 17.6 %all-to-all-start = ((bf16[16,2,1280]{2,1,0:T(2,128)(2,1)}), bf16[16,2,1280]{2,1,0:T(2,128)(2,1)S(1)}, u32[]{:S(2)}, u32[]{:S(2)}) async-start(bf16[16,2,1280]{2,1,0:T(2,128)(2,1)} %broadcast_in_dim.47), calls=%async_computation | async-start | bytes 163840 | tf_op jit(solution)/shard_map/all_to_all | solution.py:40
  18.8 135.4 %all-gather.2.cloned.1.call-start = ((), (), s32[]{:S(2)}) async-start(), calls=%async_computation.7 | async-start | bytes 1351680 | tf_op jit(solution)/shard_map/all_gather | solution.py:61
  155.6 2.5 copy-start.1
  155.6 1.4 copy-start.5
  158.1 1.1 copy-start.3
  173.5 24.4 %all-to-all-start.3 = ((bf16[8,16,1280]{2,1,0:T(8,128)(2,1)}), bf16[8,16,1280]{2,1,0:T(8,128)(2,1)S(1)}, u32[]{:S(2)}, u32[]{:S(2)}) async-start(bf16[8,16,1280]{2,1,0:T(8,128)(2,1)} %bitcast.165), calls=%async_computation.3 | async-start | bytes 655360 | tf_op jit(solution)/shard_map/all_to_all | solution.py:40
  245.6 16.8 %copy-start.2 = (bf16[2,16,8,1280]{3,2,1,0:T(8,128)(2,1)S(1)}, bf16[2,16,8,1280]{3,2,1,0:T(8,128)(2,1)}, u32[]{:S(2)}) copy-start(bf16[2,16,8,1280]{3,2,1,0:T(8,128)(2,1)} %copy-done.1) | copy-start | bytes 1966084
  247.1 16.7 %copy-start.4 = (bf16[2,256,160]{1,2,0:T(8,128)(2,1)S(1)}, bf16[2,256,160]{1,2,0:T(8,128)(2,1)}, u32[]{:S(2)}) copy-start(bf16[2,256,160]{1,2,0:T(8,128)(2,1)} %copy-done.3) | copy-start | bytes 491524
  258.9 15.2 %all-to-all-start.6 = ((bf16[16,2,1280]{2,1,0:T(2,128)(2,1)}), bf16[16,2,1280]{2,1,0:T(2,128)(2,1)S(1)}, u32[]{:S(2)}, u32[]{:S(2)}) async-start(bf16[16,2,1280]{2,1,0:T(2,128)(2,1)} %broadcast_in_dim.52), calls=%async_computation.6 | async-start | bytes 163840 | tf_op jit(solution)/shard_map/all_to_all | solution.py:40
Sparse Core Ops, SparseCore 0:
  45.5 108.6 all-gather.1

commit v10 on v9

--- a/solution.py
+++ b/solution.py
@@ -12,8 +12,10 @@
 BF16 = jnp.bfloat16
 
 
-def gelu_exact(value):
-    return jax.nn.gelu(value, approximate=False)
+def gelu_and_slope(value):
+    below = 0.5 * (1.0 + lax.erf(value * 0.5**0.5))
+    density = jnp.exp(-0.5 * value * value) * (1.0 / (2.0 * np.pi) ** 0.5)
+    return value * below, below + value * density
 
 
 def split3(value):
@@ -58,15 +60,20 @@
 
 
 def gather_dp(own):
-    whole = lax.all_gather(own, "dp", axis=0, tiled=True)
-    return whole.reshape(2, -1, 2 * own.shape[0], own.shape[1])
+    rows, d = own.shape[1:]
+    far = everywhere(own.reshape(2 * rows, d), "dp", dp_groups(1)).reshape(-1, 2, rows, d)
+    far = jnp.transpose(far, (1, 0, 2, 3)).reshape(2, -1, d)
+    return everywhere(far, "dp", dp_groups(0, 2))
 
 
 def reduce_dp(partial, rows):
     d = partial.shape[-1]
-    partial = jnp.transpose(partial.reshape(2, -1, 2, rows, d), (0, 2, 1, 3, 4)).reshape(4, -1, d)
-    total = jnp.sum(exchange(partial, "dp", dp_groups(0, 2)).astype(F32), axis=0).astype(BF16)
-    return jnp.sum(exchange(total.reshape(-1, rows, d), "dp", dp_groups(1)).astype(F32), axis=0)
+    taken = exchange(partial, "dp", dp_groups(0, 2))
+    (total,) = call(
+        functools.partial(add_square, rows), [((2 * partial.shape[2], d), BF16)], 2_000_000, taken
+    )
+    total = exchange(total.reshape(-1, 2 * rows, d), "dp", dp_groups(1))
+    return jnp.sum(total.astype(F32), axis=0)
 
 
 def dot(left, right, left_dim=1, right_dim=0):
@@ -151,42 +158,65 @@
     token_grad_ref[...] = token_grad.astype(BF16)
 
 
-def call(kernel, out_shape, *operands):
+def call(kernel, out_shape, flops, *operands):
     shapes = [jax.ShapeDtypeStruct(shape, dtype) for shape, dtype in out_shape]
+    size = sum(value.size * value.dtype.itemsize for value in list(operands) + shapes)
     return pl.pallas_call(
         kernel,
         out_shape=shapes,
         compiler_params=pltpu.CompilerParams(vmem_limit_bytes=32 * 1024 * 1024),
-        cost_estimate=pl.CostEstimate(flops=120_000_000, bytes_accessed=2_000_000, transcendentals=16384),
+        cost_estimate=pl.CostEstimate(flops=flops, bytes_accessed=size, transcendentals=16384),
     )(*operands)
 
 
-def expert_part(gathered, w_in, w_out, imgs):
-    slots, d, _ = w_in.shape
-    rows = slots * imgs
-    blocks = (gathered.shape[0], 2 * gathered.shape[1], rows, d)
-    halves = gathered.reshape(blocks[:2] + (2 * rows, d))
-    all_in = halves[:, :, :rows].reshape(-1, d)
-    all_out_grad = halves[:, :, rows:].reshape(-1, d)
-    row = lax.broadcasted_iota(jnp.int32, (slots, all_in.shape[0], 1), 1)
-    slot = lax.broadcasted_iota(jnp.int32, (slots, all_in.shape[0], 1), 0)
-    mine = row % slots == slot
-    preact = jnp.einsum("rd,sdh->srh", all_in, w_in, preferred_element_type=F32)
-    activated_wide, pullback = jax.vjp(gelu_exact, preact)
-    activated = jnp.where(mine, activated_wide, 0.0).astype(BF16)
-    slot_out = jnp.einsum("srh,shd->rd", activated, w_out, preferred_element_type=F32)
-    act_grad = jnp.einsum("rd,shd->srh", all_out_grad, w_out, preferred_element_type=F32)
-    preact_grad = jnp.where(mine, pullback(act_grad)[0], 0.0).astype(BF16)
-    slot_in_grad = jnp.einsum("srh,sdh->rd", preact_grad, w_in, preferred_element_type=F32)
-    w_out_grad = jnp.einsum(
-        "srh,rd->shd", activated, all_out_grad, preferred_element_type=F32
-    ).astype(BF16)
-    w_in_grad = jnp.einsum(
-        "rd,srh->sdh", all_in, preact_grad, preferred_element_type=F32
-    ).astype(BF16)
-    pair = [value.astype(BF16).reshape(blocks) for value in (slot_out, slot_in_grad)]
-    partial = jnp.concatenate(pair, axis=2).reshape(gathered.shape)
-    return partial, w_in_grad, w_out_grad
+def hidden(all_in, all_out_grad, w_in, w_out, own_slots):
+    shape = (all_in.shape[0], w_in.shape[0])
+    row = lax.broadcasted_iota(jnp.int32, shape, 0)
+    column = lax.broadcasted_iota(jnp.int32, shape, 1)
+    mine = row % own_slots == column // (shape[1] // own_slots)
+    activated, slope = gelu_and_slope(dot(all_in, w_in, 1, 1))
+    preact_grad = dot(all_out_grad, w_out, 1, 1) * slope
+    return (
+        jnp.where(mine, activated, 0.0).astype(BF16),
+        jnp.where(mine, preact_grad, 0.0).astype(BF16),
+    )
+
+
+def rows_of(gathered_ref, which):
+    return jnp.concatenate([gathered_ref[q, which] for q in range(gathered_ref.shape[0])], axis=0)
+
+
+def experts(
+    own_slots, gathered_ref, w_in_ref, w_out_ref, partial_ref, activated_ref, preact_grad_ref
+):
+    w_in, w_out = w_in_ref[...], w_out_ref[...]
+    activated, preact_grad = hidden(
+        rows_of(gathered_ref, 0), rows_of(gathered_ref, 1), w_in, w_out, own_slots
+    )
+    activated_ref[...] = activated
+    preact_grad_ref[...] = preact_grad
+    slot_out = dot(activated, w_out).astype(BF16)
+    slot_in_grad = dot(preact_grad, w_in).astype(BF16)
+    size = partial_ref.shape[2]
+    for q in range(partial_ref.shape[0]):
+        partial_ref[q, 0] = slot_out[q * size : (q + 1) * size]
+        partial_ref[q, 1] = slot_in_grad[q * size : (q + 1) * size]
+
+
+def weight_grads(gathered_ref, activated_ref, preact_grad_ref, w_in_grad_ref, w_out_grad_ref):
+    all_in, all_out_grad = rows_of(gathered_ref, 0), rows_of(gathered_ref, 1)
+    w_in_grad_ref[...] = dot(preact_grad_ref[...], all_in, 0, 0).astype(BF16)
+    w_out_grad_ref[...] = dot(activated_ref[...], all_out_grad, 0, 0).astype(BF16)
+
+
+def add_square(rows, taken_ref, total_ref):
+    total = taken_ref[0].astype(F32)
+    for q in range(1, taken_ref.shape[0]):
+        total += taken_ref[q].astype(F32)
+    pieces = [
+        total[which, at : at + rows] for at in range(0, total.shape[1], rows) for which in range(2)
+    ]
+    total_ref[...] = jnp.concatenate(pieces, axis=0).astype(BF16)
 
 
 def on_device(tokens, cotangent, slot_params, w_in, w_out):
@@ -202,7 +232,7 @@
     sent, logits, combine = call(
         functools.partial(route, imgs, own_slots),
         [((peers * rows, 2 * d + 128), BF16), (pairs, F32), (pairs, F32)],
-        params, both,
+        100_000_000, params, both,
     )
     taken = exchange(sent.reshape(peers, rows, 2 * d + 128), "expert")
 
@@ -213,11 +243,22 @@
     total = jnp.sum(masses * scale, axis=0)
     slot_in_wide = jnp.sum(taken[:, :, :d].astype(F32) * scale, axis=0) / total
     slot_out_grad = jnp.sum(taken[:, :, d + 128 :].astype(F32), axis=0)
-    own = jnp.concatenate([slot_in_wide.astype(BF16), slot_out_grad.astype(BF16)], axis=0)
+    own = jnp.stack([slot_in_wide.astype(BF16), slot_out_grad.astype(BF16)])
 
     gathered = gather_dp(own)
-    partial, w_in_grad, w_out_grad = expert_part(gathered, w_in, w_out, imgs)
-    owned_b = reduce_dp(partial, 2 * rows).astype(BF16).reshape(2, rows, d)
+    flat_in, flat_out = jnp.swapaxes(w_in, 1, 2).reshape(-1, d), w_out.reshape(-1, d)
+    units = (gathered.shape[0] * gathered.shape[2], flat_in.shape[0])
+    partial, activated, preact_grad = call(
+        functools.partial(experts, own_slots),
+        [(gathered.shape, BF16), (units, BF16), (units, BF16)],
+        1_000_000_000, gathered, flat_in, flat_out,
+    )
+    w_in_grad, w_out_grad = call(
+        weight_grads, [(flat_in.shape, BF16)] * 2, 600_000_000, gathered, activated, preact_grad
+    )
+    w_in_grad = jnp.swapaxes(w_in_grad.reshape(own_slots, -1, d), 1, 2)
+    w_out_grad = w_out_grad.reshape(w_out.shape)
+    owned_b = reduce_dp(partial, rows).astype(BF16).reshape(2, rows, d)
 
     col = jnp.sum(owned_b[1].astype(F32) * slot_in_wide, axis=1, keepdims=True)
     stats = jnp.concatenate(
@@ -227,7 +268,7 @@
     token_grad, share_grad = call(
         functools.partial(finish, imgs, own_slots),
         [(both.shape[1:], BF16), ((slots, d), BF16)],
-        back.reshape(peers * rows, 2 * d + 128), logits, combine, params, both,
+        100_000_000, back.reshape(peers * rows, 2 * d + 128), logits, combine, params, both,
     )
     token_grad = token_grad.reshape(tokens.shape)
 

time: 282 us -> 188 us (0.67)
  waiting for transfers between devices: 144 us -> 32.7 us
  blocking collectives: 87.5 us -> 114 us
  between operations: 14.3 us -> 0.77 us
  starting transfers between devices: 18 us -> 26.4 us
  matrix products: 5.11 us -> 0 us
  Pallas kernels: 2.25 us -> 6.3 us
    all_gather x1 -> x0, waiting for transfers between devices: 109 us -> none  [gather_dp(): whole = lax.all_gather(own, 'dp', axis=0, tiled=True)]
    all_to_all x4 -> x6, blocking collectives: 87.5 us -> 114 us  [exchange(): lax.all_to_all(value, axis, split_axis=0, concat_axis=0, axis_index_group...]
    all_to_all x3, starting transfers between devices: 18 us -> 26.4 us  [exchange(): lax.all_to_all(value, axis, split_axis=0, concat_axis=0, axis_index_group...]
    dot_general x5 -> x0, matrix products: 4.7 us -> none  [the longest x1 1.28 us: expert_part(): jnp.einsum('srh,rd->shd', activated, all_out_grad, preferred_element_type...]
    pallas_call x2 -> x5, Pallas kernels: 2.25 us -> 6.3 us  [call(): pl.pallas_call(kernel, out_shape=shapes, compiler_params=pltpu.CompilerPa...]
  transfers between devices with their start and end apart: 4 -> 3, of which waited for: 4 -> 3; matrix products, arithmetic and copies ran while one was open for 1% -> 1% of each run, Pallas kernels for 0% -> 1%
where the time goes in v10:
time: 188 us; the launch traced here: 187 us
  blocking collectives  114 us (61%)
  waiting for transfers between devices  32.7 us (17%)
  starting transfers between devices  26.4 us (14%)
  Pallas kernels  6.3 us (3%)
  local copies, waits for them, and re-layouts  4.16 us (2%)
  other arithmetic  2.67 us (1%)
    all_to_all x6, blocking collectives, exchange(): lax.all_to_all(value, axis, split_axis=0, concat_axis=0, axis_index_group...  114 us
    all_to_all x3, waiting for transfers between devices, exchange(): lax.all_to_all(value, axis, split_axis=0, concat_axis=0, axis_index_group...  32.7 us
    all_to_all x3, starting transfers between devices, exchange(): lax.all_to_all(value, axis, split_axis=0, concat_axis=0, axis_index_group...  26.4 us
    pallas_call x5, Pallas kernels, call(): pl.pallas_call(kernel, out_shape=shapes, compiler_params=pltpu.CompilerPa...  6.3 us
  transfers between devices with their start and end apart: 3, of which 3 were waited for; matrix products, arithmetic and copies ran while one was open for 1% of the time, Pallas kernels for 1%

profile of v10, /device:TPU:1, one launch (start us, length us, event | category | flops | bytes accessed | tf_op | source)
XLA Modules:
  0.0 187.0 jit_solution(6448954455083064409)
XLA Ops:
  0.6 1.4 broadcast_in_dim.20
  2.0 10.2 %all-to-all-start = ((bf16[16,2,1280]{2,1,0:T(2,128)(2,1)}), bf16[16,2,1280]{2,1,0:T(2,128)(2,1)S(1)}, u32[]{:S(2)}, u32[]{:S(2)}) async-start(bf16[16,2,1280]{2,1,0:T(2,128)(2,1)} %broadcast_in_dim.20), calls=%async_computation | async-start | bytes 163840 | tf_op jit(solution)/shard_map/all_to_all | solution.py:42
  12.2 1.0 pad_maximum_fusion.both_ref
  13.2 6.4 %all-to-all-done = bf16[16,2,1280]{2,1,0:T(2,128)(2,1)S(1)} async-done(((bf16[16,2,1280]{2,1,0:T(2,128)(2,1)}), bf16[16,2,1280]{2,1,0:T(2,128)(2,1)S(1)}, u32[]{:S(2)}, u32[]{:S(2)}) %all-to-all-start) | async-done | bytes 81952 | tf_op jit(solution)/shard_map/all_to_all | solution.py:42
  19.7 0.9 shard_map.84
  20.5 16.5 %all_to_all.45 = bf16[16,8,2688]{2,1,0:T(8,128)(2,1)S(1)} all-to-all(bf16[16,8,2688]{2,1,0:T(8,128)(2,1)S(1)} %bitcast.55), channel_id=1, replica_groups=mesh['dp'=32,'expert'=16] {'expert'}, dimensions={0} | all-to-all | bytes 1376256 | tf_op jit(solution)/shard_map/all_to_all | solution.py:42
  37.1 0.2 copy.136
  38.0 0.2 fusion.2
  38.5 33.7 %all_to_all.46 = bf16[8,16,1280]{2,1,0:T(8,128)(2,1)S(1)} all-to-all(bf16[8,16,1280]{2,1,0:T(8,128)(2,1)S(1)} %broadcast_in_dim.22), channel_id=1, replica_groups={{0,32,64,96,128,160,192,224},{16,48,80,112,144,176,208,240},{256,288,32..., dimensions={0} | all-to-all | bytes 655360 | tf_op jit(solution)/shard_map/all_to_all | solution.py:42
  72.4 14.8 %all_to_all.47.gathered_ref = bf16[4,2,64,1280]{3,2,1,0:T(8,128)(2,1)S(1)} all-to-all(bf16[4,2,64,1280]{3,2,1,0:T(8,128)(2,1)S(1)} %broadcast_in_dim.48), channel_id=1, replica_groups={{0,16,256,272},{32,48,288,304},{64,80,320,336},{96,112,352,368},{128,14..., dimensions={0} | all-to-all | bytes 2621440 | tf_op jit(solution)/shard_map/all_to_all | solution.py:42
  87.2 1.5 shard_map.85
  88.7 13.2 %all_to_all.48.taken_ref = bf16[4,2,64,1280]{3,2,1,0:T(8,128)(2,1)S(1)} all-to-all(bf16[4,2,64,1280]{3,2,1,0:T(8,128)(2,1)S(1)} %get-tuple-element.15), channel_id=1, replica_groups={{0,16,256,272},{32,48,288,304},{64,80,320,336},{96,112,352,368},{128,14..., dimensions={0} | all-to-all | bytes 2621440 | tf_op jit(solution)/shard_map/all_to_all | solution.py:42
  101.9 0.9 shard_map.86
  102.8 12.7 %all-to-all-start.5 = ((bf16[8,16,1280]{2,1,0:T(8,128)(2,1)}), bf16[8,16,1280]{2,1,0:T(8,128)(2,1)S(1)}, u32[]{:S(2)}, u32[]{:S(2)}) async-start(bf16[8,16,1280]{2,1,0:T(8,128)(2,1)} %bitcast.14), calls=%async_computation.5 | async-start | bytes 655360 | tf_op jit(solution)/shard_map/all_to_all | solution.py:42
  116.1 16.2 %all-to-all-done.5 = bf16[8,16,1280]{2,1,0:T(8,128)(2,1)S(1)} async-done(((bf16[8,16,1280]{2,1,0:T(8,128)(2,1)}), bf16[8,16,1280]{2,1,0:T(8,128)(2,1)S(1)}, u32[]{:S(2)}, u32[]{:S(2)}) %all-to-all-start.5) | async-done | bytes 327712 | tf_op jit(solution)/shard_map/all_to_all | solution.py:42
  132.3 0.2 multiply_reduce_fusion.1
  133.0 24.9 %all_to_all.49 = bf16[16,8,2688]{2,1,0:T(8,128)(2,1)S(1)} all-to-all(bf16[16,8,2688]{2,1,0:T(8,128)(2,1)S(1)} %broadcast_in_dim.50), channel_id=1, replica_groups=mesh['dp'=32,'expert'=16] {'expert'}, dimensions={0} | all-to-all | bytes 1376256 | tf_op jit(solution)/shard_map/all_to_all | solution.py:42
  157.9 1.4 shard_map.87
  159.5 10.9 %all_to_all.50 = bf16[32,2,1280]{2,1,0:T(2,128)(2,1)S(1)} all-to-all(bf16[32,2,1280]{2,1,0:T(2,128)(2,1)S(1)} %bitcast.59), channel_id=1, replica_groups={{0,1,2,3,4,5,6,7,8,9,10,11,12,13,14,15,256,257,258,259,260,261,262,263,..., dimensions={0} | all-to-all | bytes 327680 | tf_op jit(solution)/shard_map/all_to_all | solution.py:42
  170.5 0.7 broadcast_in_dim.53
  171.2 3.5 %all-to-all-start.8 = ((bf16[16,2,1280]{2,1,0:T(2,128)(2,1)}), bf16[16,2,1280]{2,1,0:T(2,128)(2,1)S(1)}, u32[]{:S(2)}, u32[]{:S(2)}) async-start(bf16[16,2,1280]{2,1,0:T(2,128)(2,1)} %broadcast_in_dim.53), calls=%async_computation.8 | async-start | bytes 163840 | tf_op jit(solution)/shard_map/all_to_all | solution.py:42
  174.7 1.6 shard_map.88
  176.3 10.1 %all-to-all-done.8 = bf16[16,2,1280]{2,1,0:T(2,128)(2,1)S(1)} async-done(((bf16[16,2,1280]{2,1,0:T(2,128)(2,1)}), bf16[16,2,1280]{2,1,0:T(2,128)(2,1)S(1)}, u32[]{:S(2)}, u32[]{:S(2)}) %all-to-all-start.8) | async-done | bytes 81952 | tf_op jit(solution)/shard_map/all_to_all | solution.py:42
  186.4 0.6 convert_reduce_fusion
  (40 shorter events, 2.5 us)
Async XLA Ops:
  2.0 17.6 %all-to-all-start = ((bf16[16,2,1280]{2,1,0:T(2,128)(2,1)}), bf16[16,2,1280]{2,1,0:T(2,128)(2,1)S(1)}, u32[]{:S(2)}, u32[]{:S(2)}) async-start(bf16[16,2,1280]{2,1,0:T(2,128)(2,1)} %broadcast_in_dim.20), calls=%async_computation | async-start | bytes 163840 | tf_op jit(solution)/shard_map/all_to_all | solution.py:42
  72.4 14.8 %copy-start = (bf16[2,1280,160]{1,2,0:T(8,128)(2,1)S(1)}, bf16[2,1280,160]{1,2,0:T(8,128)(2,1)}, u32[]{:S(2)}) copy-start(bf16[2,1280,160]{1,2,0:T(8,128)(2,1)} %param.8) | copy-start | bytes 2457604
  72.4 14.8 %copy-start.1 = (bf16[2,160,1280]{2,1,0:T(8,128)(2,1)S(1)}, bf16[2,160,1280]{2,1,0:T(8,128)(2,1)}, u32[]{:S(2)}) copy-start(bf16[2,160,1280]{2,1,0:T(8,128)(2,1)} %param.9) | copy-start | bytes 2457604
  102.8 29.5 %all-to-all-start.5 = ((bf16[8,16,1280]{2,1,0:T(8,128)(2,1)}), bf16[8,16,1280]{2,1,0:T(8,128)(2,1)S(1)}, u32[]{:S(2)}, u32[]{:S(2)}) async-start(bf16[8,16,1280]{2,1,0:T(8,128)(2,1)} %bitcast.14), calls=%async_computation.5 | async-start | bytes 655360 | tf_op jit(solution)/shard_map/all_to_all | solution.py:42
  171.2 15.2 %all-to-all-start.8 = ((bf16[16,2,1280]{2,1,0:T(2,128)(2,1)}), bf16[16,2,1280]{2,1,0:T(2,128)(2,1)S(1)}, u32[]{:S(2)}, u32[]{:S(2)}) async-start(bf16[16,2,1280]{2,1,0:T(2,128)(2,1)} %broadcast_in_dim.53), calls=%async_computation.8 | async-start | bytes 163840 | tf_op jit(solution)/shard_map/all_to_all | solution.py:42

commit v11 on v10

--- a/solution.py
+++ b/solution.py
@@ -18,18 +18,6 @@
     return value * below, below + value * density
 
 
-def split3(value):
-    high = lax.reduce_precision(value, 8, 7)
-    middle = lax.reduce_precision(value - high, 8, 7)
-    low = value - high - middle
-    return [high.astype(BF16), middle.astype(BF16), low.astype(BF16)]
-
-
-def join3(terms):
-    wide = terms.astype(F32)
-    return wide[..., 0:1] + wide[..., 1:2] + wide[..., 2:3]
-
-
 def groups_of(axis, sizes, inner):
     shape = [lax.axis_size(axis) // sizes[0] // sizes[1], sizes[0], sizes[1]]
     ids = np.arange(lax.axis_size(axis)).reshape(shape)
@@ -60,8 +48,8 @@
 
 
 def gather_dp(own):
-    rows, d = own.shape[1:]
-    far = everywhere(own.reshape(2 * rows, d), "dp", dp_groups(1)).reshape(-1, 2, rows, d)
+    rows, d = own.shape[0] // 2, own.shape[1]
+    far = everywhere(own, "dp", dp_groups(1)).reshape(-1, 2, rows, d)
     far = jnp.transpose(far, (1, 0, 2, 3)).reshape(2, -1, d)
     return everywhere(far, "dp", dp_groups(0, 2))
 
@@ -72,8 +60,7 @@
     (total,) = call(
         functools.partial(add_square, rows), [((2 * partial.shape[2], d), BF16)], 2_000_000, taken
     )
-    total = exchange(total.reshape(-1, 2 * rows, d), "dp", dp_groups(1))
-    return jnp.sum(total.astype(F32), axis=0)
+    return exchange(total.reshape(-1, 2 * rows, d), "dp", dp_groups(1))
 
 
 def dot(left, right, left_dim=1, right_dim=0):
@@ -105,7 +92,7 @@
         for term in (high, middle, value - high - middle):
             block = jnp.where(lane == at, term, block)
             at += 1
-    return block.astype(BF16)
+    return block
 
 
 def column_of(block, at):
@@ -114,11 +101,21 @@
     return jnp.sum(jnp.where(inside, block, 0.0), axis=1, keepdims=True)
 
 
-def route(imgs, own_slots, params_ref, both_ref, sent_ref, logits_ref, combine_ref):
-    tokens, cotangent = both_ref[0], both_ref[1]
+def route(
+    imgs, own_slots, params_ref, tok_ref, cot_ref, sent_ref, logits_ref, combine_ref, both_ref, sem
+):
+    copies = [
+        pltpu.make_async_copy(source, both_ref.at[at], sem.at[at])
+        for at, source in enumerate((tok_ref, cot_ref))
+    ]
+    for copy in copies:
+        copy.start()
     slots, d = params_ref.shape
     rows, columns = logits_ref.shape
     spread = dot(slot_rows(rows, slots, imgs, own_slots), params_ref[...]).astype(BF16)
+    for copy in copies:
+        copy.wait()
+    tokens, cotangent = both_ref[0], both_ref[1]
     logits = dot(spread, tokens, 1, 1)
     mine = own_image(rows, columns, imgs, own_slots, columns // imgs)
     logits = jnp.where(mine, logits, jnp.finfo(F32).min)
@@ -130,8 +127,38 @@
     weight = jnp.exp(logits - peak)
     mass = jnp.sum(weight, axis=1, keepdims=True)
     sent_ref[:, :d] = dot(weight.astype(BF16), tokens).astype(BF16)
-    sent_ref[:, d : d + 128] = lanes_of([peak, mass], rows)
+    sent_ref[:, d : d + 128] = lanes_of([peak, mass], rows).astype(BF16)
     sent_ref[:, d + 128 :] = dot(combine.astype(BF16), cotangent).astype(BF16)
+
+
+def collect(peers, taken_ref, own_ref, wide_ref, scalars_ref):
+    rows, d = wide_ref.shape
+    stats = taken_ref[:, d : d + 128].astype(F32)
+    peaks = column_of(stats, 0).reshape(peers, rows, 1)
+    masses = column_of(stats, 1).reshape(peers, rows, 1)
+    top = jnp.max(peaks, axis=0)
+    scale = jnp.exp(peaks - top[None])
+    total = jnp.sum(masses * scale, axis=0)
+    part_in = taken_ref[:, :d].astype(F32).reshape(peers, rows, d)
+    slot_in = jnp.sum(part_in * scale, axis=0) / total
+    slot_out_grad = jnp.sum(taken_ref[:, d + 128 :].astype(F32).reshape(peers, rows, d), axis=0)
+    own_ref[...] = jnp.concatenate([slot_in, slot_out_grad], axis=0).astype(BF16)
+    wide_ref[...] = slot_in
+    lane = lax.broadcasted_iota(jnp.int32, scalars_ref.shape, 1)
+    scalars_ref[...] = jnp.where(lane == 0, top, total)
+
+
+def deliver(far, peers, taken_ref, wide_ref, scalars_ref, back_ref):
+    rows, d = wide_ref.shape
+    owned = jnp.sum(taken_ref[...].astype(F32).reshape(far, 2 * rows, d), axis=0)
+    owned = owned.astype(BF16).astype(F32)
+    slot_out, slot_in_grad = owned[:rows], owned[rows:]
+    col = jnp.sum(slot_in_grad * wide_ref[...], axis=1, keepdims=True)
+    top, total = scalars_ref[:, 0:1], scalars_ref[:, 1:2]
+    stats = lanes_of([top, total, col], rows)
+    for at, value in ((0, slot_out), (d, slot_in_grad), (2 * d, stats)):
+        copies = jnp.concatenate([value] * peers, axis=0).astype(BF16)
+        back_ref[:, at : at + value.shape[1]] = copies
 
 
 def finish(
@@ -158,7 +185,7 @@
     token_grad_ref[...] = token_grad.astype(BF16)
 
 
-def call(kernel, out_shape, flops, *operands):
+def call(kernel, out_shape, flops, *operands, **options):
     shapes = [jax.ShapeDtypeStruct(shape, dtype) for shape, dtype in out_shape]
     size = sum(value.size * value.dtype.itemsize for value in list(operands) + shapes)
     return pl.pallas_call(
@@ -166,6 +193,7 @@
         out_shape=shapes,
         compiler_params=pltpu.CompilerParams(vmem_limit_bytes=32 * 1024 * 1024),
         cost_estimate=pl.CostEstimate(flops=flops, bytes_accessed=size, transcendentals=16384),
+        **options,
     )(*operands)
 
 
@@ -227,23 +255,22 @@
     rows = own_slots * imgs
 
     params = everywhere(slot_params.T, "expert").reshape(slots, d)
-    both = jnp.stack([tokens.reshape(-1, d), cotangent.reshape(-1, d)])
     pairs = (peers * rows, imgs * share)
-    sent, logits, combine = call(
+    wide = 2 * d + 128
+    flat = (imgs * share, d)
+    sent, logits, combine, both = call(
         functools.partial(route, imgs, own_slots),
-        [((peers * rows, 2 * d + 128), BF16), (pairs, F32), (pairs, F32)],
-        100_000_000, params, both,
-    )
-    taken = exchange(sent.reshape(peers, rows, 2 * d + 128), "expert")
-
-    peaks = join3(taken[:, :, d : d + 3])
-    masses = join3(taken[:, :, d + 3 : d + 6])
-    top = jnp.max(peaks, axis=0)
-    scale = jnp.exp(peaks - top[None])
-    total = jnp.sum(masses * scale, axis=0)
-    slot_in_wide = jnp.sum(taken[:, :, :d].astype(F32) * scale, axis=0) / total
-    slot_out_grad = jnp.sum(taken[:, :, d + 128 :].astype(F32), axis=0)
-    own = jnp.stack([slot_in_wide.astype(BF16), slot_out_grad.astype(BF16)])
+        [((peers * rows, wide), BF16), (pairs, F32), (pairs, F32), ((2,) + flat, BF16)],
+        100_000_000, params, tokens.reshape(flat), cotangent.reshape(flat),
+        in_specs=[pl.BlockSpec(memory_space=space) for space in (pltpu.VMEM, pltpu.HBM, pltpu.HBM)],
+        scratch_shapes=[pltpu.SemaphoreType.DMA((2,))],
+    )
+    taken = exchange(sent.reshape(peers, rows, wide), "expert")
+    own, slot_in_wide, scalars = call(
+        functools.partial(collect, peers),
+        [((2 * rows, d), BF16), ((rows, d), F32), ((rows, 128), F32)],
+        1_000_000, taken.reshape(peers * rows, wide),
+    )
 
     gathered = gather_dp(own)
     flat_in, flat_out = jnp.swapaxes(w_in, 1, 2).reshape(-1, d), w_out.reshape(-1, d)
@@ -258,17 +285,17 @@
     )
     w_in_grad = jnp.swapaxes(w_in_grad.reshape(own_slots, -1, d), 1, 2)
     w_out_grad = w_out_grad.reshape(w_out.shape)
-    owned_b = reduce_dp(partial, rows).astype(BF16).reshape(2, rows, d)
-
-    col = jnp.sum(owned_b[1].astype(F32) * slot_in_wide, axis=1, keepdims=True)
-    stats = jnp.concatenate(
-        split3(top) + split3(total) + split3(col) + [jnp.zeros((rows, 119), BF16)], axis=1
-    )
-    back = everywhere(jnp.concatenate([owned_b[0], owned_b[1], stats], axis=1), "expert")
+    terms = reduce_dp(partial, rows)
+    (back,) = call(
+        functools.partial(deliver, terms.shape[0], peers), [((peers * rows, wide), BF16)],
+        1_000_000, terms.reshape(-1, d), slot_in_wide, scalars,
+    )
+    back = exchange(back.reshape(peers, rows, wide), "expert")
+
     token_grad, share_grad = call(
         functools.partial(finish, imgs, own_slots),
         [(both.shape[1:], BF16), ((slots, d), BF16)],
-        100_000_000, back.reshape(peers * rows, 2 * d + 128), logits, combine, params, both,
+        100_000_000, back.reshape(peers * rows, wide), logits, combine, params, both,
     )
     token_grad = token_grad.reshape(tokens.shape)
 

time: 188 us -> 187 us (level)
  blocking collectives: 114 us -> 161 us
  starting transfers between devices: 26.4 us -> 3.5 us
  waiting for transfers between devices: 32.7 us -> 10.1 us
    all_to_all x6 -> x8, blocking collectives: 114 us -> 161 us  [exchange(): lax.all_to_all(value, axis, split_axis=0, concat_axis=0, axis_index_group...]
    all_to_all x3 -> x1, starting transfers between devices: 26.4 us -> 3.5 us  [exchange(): lax.all_to_all(value, axis, split_axis=0, concat_axis=0, axis_index_group...]
    all_to_all x3 -> x1, waiting for transfers between devices: 32.7 us -> 10.1 us  [exchange(): lax.all_to_all(value, axis, split_axis=0, concat_axis=0, axis_index_group...]
    pallas_call x5 -> x7, Pallas kernels: 6.3 us -> 6.47 us  [call(): pl.pallas_call(kernel, out_shape=shapes, compiler_params=pltpu.CompilerPa...]
  transfers between devices with their start and end apart: 3 -> 1, of which waited for: 3 -> 1; matrix products, arithmetic and copies ran while one was open for 1% -> 0% of each run, Pallas kernels for 1% -> 1%
where the time goes in v11:
time: 187 us; the launch traced here: 186 us
  blocking collectives  161 us (86%)
  waiting for transfers between devices  10.1 us (5%)
  Pallas kernels  6.47 us (3%)
  local copies, waits for them, and re-layouts  3.54 us (2%)
  starting transfers between devices  3.5 us (2%)
    all_to_all x8, blocking collectives, exchange(): lax.all_to_all(value, axis, split_axis=0, concat_axis=0, axis_index_group...  161 us
    all_to_all x1, waiting for transfers between devices, exchange(): lax.all_to_all(value, axis, split_axis=0, concat_axis=0, axis_index_group...  10.1 us
    pallas_call x7, Pallas kernels, call(): pl.pallas_call(kernel, out_shape=shapes, compiler_params=pltpu.CompilerPa...  6.47 us
  transfers between devices with their start and end apart: 1, of which 1 were waited for; matrix products, arithmetic and copies ran while one was open for 0% of the time, Pallas kernels for 1%

profile of v11, /device:TPU:1, one launch (start us, length us, event | category | flops | bytes accessed | tf_op | source)
XLA Modules:
  0.0 186.3 jit_solution(12205340614955914483)
XLA Ops:
  0.6 0.7 broadcast_in_dim.14
  1.4 16.7 %all_to_all.45 = bf16[16,2,1280]{2,1,0:T(2,128)(2,1)S(1)} all-to-all(bf16[16,2,1280]{2,1,0:T(2,128)(2,1)S(1)} %broadcast_in_dim.14), channel_id=1, replica_groups=mesh['dp'=32,'expert'=16] {'expert'}, dimensions={0} | all-to-all | bytes 163840 | tf_op jit(solution)/shard_map/all_to_all | solution.py:30
  18.1 0.9 copy-done
  19.1 0.9 copy-done.1
  20.0 1.4 shard_map.84
  21.3 16.5 %all_to_all.46 = bf16[16,8,2688]{2,1,0:T(8,128)(2,1)S(1)} all-to-all(bf16[16,8,2688]{2,1,0:T(8,128)(2,1)S(1)} %bitcast.32), channel_id=1, replica_groups=mesh['dp'=32,'expert'=16] {'expert'}, dimensions={0} | all-to-all | bytes 1376256 | tf_op jit(solution)/shard_map/all_to_all | solution.py:30
  37.9 0.2 shard_map.85
  38.1 34.4 %all_to_all.47 = bf16[8,16,1280]{2,1,0:T(8,128)(2,1)S(1)} all-to-all(bf16[8,16,1280]{2,1,0:T(8,128)(2,1)S(1)} %broadcast_in_dim.15), channel_id=1, replica_groups={{0,32,64,96,128,160,192,224},{16,48,80,112,144,176,208,240},{256,288,32..., dimensions={0} | all-to-all | bytes 655360 | tf_op jit(solution)/shard_map/all_to_all | solution.py:30
  72.7 14.8 %all_to_all.48.gathered_ref = bf16[4,2,64,1280]{3,2,1,0:T(8,128)(2,1)S(1)} all-to-all(bf16[4,2,64,1280]{3,2,1,0:T(8,128)(2,1)S(1)} %broadcast_in_dim.17), channel_id=1, replica_groups={{0,16,256,272},{32,48,288,304},{64,80,320,336},{96,112,352,368},{128,14..., dimensions={0} | all-to-all | bytes 2621440 | tf_op jit(solution)/shard_map/all_to_all | solution.py:30
  87.5 1.5 shard_map.86
  89.0 13.2 %all_to_all.49.taken_ref = bf16[4,2,64,1280]{3,2,1,0:T(8,128)(2,1)S(1)} all-to-all(bf16[4,2,64,1280]{3,2,1,0:T(8,128)(2,1)S(1)} %get-tuple-element.20), channel_id=1, replica_groups={{0,16,256,272},{32,48,288,304},{64,80,320,336},{96,112,352,368},{128,14..., dimensions={0} | all-to-all | bytes 2621440 | tf_op jit(solution)/shard_map/all_to_all | solution.py:30
  102.2 0.2 shard_map.87
  102.4 30.6 %all_to_all.50 = bf16[8,16,1280]{2,1,0:T(8,128)(2,1)S(1)} all-to-all(bf16[8,16,1280]{2,1,0:T(8,128)(2,1)S(1)} %bitcast.31), channel_id=1, replica_groups={{0,32,64,96,128,160,192,224},{16,48,80,112,144,176,208,240},{256,288,32..., dimensions={0} | all-to-all | bytes 655360 | tf_op jit(solution)/shard_map/all_to_all | solution.py:30
  133.0 0.1 shard_map.88
  133.2 23.9 %all_to_all.51 = bf16[16,8,2688]{2,1,0:T(8,128)(2,1)S(1)} all-to-all(bf16[16,8,2688]{2,1,0:T(8,128)(2,1)S(1)} %bitcast.29), channel_id=1, replica_groups=mesh['dp'=32,'expert'=16] {'expert'}, dimensions={0} | all-to-all | bytes 1376256 | tf_op jit(solution)/shard_map/all_to_all | solution.py:30
  157.1 1.4 shard_map.89
  158.6 0.1 broadcast_in_dim.37
  158.7 10.9 %all_to_all.52 = bf16[32,2,1280]{2,1,0:T(2,128)(2,1)S(1)} all-to-all(bf16[32,2,1280]{2,1,0:T(2,128)(2,1)S(1)} %bitcast.37), channel_id=1, replica_groups={{0,1,2,3,4,5,6,7,8,9,10,11,12,13,14,15,256,257,258,259,260,261,262,263,..., dimensions={0} | all-to-all | bytes 327680 | tf_op jit(solution)/shard_map/all_to_all | solution.py:30
  169.6 0.2 reduce_sum.21
  169.7 0.7 broadcast_in_dim.38
  170.4 3.5 %all-to-all-start.8 = ((bf16[16,2,1280]{2,1,0:T(2,128)(2,1)}), bf16[16,2,1280]{2,1,0:T(2,128)(2,1)S(1)}, u32[]{:S(2)}, u32[]{:S(2)}) async-start(bf16[16,2,1280]{2,1,0:T(2,128)(2,1)} %broadcast_in_dim.38), calls=%async_computation.8 | async-start | bytes 163840 | tf_op jit(solution)/shard_map/all_to_all | solution.py:30
  173.9 1.6 shard_map.90
  175.5 10.1 %all-to-all-done.8 = bf16[16,2,1280]{2,1,0:T(2,128)(2,1)S(1)} async-done(((bf16[16,2,1280]{2,1,0:T(2,128)(2,1)}), bf16[16,2,1280]{2,1,0:T(2,128)(2,1)S(1)}, u32[]{:S(2)}, u32[]{:S(2)}) %all-to-all-start.8) | async-done | bytes 81952 | tf_op jit(solution)/shard_map/all_to_all | solution.py:30
  185.6 0.6 convert_reduce_fusion
  (11 shorter events, 0.2 us)
Async XLA Ops:
  18.1 0.9 copy-start
  19.1 0.9 copy-start.1
  72.7 14.8 %copy-start.2 = (bf16[2,1280,160]{1,2,0:T(8,128)(2,1)S(1)}, bf16[2,1280,160]{1,2,0:T(8,128)(2,1)}, u32[]{:S(2)}) copy-start(bf16[2,1280,160]{1,2,0:T(8,128)(2,1)} %param.8) | copy-start | bytes 2457604
  72.7 14.8 %copy-start.3 = (bf16[2,160,1280]{2,1,0:T(8,128)(2,1)S(1)}, bf16[2,160,1280]{2,1,0:T(8,128)(2,1)}, u32[]{:S(2)}) copy-start(bf16[2,160,1280]{2,1,0:T(8,128)(2,1)} %param.9) | copy-start | bytes 2457604
  170.4 15.2 %all-to-all-start.8 = ((bf16[16,2,1280]{2,1,0:T(2,128)(2,1)}), bf16[16,2,1280]{2,1,0:T(2,128)(2,1)S(1)}, u32[]{:S(2)}, u32[]{:S(2)}) async-start(bf16[16,2,1280]{2,1,0:T(2,128)(2,1)} %broadcast_in_dim.38), calls=%async_computation.8 | async-start | bytes 163840 | tf_op jit(solution)/shard_map/all_to_all | solution.py:30

commit v12 on v11

--- a/solution.py
+++ b/solution.py
@@ -41,6 +41,10 @@
     return groups_of("dp", (lax.axis_size("dp") // 4, 2), inner)
 
 
+def expert_groups(*inner):
+    return groups_of("expert", (2, 2), inner)
+
+
 def plane_groups():
     peers, depth = lax.axis_size("expert"), lax.axis_size("dp") // 2
     ids = np.arange(2 * depth * peers).reshape(2, depth, peers)
@@ -75,10 +79,14 @@
     return (row // own_slots) % imgs == column // share
 
 
-def slot_rows(rows, slots, imgs, own_slots):
+def slot_rows(rows, slots, imgs, own_slots, core_first=False):
     row = lax.broadcasted_iota(jnp.int32, (rows, slots), 0)
     column = lax.broadcasted_iota(jnp.int32, (rows, slots), 1)
-    slot = (row // (imgs * own_slots)) * own_slots + row % own_slots
+    expert = row // (imgs * own_slots)
+    if core_first:
+        half = slots // own_slots // 2
+        expert = (expert % half) * 2 + expert // half
+    slot = expert * own_slots + row % own_slots
     return jnp.where(slot == column, 1.0, 0.0).astype(BF16)
 
 
@@ -101,21 +109,11 @@
     return jnp.sum(jnp.where(inside, block, 0.0), axis=1, keepdims=True)
 
 
-def route(
-    imgs, own_slots, params_ref, tok_ref, cot_ref, sent_ref, logits_ref, combine_ref, both_ref, sem
-):
-    copies = [
-        pltpu.make_async_copy(source, both_ref.at[at], sem.at[at])
-        for at, source in enumerate((tok_ref, cot_ref))
-    ]
-    for copy in copies:
-        copy.start()
+def route(imgs, own_slots, params_ref, both_ref, sent_ref, logits_ref, combine_ref):
+    tokens, cotangent = both_ref[0], both_ref[1]
     slots, d = params_ref.shape
     rows, columns = logits_ref.shape
     spread = dot(slot_rows(rows, slots, imgs, own_slots), params_ref[...]).astype(BF16)
-    for copy in copies:
-        copy.wait()
-    tokens, cotangent = both_ref[0], both_ref[1]
     logits = dot(spread, tokens, 1, 1)
     mine = own_image(rows, columns, imgs, own_slots, columns // imgs)
     logits = jnp.where(mine, logits, jnp.finfo(F32).min)
@@ -168,16 +166,19 @@
     tokens, cotangent = both_ref[0], both_ref[1]
     slots, d = params_ref.shape
     rows = logits_ref.shape[0]
+    block = imgs * own_slots
+    order = [at for core in range(2) for at in range(core * block, rows, 2 * block)]
+    logits = jnp.concatenate([logits_ref[at : at + block] for at in order], axis=0)
+    combine = jnp.concatenate([combine_ref[at : at + block] for at in order], axis=0)
     slot_out, slot_in_grad = back_ref[:, :d], back_ref[:, d : 2 * d]
     stats = back_ref[:, 2 * d :].astype(F32)
     top, total, col = [column_of(stats, at) for at in range(3)]
-    combine = combine_ref[...]
-    dispatch = jnp.exp(logits_ref[...] - top) / total
+    dispatch = jnp.exp(logits - top) / total
     combine_grad = dot(slot_out, cotangent, 1, 1)
     dispatch_grad = dot(slot_in_grad, tokens, 1, 1)
     row_sums = jnp.sum(combine * combine_grad, axis=0, keepdims=True)
     logit_grad = dispatch * (dispatch_grad - col) + combine * (combine_grad - row_sums)
-    members = slot_rows(rows, slots, imgs, own_slots)
+    members = slot_rows(rows, slots, imgs, own_slots, True)
     by_slot = dot(members, logit_grad.astype(BF16), 0, 0).astype(BF16)
     share_ref[...] = dot(by_slot, tokens).astype(BF16)
     token_grad = dot(dispatch.astype(BF16), slot_in_grad, 0, 0)
@@ -185,7 +186,7 @@
     token_grad_ref[...] = token_grad.astype(BF16)
 
 
-def call(kernel, out_shape, flops, *operands, **options):
+def call(kernel, out_shape, flops, *operands):
     shapes = [jax.ShapeDtypeStruct(shape, dtype) for shape, dtype in out_shape]
     size = sum(value.size * value.dtype.itemsize for value in list(operands) + shapes)
     return pl.pallas_call(
@@ -193,7 +194,6 @@
         out_shape=shapes,
         compiler_params=pltpu.CompilerParams(vmem_limit_bytes=32 * 1024 * 1024),
         cost_estimate=pl.CostEstimate(flops=flops, bytes_accessed=size, transcendentals=16384),
-        **options,
     )(*operands)
 
 
@@ -258,12 +258,12 @@
     pairs = (peers * rows, imgs * share)
     wide = 2 * d + 128
     flat = (imgs * share, d)
-    sent, logits, combine, both = call(
+    params, tokens, cotangent = lax.optimization_barrier((params, tokens, cotangent))
+    both = jnp.stack([tokens.reshape(flat), cotangent.reshape(flat)])
+    sent, logits, combine = call(
         functools.partial(route, imgs, own_slots),
-        [((peers * rows, wide), BF16), (pairs, F32), (pairs, F32), ((2,) + flat, BF16)],
-        100_000_000, params, tokens.reshape(flat), cotangent.reshape(flat),
-        in_specs=[pl.BlockSpec(memory_space=space) for space in (pltpu.VMEM, pltpu.HBM, pltpu.HBM)],
-        scratch_shapes=[pltpu.SemaphoreType.DMA((2,))],
+        [((peers * rows, wide), BF16), (pairs, F32), (pairs, F32)],
+        100_000_000, params, both,
     )
     taken = exchange(sent.reshape(peers, rows, wide), "expert")
     own, slot_in_wide, scalars = call(
@@ -287,14 +287,15 @@
     w_out_grad = w_out_grad.reshape(w_out.shape)
     terms = reduce_dp(partial, rows)
     (back,) = call(
-        functools.partial(deliver, terms.shape[0], peers), [((peers * rows, wide), BF16)],
+        functools.partial(deliver, terms.shape[0], peers // 2), [((peers // 2 * rows, wide), BF16)],
         1_000_000, terms.reshape(-1, d), slot_in_wide, scalars,
     )
-    back = exchange(back.reshape(peers, rows, wide), "expert")
+    back = exchange(back.reshape(peers // 2, rows, wide), "expert", expert_groups(0, 1))
+    back = everywhere(back.reshape(-1, wide), "expert", expert_groups(2))
 
     token_grad, share_grad = call(
         functools.partial(finish, imgs, own_slots),
-        [(both.shape[1:], BF16), ((slots, d), BF16)],
+        [(flat, BF16), ((slots, d), BF16)],
         100_000_000, back.reshape(peers * rows, wide), logits, combine, params, both,
     )
     token_grad = token_grad.reshape(tokens.shape)

time: 187 us -> 185 us (0.989)
    all_to_all x8 -> x9, blocking collectives: 161 us -> 161 us  [exchange(): lax.all_to_all(value, axis, split_axis=0, concat_axis=0, axis_index_group...]
where the time goes in v12:
time: 185 us; the launch traced here: 184 us
  blocking collectives  161 us (87%)
  waiting for transfers between devices  10.1 us (5%)
  Pallas kernels  5.94 us (3%)
  starting transfers between devices  3.5 us (2%)
    all_to_all x9, blocking collectives, exchange(): lax.all_to_all(value, axis, split_axis=0, concat_axis=0, axis_index_group...  161 us
    all_to_all x1, waiting for transfers between devices, exchange(): lax.all_to_all(value, axis, split_axis=0, concat_axis=0, axis_index_group...  10.1 us
    pallas_call x7, Pallas kernels, call(): pl.pallas_call(kernel, out_shape=shapes, compiler_params=pltpu.CompilerPa...  5.94 us
  transfers between devices with their start and end apart: 1, of which 1 were waited for; matrix products, arithmetic and copies ran while one was open for 0% of the time, Pallas kernels for 1%

profile of v12, /device:TPU:1, one launch (start us, length us, event | category | flops | bytes accessed | tf_op | source)
XLA Modules:
  0.0 184.4 jit_solution(3811750288544532342)
XLA Ops:
  0.6 0.7 broadcast_in_dim.18
  1.4 16.7 %all_to_all.50 = bf16[16,2,1280]{2,1,0:T(2,128)(2,1)S(1)} all-to-all(bf16[16,2,1280]{2,1,0:T(2,128)(2,1)S(1)} %broadcast_in_dim.18), channel_id=1, replica_groups=mesh['dp'=32,'expert'=16] {'expert'}, dimensions={0} | all-to-all | bytes 163840 | tf_op jit(solution)/shard_map/all_to_all | solution.py:30
  18.1 1.0 pad_maximum_fusion.both_ref
  19.2 0.8 shard_map.84
  20.0 16.5 %all_to_all.51 = bf16[16,8,2688]{2,1,0:T(8,128)(2,1)S(1)} all-to-all(bf16[16,8,2688]{2,1,0:T(8,128)(2,1)S(1)} %bitcast.33), channel_id=1, replica_groups=mesh['dp'=32,'expert'=16] {'expert'}, dimensions={0} | all-to-all | bytes 1376256 | tf_op jit(solution)/shard_map/all_to_all | solution.py:30
  36.5 0.2 shard_map.85
  36.8 34.4 %all_to_all.52 = bf16[8,16,1280]{2,1,0:T(8,128)(2,1)S(1)} all-to-all(bf16[8,16,1280]{2,1,0:T(8,128)(2,1)S(1)} %broadcast_in_dim.19), channel_id=1, replica_groups={{0,32,64,96,128,160,192,224},{16,48,80,112,144,176,208,240},{256,288,32..., dimensions={0} | all-to-all | bytes 655360 | tf_op jit(solution)/shard_map/all_to_all | solution.py:30
  71.4 14.8 %all_to_all.53.gathered_ref = bf16[4,2,64,1280]{3,2,1,0:T(8,128)(2,1)S(1)} all-to-all(bf16[4,2,64,1280]{3,2,1,0:T(8,128)(2,1)S(1)} %broadcast_in_dim.42), channel_id=1, replica_groups={{0,16,256,272},{32,48,288,304},{64,80,320,336},{96,112,352,368},{128,14..., dimensions={0} | all-to-all | bytes 2621440 | tf_op jit(solution)/shard_map/all_to_all | solution.py:30
  86.2 1.5 shard_map.86
  87.7 13.2 %all_to_all.54.taken_ref = bf16[4,2,64,1280]{3,2,1,0:T(8,128)(2,1)S(1)} all-to-all(bf16[4,2,64,1280]{3,2,1,0:T(8,128)(2,1)S(1)} %get-tuple-element.25), channel_id=1, replica_groups={{0,16,256,272},{32,48,288,304},{64,80,320,336},{96,112,352,368},{128,14..., dimensions={0} | all-to-all | bytes 2621440 | tf_op jit(solution)/shard_map/all_to_all | solution.py:30
  100.9 0.2 shard_map.87
  101.0 30.6 %all_to_all.55 = bf16[8,16,1280]{2,1,0:T(8,128)(2,1)S(1)} all-to-all(bf16[8,16,1280]{2,1,0:T(8,128)(2,1)S(1)} %bitcast.32), channel_id=1, replica_groups={{0,32,64,96,128,160,192,224},{16,48,80,112,144,176,208,240},{256,288,32..., dimensions={0} | all-to-all | bytes 655360 | tf_op jit(solution)/shard_map/all_to_all | solution.py:30
  131.7 0.1 shard_map.88
  131.8 10.5 %all_to_all.56 = bf16[8,8,2688]{2,1,0:T(8,128)(2,1)S(1)} all-to-all(bf16[8,8,2688]{2,1,0:T(8,128)(2,1)S(1)} %bitcast.30), channel_id=1, replica_groups={{0,2,4,6,8,10,12,14},{1,3,5,7,9,11,13,15},{16,18,20,22,24,26,28,30},{17..., dimensions={0} | all-to-all | bytes 688128 | tf_op jit(solution)/shard_map/all_to_all | solution.py:30
  142.4 12.9 %all_to_all.57 = bf16[2,64,2688]{2,1,0:T(8,128)(2,1)S(1)} all-to-all(bf16[2,64,2688]{2,1,0:T(8,128)(2,1)S(1)} %broadcast_in_dim.44), channel_id=1, replica_groups={{0,1},{2,3},{4,5},{6,7},{8,9},{10,11},{12,13},{14,15},{16,17},{18,19},{..., dimensions={0} | all-to-all | bytes 1376256 | tf_op jit(solution)/shard_map/all_to_all | solution.py:30
  155.3 1.4 shard_map.89
  156.8 0.1 broadcast_in_dim.46
  156.9 10.9 %all_to_all.58 = bf16[32,2,1280]{2,1,0:T(2,128)(2,1)S(1)} all-to-all(bf16[32,2,1280]{2,1,0:T(2,128)(2,1)S(1)} %bitcast.37), channel_id=1, replica_groups={{0,1,2,3,4,5,6,7,8,9,10,11,12,13,14,15,256,257,258,259,260,261,262,263,..., dimensions={0} | all-to-all | bytes 327680 | tf_op jit(solution)/shard_map/all_to_all | solution.py:30
  167.8 0.2 reduce_sum.21
  167.9 0.7 broadcast_in_dim.47
  168.6 3.5 %all-to-all-start.9 = ((bf16[16,2,1280]{2,1,0:T(2,128)(2,1)}), bf16[16,2,1280]{2,1,0:T(2,128)(2,1)S(1)}, u32[]{:S(2)}, u32[]{:S(2)}) async-start(bf16[16,2,1280]{2,1,0:T(2,128)(2,1)} %broadcast_in_dim.47), calls=%async_computation.9 | async-start | bytes 163840 | tf_op jit(solution)/shard_map/all_to_all | solution.py:30
  172.1 1.6 shard_map.90
  173.7 10.1 %all-to-all-done.9 = bf16[16,2,1280]{2,1,0:T(2,128)(2,1)S(1)} async-done(((bf16[16,2,1280]{2,1,0:T(2,128)(2,1)}), bf16[16,2,1280]{2,1,0:T(2,128)(2,1)S(1)}, u32[]{:S(2)}, u32[]{:S(2)}) %all-to-all-start.9) | async-done | bytes 81952 | tf_op jit(solution)/shard_map/all_to_all | solution.py:30
  183.8 0.6 convert_reduce_fusion
  (10 shorter events, 0.3 us)
Async XLA Ops:
  71.4 14.8 %copy-start = (bf16[2,1280,160]{1,2,0:T(8,128)(2,1)S(1)}, bf16[2,1280,160]{1,2,0:T(8,128)(2,1)}, u32[]{:S(2)}) copy-start(bf16[2,1280,160]{1,2,0:T(8,128)(2,1)} %param.8) | copy-start | bytes 2457604
  71.4 14.8 %copy-start.1 = (bf16[2,160,1280]{2,1,0:T(8,128)(2,1)S(1)}, bf16[2,160,1280]{2,1,0:T(8,128)(2,1)}, u32[]{:S(2)}) copy-start(bf16[2,160,1280]{2,1,0:T(8,128)(2,1)} %param.9) | copy-start | bytes 2457604
  168.6 15.2 %all-to-all-start.9 = ((bf16[16,2,1280]{2,1,0:T(2,128)(2,1)}), bf16[16,2,1280]{2,1,0:T(2,128)(2,1)S(1)}, u32[]{:S(2)}, u32[]{:S(2)}) async-start(bf16[16,2,1280]{2,1,0:T(2,128)(2,1)} %broadcast_in_dim.47), calls=%async_computation.9 | async-start | bytes 163840 | tf_op jit(solution)/shard_map/all_to_all | solution.py:30

commit v13 on v12

--- a/solution.py
+++ b/solution.py
@@ -41,6 +41,16 @@
     return groups_of("dp", (lax.axis_size("dp") // 4, 2), inner)
 
 
+def far_groups():
+    depth = lax.axis_size("dp") // 2
+    late = [int(pair >= depth // 4) for pair in range(depth // 2)]
+    return [
+        [y * depth + 2 * pair + (late[pair] ^ which) for pair in range(depth // 2)]
+        for y in range(2)
+        for which in range(2)
+    ]
+
+
 def expert_groups(*inner):
     return groups_of("expert", (2, 2), inner)
 
@@ -53,7 +63,7 @@
 
 def gather_dp(own):
     rows, d = own.shape[0] // 2, own.shape[1]
-    far = everywhere(own, "dp", dp_groups(1)).reshape(-1, 2, rows, d)
+    far = everywhere(own, "dp", far_groups()).reshape(-1, 2, rows, d)
     far = jnp.transpose(far, (1, 0, 2, 3)).reshape(2, -1, d)
     return everywhere(far, "dp", dp_groups(0, 2))
 
@@ -64,7 +74,7 @@
     (total,) = call(
         functools.partial(add_square, rows), [((2 * partial.shape[2], d), BF16)], 2_000_000, taken
     )
-    return exchange(total.reshape(-1, 2 * rows, d), "dp", dp_groups(1))
+    return exchange(total.reshape(-1, 2 * rows, d), "dp", far_groups())
 
 
 def dot(left, right, left_dim=1, right_dim=0):

time: 185 us -> 183 us (0.989)
  blocking collectives: 161 us -> 154 us
  starting transfers between devices: 3.5 us -> 7.33 us
    all_to_all x9, blocking collectives: 161 us -> 154 us  [exchange(): lax.all_to_all(value, axis, split_axis=0, concat_axis=0, axis_index_group...]
    all_to_all x1, starting transfers between devices: 3.5 us -> 7.33 us  [exchange(): lax.all_to_all(value, axis, split_axis=0, concat_axis=0, axis_index_group...]
where the time goes in v13:
time: 183 us; the launch traced here: 182 us
  blocking collectives  154 us (84%)
  waiting for transfers between devices  10.2 us (6%)
  starting transfers between devices  7.33 us (4%)
  Pallas kernels  5.94 us (3%)
    all_to_all x9, blocking collectives, exchange(): lax.all_to_all(value, axis, split_axis=0, concat_axis=0, axis_index_group...  154 us
    all_to_all x1, waiting for transfers between devices, exchange(): lax.all_to_all(value, axis, split_axis=0, concat_axis=0, axis_index_group...  10.2 us
    all_to_all x1, starting transfers between devices, exchange(): lax.all_to_all(value, axis, split_axis=0, concat_axis=0, axis_index_group...  7.33 us
    pallas_call x7, Pallas kernels, call(): pl.pallas_call(kernel, out_shape=shapes, compiler_params=pltpu.CompilerPa...  5.94 us
  transfers between devices with their start and end apart: 1, of which 1 were waited for; matrix products, arithmetic and copies ran while one was open for 0% of the time, Pallas kernels for 1%

profile of v13, /device:TPU:1, one launch (start us, length us, event | category | flops | bytes accessed | tf_op | source)
XLA Modules:
  0.0 182.2 jit_solution(1047223015503295567)
XLA Ops:
  0.6 0.7 broadcast_in_dim.18
  1.4 16.7 %all_to_all.50 = bf16[16,2,1280]{2,1,0:T(2,128)(2,1)S(1)} all-to-all(bf16[16,2,1280]{2,1,0:T(2,128)(2,1)S(1)} %broadcast_in_dim.18), channel_id=1, replica_groups=mesh['dp'=32,'expert'=16] {'expert'}, dimensions={0} | all-to-all | bytes 163840 | tf_op jit(solution)/shard_map/all_to_all | solution.py:30
  18.1 1.0 pad_maximum_fusion.both_ref
  19.2 0.8 shard_map.84
  20.0 16.5 %all_to_all.51 = bf16[16,8,2688]{2,1,0:T(8,128)(2,1)S(1)} all-to-all(bf16[16,8,2688]{2,1,0:T(8,128)(2,1)S(1)} %bitcast.33), channel_id=1, replica_groups=mesh['dp'=32,'expert'=16] {'expert'}, dimensions={0} | all-to-all | bytes 1376256 | tf_op jit(solution)/shard_map/all_to_all | solution.py:30
  36.5 0.2 shard_map.85
  36.8 32.7 %all_to_all.52 = bf16[8,16,1280]{2,1,0:T(8,128)(2,1)S(1)} all-to-all(bf16[8,16,1280]{2,1,0:T(8,128)(2,1)S(1)} %broadcast_in_dim.19), channel_id=1, replica_groups={{0,32,64,96,144,176,208,240},{16,48,80,112,128,160,192,224},{256,288,32..., dimensions={0} | all-to-all | bytes 655360 | tf_op jit(solution)/shard_map/all_to_all | solution.py:30
  69.7 19.0 %all_to_all.53.gathered_ref = bf16[4,2,64,1280]{3,2,1,0:T(8,128)(2,1)S(1)} all-to-all(bf16[4,2,64,1280]{3,2,1,0:T(8,128)(2,1)S(1)} %broadcast_in_dim.42), channel_id=1, replica_groups={{0,16,256,272},{32,48,288,304},{64,80,320,336},{96,112,352,368},{128,14..., dimensions={0} | all-to-all | bytes 2621440 | tf_op jit(solution)/shard_map/all_to_all | solution.py:30
  88.6 1.5 shard_map.86
  90.2 15.3 %all_to_all.54.taken_ref = bf16[4,2,64,1280]{3,2,1,0:T(8,128)(2,1)S(1)} all-to-all(bf16[4,2,64,1280]{3,2,1,0:T(8,128)(2,1)S(1)} %get-tuple-element.25), channel_id=1, replica_groups={{0,16,256,272},{32,48,288,304},{64,80,320,336},{96,112,352,368},{128,14..., dimensions={0} | all-to-all | bytes 2621440 | tf_op jit(solution)/shard_map/all_to_all | solution.py:30
  105.5 0.2 shard_map.87
  105.7 21.6 %all_to_all.55 = bf16[8,16,1280]{2,1,0:T(8,128)(2,1)S(1)} all-to-all(bf16[8,16,1280]{2,1,0:T(8,128)(2,1)S(1)} %bitcast.32), channel_id=1, replica_groups={{0,32,64,96,144,176,208,240},{16,48,80,112,128,160,192,224},{256,288,32..., dimensions={0} | all-to-all | bytes 655360 | tf_op jit(solution)/shard_map/all_to_all | solution.py:30
  127.3 0.1 shard_map.88
  127.4 10.4 %all_to_all.56 = bf16[8,8,2688]{2,1,0:T(8,128)(2,1)S(1)} all-to-all(bf16[8,8,2688]{2,1,0:T(8,128)(2,1)S(1)} %bitcast.30), channel_id=1, replica_groups={{0,2,4,6,8,10,12,14},{1,3,5,7,9,11,13,15},{16,18,20,22,24,26,28,30},{17..., dimensions={0} | all-to-all | bytes 688128 | tf_op jit(solution)/shard_map/all_to_all | solution.py:30
  137.9 11.3 %all_to_all.57 = bf16[2,64,2688]{2,1,0:T(8,128)(2,1)S(1)} all-to-all(bf16[2,64,2688]{2,1,0:T(8,128)(2,1)S(1)} %broadcast_in_dim.44), channel_id=1, replica_groups={{0,1},{2,3},{4,5},{6,7},{8,9},{10,11},{12,13},{14,15},{16,17},{18,19},{..., dimensions={0} | all-to-all | bytes 1376256 | tf_op jit(solution)/shard_map/all_to_all | solution.py:30
  149.1 1.4 shard_map.89
  150.6 0.1 broadcast_in_dim.46
  150.7 10.9 %all_to_all.58 = bf16[32,2,1280]{2,1,0:T(2,128)(2,1)S(1)} all-to-all(bf16[32,2,1280]{2,1,0:T(2,128)(2,1)S(1)} %bitcast.37), channel_id=1, replica_groups={{0,1,2,3,4,5,6,7,8,9,10,11,12,13,14,15,256,257,258,259,260,261,262,263,..., dimensions={0} | all-to-all | bytes 327680 | tf_op jit(solution)/shard_map/all_to_all | solution.py:30
  161.6 0.2 reduce_sum.21
  161.8 0.7 broadcast_in_dim.47
  162.4 7.3 %all-to-all-start.9 = ((bf16[16,2,1280]{2,1,0:T(2,128)(2,1)}), bf16[16,2,1280]{2,1,0:T(2,128)(2,1)S(1)}, u32[]{:S(2)}, u32[]{:S(2)}) async-start(bf16[16,2,1280]{2,1,0:T(2,128)(2,1)} %broadcast_in_dim.47), calls=%async_computation.9 | async-start | bytes 163840 | tf_op jit(solution)/shard_map/all_to_all | solution.py:30
  169.8 1.6 shard_map.90
  171.4 10.2 %all-to-all-done.9 = bf16[16,2,1280]{2,1,0:T(2,128)(2,1)S(1)} async-done(((bf16[16,2,1280]{2,1,0:T(2,128)(2,1)}), bf16[16,2,1280]{2,1,0:T(2,128)(2,1)S(1)}, u32[]{:S(2)}, u32[]{:S(2)}) %all-to-all-start.9) | async-done | bytes 81952 | tf_op jit(solution)/shard_map/all_to_all | solution.py:30
  181.6 0.6 convert_reduce_fusion
  (10 shorter events, 0.3 us)
Async XLA Ops:
  69.6 19.0 %copy-start = (bf16[2,1280,160]{1,2,0:T(8,128)(2,1)S(1)}, bf16[2,1280,160]{1,2,0:T(8,128)(2,1)}, u32[]{:S(2)}) copy-start(bf16[2,1280,160]{1,2,0:T(8,128)(2,1)} %param.8) | copy-start | bytes 2457604
  69.6 19.0 %copy-start.1 = (bf16[2,160,1280]{2,1,0:T(8,128)(2,1)S(1)}, bf16[2,160,1280]{2,1,0:T(8,128)(2,1)}, u32[]{:S(2)}) copy-start(bf16[2,160,1280]{2,1,0:T(8,128)(2,1)} %param.9) | copy-start | bytes 2457604
  162.4 19.1 %all-to-all-start.9 = ((bf16[16,2,1280]{2,1,0:T(2,128)(2,1)}), bf16[16,2,1280]{2,1,0:T(2,128)(2,1)S(1)}, u32[]{:S(2)}, u32[]{:S(2)}) async-start(bf16[16,2,1280]{2,1,0:T(2,128)(2,1)} %broadcast_in_dim.47), calls=%async_computation.9 | async-start | bytes 163840 | tf_op jit(solution)/shard_map/all_to_all | solution.py:30

commit v14 on v13

--- a/solution.py
+++ b/solution.py
@@ -41,13 +41,28 @@
     return groups_of("dp", (lax.axis_size("dp") // 4, 2), inner)
 
 
-def far_groups():
-    depth = lax.axis_size("dp") // 2
+def z_groups(of_core):
+    peers, depth = lax.axis_size("expert"), lax.axis_size("dp") // 2
+    return [
+        [(y * depth + z % depth) * peers + expert for y, z in group]
+        for expert in range(peers)
+        for group in of_core(expert % 2, depth)
+    ]
+
+
+def far_of_core(core, depth):
     late = [int(pair >= depth // 4) for pair in range(depth // 2)]
     return [
-        [y * depth + 2 * pair + (late[pair] ^ which) for pair in range(depth // 2)]
+        [(y, 2 * pair + (late[pair] ^ which) + core) for pair in range(depth // 2)]
         for y in range(2)
         for which in range(2)
+    ]
+
+
+def square_of_core(core, depth):
+    return [
+        [(y, 2 * pair + near + core) for y in range(2) for near in range(2)]
+        for pair in range(depth // 2)
     ]
 
 
@@ -63,18 +78,18 @@
 
 def gather_dp(own):
     rows, d = own.shape[0] // 2, own.shape[1]
-    far = everywhere(own, "dp", far_groups()).reshape(-1, 2, rows, d)
+    far = everywhere(own, ("dp", "expert"), z_groups(far_of_core)).reshape(-1, 2, rows, d)
     far = jnp.transpose(far, (1, 0, 2, 3)).reshape(2, -1, d)
-    return everywhere(far, "dp", dp_groups(0, 2))
+    return everywhere(far, ("dp", "expert"), z_groups(square_of_core))
 
 
 def reduce_dp(partial, rows):
     d = partial.shape[-1]
-    taken = exchange(partial, "dp", dp_groups(0, 2))
+    taken = exchange(partial, ("dp", "expert"), z_groups(square_of_core))
     (total,) = call(
         functools.partial(add_square, rows), [((2 * partial.shape[2], d), BF16)], 2_000_000, taken
     )
-    return exchange(total.reshape(-1, 2 * rows, d), "dp", far_groups())
+    return exchange(total.reshape(-1, 2 * rows, d), ("dp", "expert"), z_groups(far_of_core))
 
 
 def dot(left, right, left_dim=1, right_dim=0):

time: 183 us -> 188 us (1.027)
  blocking collectives: 154 us -> 163 us
  starting transfers between devices: 7.33 us -> 3.51 us
    all_to_all x9, blocking collectives: 154 us -> 163 us  [exchange(): lax.all_to_all(value, axis, split_axis=0, concat_axis=0, axis_index_group...]
    all_to_all x1, starting transfers between devices: 7.33 us -> 3.51 us  [exchange(): lax.all_to_all(value, axis, split_axis=0, concat_axis=0, axis_index_group...]
where the time goes in v14:
time: 188 us; the launch traced here: 187 us
  blocking collectives  163 us (87%)
  waiting for transfers between devices  10.2 us (5%)
  Pallas kernels  5.95 us (3%)
  starting transfers between devices  3.51 us (2%)
    all_to_all x9, blocking collectives, exchange(): lax.all_to_all(value, axis, split_axis=0, concat_axis=0, axis_index_group...  163 us
    all_to_all x1, waiting for transfers between devices, exchange(): lax.all_to_all(value, axis, split_axis=0, concat_axis=0, axis_index_group...  10.2 us
    pallas_call x7, Pallas kernels, call(): pl.pallas_call(kernel, out_shape=shapes, compiler_params=pltpu.CompilerPa...  5.95 us
  transfers between devices with their start and end apart: 1, of which 1 were waited for; matrix products, arithmetic and copies ran while one was open for 0% of the time, Pallas kernels for 1%

profile of v14, /device:TPU:1, one launch (start us, length us, event | category | flops | bytes accessed | tf_op | source)
XLA Modules:
  0.0 187.3 jit_solution(11897771899134759111)
XLA Ops:
  0.6 0.7 broadcast_in_dim.18
  1.4 16.7 %all_to_all.50 = bf16[16,2,1280]{2,1,0:T(2,128)(2,1)S(1)} all-to-all(bf16[16,2,1280]{2,1,0:T(2,128)(2,1)S(1)} %broadcast_in_dim.18), channel_id=1, replica_groups=mesh['dp'=32,'expert'=16] {'expert'}, dimensions={0} | all-to-all | bytes 163840 | tf_op jit(solution)/shard_map/all_to_all | solution.py:30
  18.1 1.0 pad_maximum_fusion.both_ref
  19.2 0.8 shard_map.84
  20.0 16.5 %all_to_all.51 = bf16[16,8,2688]{2,1,0:T(8,128)(2,1)S(1)} all-to-all(bf16[16,8,2688]{2,1,0:T(8,128)(2,1)S(1)} %bitcast.33), channel_id=1, replica_groups=mesh['dp'=32,'expert'=16] {'expert'}, dimensions={0} | all-to-all | bytes 1376256 | tf_op jit(solution)/shard_map/all_to_all | solution.py:30
  36.5 0.2 shard_map.85
  36.8 30.9 %all_to_all.52 = bf16[8,16,1280]{2,1,0:T(8,128)(2,1)S(1)} all-to-all(bf16[8,16,1280]{2,1,0:T(8,128)(2,1)S(1)} %broadcast_in_dim.19), channel_id=1, replica_groups={{0,32,64,96,144,176,208,240},{16,48,80,112,128,160,192,224},{256,288,32..., dimensions={0} | all-to-all | bytes 655360 | tf_op jit(solution)/shard_map/all_to_all | solution.py:30
  67.9 25.0 %all_to_all.53.gathered_ref = bf16[4,2,64,1280]{3,2,1,0:T(8,128)(2,1)S(1)} all-to-all(bf16[4,2,64,1280]{3,2,1,0:T(8,128)(2,1)S(1)} %broadcast_in_dim.42), channel_id=1, replica_groups={{0,16,256,272},{32,48,288,304},{64,80,320,336},{96,112,352,368},{128,14..., dimensions={0} | all-to-all | bytes 2621440 | tf_op jit(solution)/shard_map/all_to_all | solution.py:30
  92.8 1.5 shard_map.86
  94.4 20.9 %all_to_all.54.taken_ref = bf16[4,2,64,1280]{3,2,1,0:T(8,128)(2,1)S(1)} all-to-all(bf16[4,2,64,1280]{3,2,1,0:T(8,128)(2,1)S(1)} %get-tuple-element.25), channel_id=1, replica_groups={{0,16,256,272},{32,48,288,304},{64,80,320,336},{96,112,352,368},{128,14..., dimensions={0} | all-to-all | bytes 2621440 | tf_op jit(solution)/shard_map/all_to_all | solution.py:30
  115.3 0.2 shard_map.87
  115.4 15.0 %all_to_all.55 = bf16[8,16,1280]{2,1,0:T(8,128)(2,1)S(1)} all-to-all(bf16[8,16,1280]{2,1,0:T(8,128)(2,1)S(1)} %bitcast.32), channel_id=1, replica_groups={{0,32,64,96,144,176,208,240},{16,48,80,112,128,160,192,224},{256,288,32..., dimensions={0} | all-to-all | bytes 655360 | tf_op jit(solution)/shard_map/all_to_all | solution.py:30
  130.4 0.1 shard_map.88
  130.6 12.5 %all_to_all.56 = bf16[8,8,2688]{2,1,0:T(8,128)(2,1)S(1)} all-to-all(bf16[8,8,2688]{2,1,0:T(8,128)(2,1)S(1)} %bitcast.30), channel_id=1, replica_groups={{0,2,4,6,8,10,12,14},{1,3,5,7,9,11,13,15},{16,18,20,22,24,26,28,30},{17..., dimensions={0} | all-to-all | bytes 688128 | tf_op jit(solution)/shard_map/all_to_all | solution.py:30
  143.1 14.9 %all_to_all.57 = bf16[2,64,2688]{2,1,0:T(8,128)(2,1)S(1)} all-to-all(bf16[2,64,2688]{2,1,0:T(8,128)(2,1)S(1)} %broadcast_in_dim.44), channel_id=1, replica_groups={{0,1},{2,3},{4,5},{6,7},{8,9},{10,11},{12,13},{14,15},{16,17},{18,19},{..., dimensions={0} | all-to-all | bytes 1376256 | tf_op jit(solution)/shard_map/all_to_all | solution.py:30
  158.0 1.4 shard_map.89
  159.5 0.1 broadcast_in_dim.46
  159.6 10.9 %all_to_all.58 = bf16[32,2,1280]{2,1,0:T(2,128)(2,1)S(1)} all-to-all(bf16[32,2,1280]{2,1,0:T(2,128)(2,1)S(1)} %bitcast.37), channel_id=1, replica_groups={{0,1,2,3,4,5,6,7,8,9,10,11,12,13,14,15,256,257,258,259,260,261,262,263,..., dimensions={0} | all-to-all | bytes 327680 | tf_op jit(solution)/shard_map/all_to_all | solution.py:30
  170.5 0.2 reduce_sum.21
  170.7 0.7 broadcast_in_dim.47
  171.3 3.5 %all-to-all-start.9 = ((bf16[16,2,1280]{2,1,0:T(2,128)(2,1)}), bf16[16,2,1280]{2,1,0:T(2,128)(2,1)S(1)}, u32[]{:S(2)}, u32[]{:S(2)}) async-start(bf16[16,2,1280]{2,1,0:T(2,128)(2,1)} %broadcast_in_dim.47), calls=%async_computation.9 | async-start | bytes 163840 | tf_op jit(solution)/shard_map/all_to_all | solution.py:30
  174.9 1.6 shard_map.90
  176.5 10.2 %all-to-all-done.9 = bf16[16,2,1280]{2,1,0:T(2,128)(2,1)S(1)} async-done(((bf16[16,2,1280]{2,1,0:T(2,128)(2,1)}), bf16[16,2,1280]{2,1,0:T(2,128)(2,1)S(1)}, u32[]{:S(2)}, u32[]{:S(2)}) %all-to-all-start.9) | async-done | bytes 81952 | tf_op jit(solution)/shard_map/all_to_all | solution.py:30
  186.6 0.6 convert_reduce_fusion
  (10 shorter events, 0.3 us)
Async XLA Ops:
  67.9 25.0 %copy-start = (bf16[2,1280,160]{1,2,0:T(8,128)(2,1)S(1)}, bf16[2,1280,160]{1,2,0:T(8,128)(2,1)}, u32[]{:S(2)}) copy-start(bf16[2,1280,160]{1,2,0:T(8,128)(2,1)} %param.8) | copy-start | bytes 2457604
  67.9 25.0 %copy-start.1 = (bf16[2,160,1280]{2,1,0:T(8,128)(2,1)S(1)}, bf16[2,160,1280]{2,1,0:T(8,128)(2,1)}, u32[]{:S(2)}) copy-start(bf16[2,160,1280]{2,1,0:T(8,128)(2,1)} %param.9) | copy-start | bytes 2457604
  171.3 15.3 %all-to-all-start.9 = ((bf16[16,2,1280]{2,1,0:T(2,128)(2,1)}), bf16[16,2,1280]{2,1,0:T(2,128)(2,1)S(1)}, u32[]{:S(2)}, u32[]{:S(2)}) async-start(bf16[16,2,1280]{2,1,0:T(2,128)(2,1)} %broadcast_in_dim.47), calls=%async_computation.9 | async-start | bytes 163840 | tf_op jit(solution)/shard_map/all_to_all | solution.py:30

commit v15 on v13

--- a/solution.py
+++ b/solution.py
@@ -170,11 +170,10 @@
 
 
 def finish(
-    imgs, own_slots, back_ref, logits_ref, combine_ref, params_ref, both_ref,
-    token_grad_ref, share_ref,
+    imgs, own_slots, back_ref, logits_ref, combine_ref, both_ref, share_ref, dispatch_ref, grad_ref
 ):
     tokens, cotangent = both_ref[0], both_ref[1]
-    slots, d = params_ref.shape
+    slots, d = share_ref.shape
     rows = logits_ref.shape[0]
     block = imgs * own_slots
     order = [at for core in range(2) for at in range(core * block, rows, 2 * block)]
@@ -191,8 +190,14 @@
     members = slot_rows(rows, slots, imgs, own_slots, True)
     by_slot = dot(members, logit_grad.astype(BF16), 0, 0).astype(BF16)
     share_ref[...] = dot(by_slot, tokens).astype(BF16)
-    token_grad = dot(dispatch.astype(BF16), slot_in_grad, 0, 0)
-    token_grad = token_grad + dot(by_slot, params_ref[...], 0, 0)
+    dispatch_ref[...] = dispatch.astype(BF16)
+    grad_ref[...] = by_slot
+
+
+def token_grads(back_ref, dispatch_ref, grad_ref, params_ref, token_grad_ref):
+    d = params_ref.shape[1]
+    token_grad = dot(dispatch_ref[...], back_ref[:, d : 2 * d], 0, 0)
+    token_grad = token_grad + dot(grad_ref[...], params_ref[...], 0, 0)
     token_grad_ref[...] = token_grad.astype(BF16)
 
 
@@ -303,10 +308,14 @@
     back = exchange(back.reshape(peers // 2, rows, wide), "expert", expert_groups(0, 1))
     back = everywhere(back.reshape(-1, wide), "expert", expert_groups(2))
 
-    token_grad, share_grad = call(
+    back = back.reshape(peers * rows, wide)
+    share_grad, dispatch, by_slot = call(
         functools.partial(finish, imgs, own_slots),
-        [(flat, BF16), ((slots, d), BF16)],
-        100_000_000, back.reshape(peers * rows, wide), logits, combine, params, both,
+        [((slots, d), BF16), (pairs, BF16), ((slots, imgs * share), BF16)],
+        70_000_000, back, logits, combine, both,
+    )
+    (token_grad,) = call(
+        token_grads, [(flat, BF16)], 30_000_000, back, dispatch, by_slot, params
     )
     token_grad = token_grad.reshape(tokens.shape)
 

time: 183 us -> 182 us (level)
    pallas_call x7 -> x8, Pallas kernels: 5.94 us -> 6.07 us  [call(): pl.pallas_call(kernel, out_shape=shapes, compiler_params=pltpu.CompilerPa...]
where the time goes in v15:
time: 182 us; the launch traced here: 181 us
  blocking collectives  154 us (85%)
  waiting for transfers between devices  9.25 us (5%)
  starting transfers between devices  7.34 us (4%)
  Pallas kernels  6.07 us (3%)
  other arithmetic  1.82 us (1%)
    all_to_all x9, blocking collectives, exchange(): lax.all_to_all(value, axis, split_axis=0, concat_axis=0, axis_index_group...  154 us
    all_to_all x1, waiting for transfers between devices, exchange(): lax.all_to_all(value, axis, split_axis=0, concat_axis=0, axis_index_group...  9.25 us
    all_to_all x1, starting transfers between devices, exchange(): lax.all_to_all(value, axis, split_axis=0, concat_axis=0, axis_index_group...  7.34 us
    pallas_call x8, Pallas kernels, call(): pl.pallas_call(kernel, out_shape=shapes, compiler_params=pltpu.CompilerPa...  6.07 us
  transfers between devices with their start and end apart: 1, of which 1 were waited for; matrix products, arithmetic and copies ran while one was open for 0% of the time, Pallas kernels for 1%

profile of v15, /device:TPU:1, one launch (start us, length us, event | category | flops | bytes accessed | tf_op | source)
XLA Modules:
  0.0 181.4 jit_solution(494040191265532922)
XLA Ops:
  0.6 0.7 broadcast_in_dim.18
  1.4 16.7 %all_to_all.50 = bf16[16,2,1280]{2,1,0:T(2,128)(2,1)S(1)} all-to-all(bf16[16,2,1280]{2,1,0:T(2,128)(2,1)S(1)} %broadcast_in_dim.18), channel_id=1, replica_groups=mesh['dp'=32,'expert'=16] {'expert'}, dimensions={0} | all-to-all | bytes 163840 | tf_op jit(solution)/shard_map/all_to_all | solution.py:30
  18.1 1.0 pad_maximum_fusion.both_ref
  19.2 0.8 shard_map.84
  20.0 16.5 %all_to_all.51 = bf16[16,8,2688]{2,1,0:T(8,128)(2,1)S(1)} all-to-all(bf16[16,8,2688]{2,1,0:T(8,128)(2,1)S(1)} %bitcast.34), channel_id=1, replica_groups=mesh['dp'=32,'expert'=16] {'expert'}, dimensions={0} | all-to-all | bytes 1376256 | tf_op jit(solution)/shard_map/all_to_all | solution.py:30
  36.5 0.2 shard_map.85
  36.8 32.7 %all_to_all.52 = bf16[8,16,1280]{2,1,0:T(8,128)(2,1)S(1)} all-to-all(bf16[8,16,1280]{2,1,0:T(8,128)(2,1)S(1)} %broadcast_in_dim.19), channel_id=1, replica_groups={{0,32,64,96,144,176,208,240},{16,48,80,112,128,160,192,224},{256,288,32..., dimensions={0} | all-to-all | bytes 655360 | tf_op jit(solution)/shard_map/all_to_all | solution.py:30
  69.7 19.0 %all_to_all.53.gathered_ref = bf16[4,2,64,1280]{3,2,1,0:T(8,128)(2,1)S(1)} all-to-all(bf16[4,2,64,1280]{3,2,1,0:T(8,128)(2,1)S(1)} %broadcast_in_dim.42), channel_id=1, replica_groups={{0,16,256,272},{32,48,288,304},{64,80,320,336},{96,112,352,368},{128,14..., dimensions={0} | all-to-all | bytes 2621440 | tf_op jit(solution)/shard_map/all_to_all | solution.py:30
  88.6 1.5 shard_map.86
  90.2 15.3 %all_to_all.54.taken_ref = bf16[4,2,64,1280]{3,2,1,0:T(8,128)(2,1)S(1)} all-to-all(bf16[4,2,64,1280]{3,2,1,0:T(8,128)(2,1)S(1)} %get-tuple-element.26), channel_id=1, replica_groups={{0,16,256,272},{32,48,288,304},{64,80,320,336},{96,112,352,368},{128,14..., dimensions={0} | all-to-all | bytes 2621440 | tf_op jit(solution)/shard_map/all_to_all | solution.py:30
  105.5 0.2 shard_map.87
  105.7 21.6 %all_to_all.55 = bf16[8,16,1280]{2,1,0:T(8,128)(2,1)S(1)} all-to-all(bf16[8,16,1280]{2,1,0:T(8,128)(2,1)S(1)} %bitcast.33), channel_id=1, replica_groups={{0,32,64,96,144,176,208,240},{16,48,80,112,128,160,192,224},{256,288,32..., dimensions={0} | all-to-all | bytes 655360 | tf_op jit(solution)/shard_map/all_to_all | solution.py:30
  127.3 0.1 shard_map.88
  127.4 10.4 %all_to_all.56 = bf16[8,8,2688]{2,1,0:T(8,128)(2,1)S(1)} all-to-all(bf16[8,8,2688]{2,1,0:T(8,128)(2,1)S(1)} %bitcast.31), channel_id=1, replica_groups={{0,2,4,6,8,10,12,14},{1,3,5,7,9,11,13,15},{16,18,20,22,24,26,28,30},{17..., dimensions={0} | all-to-all | bytes 688128 | tf_op jit(solution)/shard_map/all_to_all | solution.py:30
  137.9 11.3 %all_to_all.57 = bf16[2,64,2688]{2,1,0:T(8,128)(2,1)S(1)} all-to-all(bf16[2,64,2688]{2,1,0:T(8,128)(2,1)S(1)} %broadcast_in_dim.44), channel_id=1, replica_groups={{0,1},{2,3},{4,5},{6,7},{8,9},{10,11},{12,13},{14,15},{16,17},{18,19},{..., dimensions={0} | all-to-all | bytes 1376256 | tf_op jit(solution)/shard_map/all_to_all | solution.py:30
  149.1 0.6 shard_map.89
  149.9 10.9 %all_to_all.58 = bf16[32,2,1280]{2,1,0:T(2,128)(2,1)S(1)} all-to-all(bf16[32,2,1280]{2,1,0:T(2,128)(2,1)S(1)} %bitcast.38), channel_id=1, replica_groups={{0,1,2,3,4,5,6,7,8,9,10,11,12,13,14,15,256,257,258,259,260,261,262,263,..., dimensions={0} | all-to-all | bytes 327680 | tf_op jit(solution)/shard_map/all_to_all | solution.py:30
  160.8 0.2 reduce_sum.21
  161.0 0.7 broadcast_in_dim.47
  161.6 7.3 %all-to-all-start.9 = ((bf16[16,2,1280]{2,1,0:T(2,128)(2,1)}), bf16[16,2,1280]{2,1,0:T(2,128)(2,1)S(1)}, u32[]{:S(2)}, u32[]{:S(2)}) async-start(bf16[16,2,1280]{2,1,0:T(2,128)(2,1)} %broadcast_in_dim.47), calls=%async_computation.9 | async-start | bytes 163840 | tf_op jit(solution)/shard_map/all_to_all | solution.py:30
  169.0 1.6 shard_map.91
  170.6 0.9 shard_map.90
  171.5 9.3 %all-to-all-done.9 = bf16[16,2,1280]{2,1,0:T(2,128)(2,1)S(1)} async-done(((bf16[16,2,1280]{2,1,0:T(2,128)(2,1)}), bf16[16,2,1280]{2,1,0:T(2,128)(2,1)S(1)}, u32[]{:S(2)}, u32[]{:S(2)}) %all-to-all-start.9) | async-done | bytes 81952 | tf_op jit(solution)/shard_map/all_to_all | solution.py:30
  180.8 0.6 convert_reduce_fusion
  (11 shorter events, 0.4 us)
Async XLA Ops:
  69.6 19.0 %copy-start = (bf16[2,1280,160]{1,2,0:T(8,128)(2,1)S(1)}, bf16[2,1280,160]{1,2,0:T(8,128)(2,1)}, u32[]{:S(2)}) copy-start(bf16[2,1280,160]{1,2,0:T(8,128)(2,1)} %param.8) | copy-start | bytes 2457604
  69.6 19.0 %copy-start.1 = (bf16[2,160,1280]{2,1,0:T(8,128)(2,1)S(1)}, bf16[2,160,1280]{2,1,0:T(8,128)(2,1)}, u32[]{:S(2)}) copy-start(bf16[2,160,1280]{2,1,0:T(8,128)(2,1)} %param.9) | copy-start | bytes 2457604
  161.6 19.2 %all-to-all-start.9 = ((bf16[16,2,1280]{2,1,0:T(2,128)(2,1)}), bf16[16,2,1280]{2,1,0:T(2,128)(2,1)S(1)}, u32[]{:S(2)}, u32[]{:S(2)}) async-start(bf16[16,2,1280]{2,1,0:T(2,128)(2,1)} %broadcast_in_dim.47), calls=%async_computation.9 | async-start | bytes 163840 | tf_op jit(solution)/shard_map/all_to_all | solution.py:30

commit v16 on v15

--- a/solution.py
+++ b/solution.py
@@ -51,6 +51,10 @@
     ]
 
 
+def square_groups():
+    return [[at[0], at[1], at[3], at[2]] for at in dp_groups(0, 2)]
+
+
 def expert_groups(*inner):
     return groups_of("expert", (2, 2), inner)
 
@@ -65,12 +69,12 @@
     rows, d = own.shape[0] // 2, own.shape[1]
     far = everywhere(own, "dp", far_groups()).reshape(-1, 2, rows, d)
     far = jnp.transpose(far, (1, 0, 2, 3)).reshape(2, -1, d)
-    return everywhere(far, "dp", dp_groups(0, 2))
+    return everywhere(far, "dp", square_groups())
 
 
 def reduce_dp(partial, rows):
     d = partial.shape[-1]
-    taken = exchange(partial, "dp", dp_groups(0, 2))
+    taken = exchange(partial, "dp", square_groups())
     (total,) = call(
         functools.partial(add_square, rows), [((2 * partial.shape[2], d), BF16)], 2_000_000, taken
     )

time: 182 us -> 183 us (level)
  no operation moved by 1% of the time
where the time goes in v16:
time: 183 us
  blocking collectives  155 us (85%)
  waiting for transfers between devices  9.26 us (5%)
  starting transfers between devices  7.7 us (4%)
  Pallas kernels  6.06 us (3%)
    all_to_all x9, blocking collectives, exchange(): lax.all_to_all(value, axis, split_axis=0, concat_axis=0, axis_index_group...  155 us
    all_to_all x1, waiting for transfers between devices, exchange(): lax.all_to_all(value, axis, split_axis=0, concat_axis=0, axis_index_group...  9.26 us
    all_to_all x1, starting transfers between devices, exchange(): lax.all_to_all(value, axis, split_axis=0, concat_axis=0, axis_index_group...  7.7 us
    pallas_call x8, Pallas kernels, call(): pl.pallas_call(kernel, out_shape=shapes, compiler_params=pltpu.CompilerPa...  6.06 us
  transfers between devices with their start and end apart: 1, of which 1 were waited for; matrix products, arithmetic and copies ran while one was open for 0% of the time, Pallas kernels for 1%

profile of v16, /device:TPU:1, one launch (start us, length us, event | category | flops | bytes accessed | tf_op | source)
XLA Modules:
  0.0 182.7 jit_solution(3529872959489287004)
XLA Ops:
  0.6 0.7 broadcast_in_dim.18
  1.4 16.7 %all_to_all.50 = bf16[16,2,1280]{2,1,0:T(2,128)(2,1)S(1)} all-to-all(bf16[16,2,1280]{2,1,0:T(2,128)(2,1)S(1)} %broadcast_in_dim.18), channel_id=1, replica_groups=mesh['dp'=32,'expert'=16] {'expert'}, dimensions={0} | all-to-all | bytes 163840 | tf_op jit(solution)/shard_map/all_to_all | solution.py:30
  18.1 1.0 pad_maximum_fusion.both_ref
  19.2 0.8 shard_map.84
  20.0 16.5 %all_to_all.51 = bf16[16,8,2688]{2,1,0:T(8,128)(2,1)S(1)} all-to-all(bf16[16,8,2688]{2,1,0:T(8,128)(2,1)S(1)} %bitcast.34), channel_id=1, replica_groups=mesh['dp'=32,'expert'=16] {'expert'}, dimensions={0} | all-to-all | bytes 1376256 | tf_op jit(solution)/shard_map/all_to_all | solution.py:30
  36.5 0.2 shard_map.85
  36.8 32.7 %all_to_all.52 = bf16[8,16,1280]{2,1,0:T(8,128)(2,1)S(1)} all-to-all(bf16[8,16,1280]{2,1,0:T(8,128)(2,1)S(1)} %broadcast_in_dim.19), channel_id=1, replica_groups={{0,32,64,96,144,176,208,240},{16,48,80,112,128,160,192,224},{256,288,32..., dimensions={0} | all-to-all | bytes 655360 | tf_op jit(solution)/shard_map/all_to_all | solution.py:30
  69.7 19.7 %all_to_all.53.gathered_ref = bf16[4,2,64,1280]{3,2,1,0:T(8,128)(2,1)S(1)} all-to-all(bf16[4,2,64,1280]{3,2,1,0:T(8,128)(2,1)S(1)} %broadcast_in_dim.42), channel_id=1, replica_groups={{0,16,272,256},{32,48,304,288},{64,80,336,320},{96,112,368,352},{128,14..., dimensions={0} | all-to-all | bytes 2621440 | tf_op jit(solution)/shard_map/all_to_all | solution.py:30
  89.4 1.5 shard_map.86
  90.9 16.6 %all_to_all.54.taken_ref = bf16[4,2,64,1280]{3,2,1,0:T(8,128)(2,1)S(1)} all-to-all(bf16[4,2,64,1280]{3,2,1,0:T(8,128)(2,1)S(1)} %get-tuple-element.26), channel_id=1, replica_groups={{0,16,272,256},{32,48,304,288},{64,80,336,320},{96,112,368,352},{128,14..., dimensions={0} | all-to-all | bytes 2621440 | tf_op jit(solution)/shard_map/all_to_all | solution.py:30
  107.5 0.2 shard_map.87
  107.6 20.7 %all_to_all.55 = bf16[8,16,1280]{2,1,0:T(8,128)(2,1)S(1)} all-to-all(bf16[8,16,1280]{2,1,0:T(8,128)(2,1)S(1)} %bitcast.33), channel_id=1, replica_groups={{0,32,64,96,144,176,208,240},{16,48,80,112,128,160,192,224},{256,288,32..., dimensions={0} | all-to-all | bytes 655360 | tf_op jit(solution)/shard_map/all_to_all | solution.py:30
  128.3 0.1 shard_map.88
  128.5 10.4 %all_to_all.56 = bf16[8,8,2688]{2,1,0:T(8,128)(2,1)S(1)} all-to-all(bf16[8,8,2688]{2,1,0:T(8,128)(2,1)S(1)} %bitcast.31), channel_id=1, replica_groups={{0,2,4,6,8,10,12,14},{1,3,5,7,9,11,13,15},{16,18,20,22,24,26,28,30},{17..., dimensions={0} | all-to-all | bytes 688128 | tf_op jit(solution)/shard_map/all_to_all | solution.py:30
  138.9 11.1 %all_to_all.57 = bf16[2,64,2688]{2,1,0:T(8,128)(2,1)S(1)} all-to-all(bf16[2,64,2688]{2,1,0:T(8,128)(2,1)S(1)} %broadcast_in_dim.44), channel_id=1, replica_groups={{0,1},{2,3},{4,5},{6,7},{8,9},{10,11},{12,13},{14,15},{16,17},{18,19},{..., dimensions={0} | all-to-all | bytes 1376256 | tf_op jit(solution)/shard_map/all_to_all | solution.py:30
  150.1 0.6 shard_map.89
  150.8 10.9 %all_to_all.58 = bf16[32,2,1280]{2,1,0:T(2,128)(2,1)S(1)} all-to-all(bf16[32,2,1280]{2,1,0:T(2,128)(2,1)S(1)} %bitcast.38), channel_id=1, replica_groups={{0,1,2,3,4,5,6,7,8,9,10,11,12,13,14,15,256,257,258,259,260,261,262,263,..., dimensions={0} | all-to-all | bytes 327680 | tf_op jit(solution)/shard_map/all_to_all | solution.py:30
  161.7 0.2 reduce_sum.21
  161.9 0.7 broadcast_in_dim.47
  162.6 7.7 %all-to-all-start.9 = ((bf16[16,2,1280]{2,1,0:T(2,128)(2,1)}), bf16[16,2,1280]{2,1,0:T(2,128)(2,1)S(1)}, u32[]{:S(2)}, u32[]{:S(2)}) async-start(bf16[16,2,1280]{2,1,0:T(2,128)(2,1)} %broadcast_in_dim.47), calls=%async_computation.9 | async-start | bytes 163840 | tf_op jit(solution)/shard_map/all_to_all | solution.py:30
  170.3 1.6 shard_map.91
  171.9 0.9 shard_map.90
  172.8 9.3 %all-to-all-done.9 = bf16[16,2,1280]{2,1,0:T(2,128)(2,1)S(1)} async-done(((bf16[16,2,1280]{2,1,0:T(2,128)(2,1)}), bf16[16,2,1280]{2,1,0:T(2,128)(2,1)S(1)}, u32[]{:S(2)}, u32[]{:S(2)}) %all-to-all-start.9) | async-done | bytes 81952 | tf_op jit(solution)/shard_map/all_to_all | solution.py:30
  182.1 0.6 convert_reduce_fusion
  (11 shorter events, 0.4 us)
Async XLA Ops:
  69.6 19.7 %copy-start = (bf16[2,1280,160]{1,2,0:T(8,128)(2,1)S(1)}, bf16[2,1280,160]{1,2,0:T(8,128)(2,1)}, u32[]{:S(2)}) copy-start(bf16[2,1280,160]{1,2,0:T(8,128)(2,1)} %param.8) | copy-start | bytes 2457604
  69.6 19.7 %copy-start.1 = (bf16[2,160,1280]{2,1,0:T(8,128)(2,1)S(1)}, bf16[2,160,1280]{2,1,0:T(8,128)(2,1)}, u32[]{:S(2)}) copy-start(bf16[2,160,1280]{2,1,0:T(8,128)(2,1)} %param.9) | copy-start | bytes 2457604
  162.6 19.5 %all-to-all-start.9 = ((bf16[16,2,1280]{2,1,0:T(2,128)(2,1)}), bf16[16,2,1280]{2,1,0:T(2,128)(2,1)S(1)}, u32[]{:S(2)}, u32[]{:S(2)}) async-start(bf16[16,2,1280]{2,1,0:T(2,128)(2,1)} %broadcast_in_dim.47), calls=%async_computation.9 | async-start | bytes 163840 | tf_op jit(solution)/shard_map/all_to_all | solution.py:30
